TPU v7x, 128 devices: a whole 4x4x4 slice. The times are simulated.
128 devices in a mesh: tx: 8 (over x_hi, z), ty: 16 (over x_lo, y, core).
Axes of the slice: x: 4 (x_hi: 2, x_lo: 2; x = x_hi * 2 + x_lo), y: 4, z: 4, core: 2. Of those that a mesh axis runs over, the one named last changes fastest.
Arguments:
- reduced_heat: float32 [8, 512, 1024], P(None, 'ty', 'tx'), may hold values from 0.3 to 1.2
- substance_kind: int32 [8, 512, 1024], P(None, 'ty', 'tx'), may hold values from 0 to 3
- moment_vector: float32 [3, 8, 512, 1024], P(None, None, 'ty', 'tx'), may hold values from -4 to 4
- stray_tensor: float32 [6, 16, 1024, 2048], P(None, 'tx', None, 'ty'), may hold values from -8 to 8
- diffusivity_nodes: float32 [16], replicated, may hold values from 0.5 to 1.5
- substance_factor: float32 [4], replicated, may hold values from 0.5 to 2
- ordering_threshold: float32 [4], replicated, may hold values from 0.7 to 1.1
- beam_transverse_spot: int32 [2], replicated, may hold values from 0 to 511
- beam_downtrack_spot: int32 [2], replicated, may hold values from 0 to 1023
Outputs:
- warmed_state: float32 [8, 512, 1024], P(None, 'ty', 'tx')
- demag_field: float32 [3, 8, 512, 1024], P(None, None, 'ty', 'tx')
All inputs are finite; a program needn't handle non-finite values.
Results may differ from a plain program's by a relative error of at most 0.00007.
Values sent between devices are 32-bit elements; how exact they have to be, the bound alone decides.
No kernel may reach another device: no remote copies, remote signals or barrier semaphores. Data moves between devices by JAX's collectives and lax.ppermute only.
A program may use at most 128 MiB of HBM per device.

v0:
```python
import math

import jax
import jax.numpy as jnp
from jax import lax
from jax.sharding import PartitionSpec as P

SWEEPS = 2


AMBIENT_HEAT = 0.3
STEP_RATE = 0.05
LASER_POWER = 4.0
LASER_DEPTH = 4.0
ORDERING_SPREAD = 0.08
TABLE_LOW = 0.2
TABLE_SPAN = 1.6
RADIX_PARTS = 16
HIGHEST = lax.Precision.HIGHEST


def extended(value, sides, width, wrap):
    for axis, dim in sides:
        count, length = (lax.axis_size(axis), value.shape[dim])
        up = [(i, (i + 1) % count) for i in range(count if wrap else count - 1)]
        down = [(j, i) for i, j in up]
        last = lax.slice_in_dim(value, length - width, length, axis=dim)
        first = lax.slice_in_dim(value, 0, width, axis=dim)
        before = lax.ppermute(last, axis, up)
        after = lax.ppermute(first, axis, down)
        value = jnp.concatenate([before, value, after], axis=dim)
    return value


def lookup_diffusivity(absolute, diffusivity_nodes):
    nodes = diffusivity_nodes.shape[0]
    spacing = TABLE_SPAN / (nodes - 1)
    total = jnp.zeros_like(absolute) + diffusivity_nodes[0]
    for index in range(nodes - 1):
        start_node = TABLE_LOW + index * spacing
        total = total + (diffusivity_nodes[index + 1] - diffusivity_nodes[index]) * jnp.clip(
            (absolute - start_node) / spacing, 0.0, 1.0
        )
    return total


def per_particle(substance_kind, values):
    result = jnp.zeros(substance_kind.shape, jnp.float32)
    for grain in range(values.shape[0]):
        result = result + jnp.where(substance_kind == grain, values[grain], 0.0)
    return result


def laser_heating(
    row_ids, col_ids, sheet_indices, spot_row, spot_col, total_cols, col_width, row_width
):
    along = ((col_ids - spot_col + total_cols // 2) % total_cols - total_cols // 2).astype(
        jnp.float32
    ) / col_width
    across = (row_ids - spot_row).astype(jnp.float32) / row_width
    col_factor = jnp.exp(-0.5 * along * along)
    row_factor = jnp.exp(-0.5 * across * across)
    layer_factor = jnp.exp(-jnp.arange(sheet_indices, dtype=jnp.float32) / LASER_DEPTH)
    return layer_factor[:, None, None] * row_factor[None, :, None] * col_factor[None, None, :]


def heat_update(center, diffusivity, neighbours, heating):
    flux = jnp.zeros_like(center)
    for other_temp, other_cond in neighbours:
        flux = flux + 0.5 * (diffusivity + other_cond) * (other_temp - center)
    vertical = 0.5 * (diffusivity[1:] + diffusivity[:-1]) * (center[1:] - center[:-1])
    zero_layer = jnp.zeros_like(center[:1])
    flux = (
        flux
        + jnp.concatenate([vertical, zero_layer], 0)
        - jnp.concatenate([zero_layer, vertical], 0)
    )
    return center + STEP_RATE * (flux + LASER_POWER * heating)


def phase_table(count_in, width, length):
    inputs = jnp.arange(count_in, dtype=jnp.int32)[:, None]
    outputs = jnp.arange(width, dtype=jnp.int32)[None, :]
    angles = (inputs * outputs % length).astype(jnp.float32) * (2.0 * math.pi / length)
    return (jnp.cos(angles), jnp.sin(angles))


def signed_table(rows_count, cols_count, modulus, sign):
    cosine, sine = phase_table(rows_count, cols_count, modulus)
    return (cosine, sign * sine)


def complex_product(form, real_part, imag_part, cosine, sine):

    def product(values, table):
        return jnp.einsum(form, values, table, precision=HIGHEST)

    return (
        product(real_part, cosine) - product(imag_part, sine),
        product(real_part, sine) + product(imag_part, cosine),
    )


def sectioned_dft(real_part, imag_part, count_out, length, sign, on_rows):
    count_in = real_part.shape[-2] if on_rows else real_part.shape[-1]
    span = length // RADIX_PARTS
    first_in = count_in // span
    last_out = count_out // RADIX_PARTS
    first_cos, first_sin = signed_table(first_in, RADIX_PARTS, RADIX_PARTS, sign)
    twist_cos, twist_sin = signed_table(RADIX_PARTS, span, length, sign)
    second_cos, second_sin = signed_table(span, last_out, span, sign)
    if on_rows:
        lead = real_part.shape[:-2]
        tail = real_part.shape[-1]
        split = lead + (first_in, span, tail)
        joined = lead + (last_out * RADIX_PARTS, tail)
        first_form = "...pqx,pk->...kqx"
        second_form = "...kqx,qm->...mkx"
        twist_cos = twist_cos[:, :, None]
        twist_sin = twist_sin[:, :, None]
    else:
        lead = real_part.shape[:-1]
        split = lead + (first_in, span)
        joined = lead + (last_out * RADIX_PARTS,)
        first_form = "...pq,pk->...kq"
        second_form = "...kq,qm->...mk"
    real_part, imag_part = complex_product(
        first_form, real_part.reshape(split), imag_part.reshape(split), first_cos, first_sin
    )
    real_part, imag_part = (
        real_part * twist_cos - imag_part * twist_sin,
        real_part * twist_sin + imag_part * twist_cos,
    )
    real_part, imag_part = complex_product(
        second_form, real_part, imag_part, second_cos, second_sin
    )
    return (real_part.reshape(joined), imag_part.reshape(joined))


def along_last(spectra, count_out, length, sign, factor):
    out_real, out_imag = sectioned_dft(spectra[0], spectra[1], count_out, length, sign, False)
    return jnp.stack([out_real, out_imag]) * factor


def along_rows(spectra, count_out, length, sign, factor):
    out_real, out_imag = sectioned_dft(spectra[0], spectra[1], count_out, length, sign, True)
    return jnp.stack([out_real, out_imag]) * factor


def forward_layers(values, cosine, sine):
    out_real = jnp.einsum("czyx,zk->ckyx", values, cosine, precision=HIGHEST)
    out_imag = -jnp.einsum("czyx,zk->ckyx", values, sine, precision=HIGHEST)
    return jnp.stack([out_real, out_imag])


def apply_kernel(stray_tensor, spectra):
    pairs = ((0, 3, 4), (3, 1, 5), (4, 5, 2))
    fields = []
    for target in range(3):
        total = (
            stray_tensor[pairs[target][0]] * spectra[:, 0]
            + stray_tensor[pairs[target][1]] * spectra[:, 1]
            + stray_tensor[pairs[target][2]] * spectra[:, 2]
        )
        fields.append(-total)
    return jnp.stack(fields, axis=1)


def local(
    reduced_heat,
    substance_kind,
    moment_vector,
    stray_tensor,
    diffusivity_nodes,
    substance_factor,
    ordering_threshold,
    beam_transverse_spot,
    beam_downtrack_spot,
):
    sheet_indices, downtrack_indices, transverse_indices = reduced_heat.shape
    total_rows = downtrack_indices * lax.axis_size("ty")
    total_cols = transverse_indices * lax.axis_size("tx")
    row_base = lax.axis_index("ty") * downtrack_indices
    col_base = lax.axis_index("tx") * transverse_indices
    rotation_phase = reduced_heat - AMBIENT_HEAT
    site_multiplier = per_particle(substance_kind, substance_factor)
    row_ids = row_base + jnp.arange(downtrack_indices, dtype=jnp.int32)
    col_ids = col_base + jnp.arange(transverse_indices, dtype=jnp.int32)
    for sweep in range(SWEEPS):
        diffusivity = site_multiplier * lookup_diffusivity(
            rotation_phase + AMBIENT_HEAT, diffusivity_nodes
        )
        fields = jnp.stack([rotation_phase, diffusivity])
        along = extended(fields, (("tx", 3),), 1, True)
        across = extended(fields, (("ty", 2),), 1, False)
        neighbours = [
            (along[0, :, :, :-2], along[1, :, :, :-2]),
            (along[0, :, :, 2:], along[1, :, :, 2:]),
            (across[0, :, :-2], across[1, :, :-2]),
            (across[0, :, 2:], across[1, :, 2:]),
        ]
        heating = laser_heating(
            row_ids,
            col_ids,
            sheet_indices,
            beam_transverse_spot[sweep],
            beam_downtrack_spot[sweep],
            total_cols,
            0.5 * transverse_indices,
            1.0 * downtrack_indices,
        )
        rotation_phase = heat_update(rotation_phase, diffusivity, neighbours, heating)
    warmed_state = rotation_phase + AMBIENT_HEAT
    proportion = jax.nn.sigmoid(
        (per_particle(substance_kind, ordering_threshold) - warmed_state) / ORDERING_SPREAD
    )
    scaled = moment_vector * proportion[None]
    double_layers = 2 * sheet_indices
    layer_cos, layer_sin = phase_table(sheet_indices, double_layers, double_layers)
    spectra = forward_layers(scaled, layer_cos, layer_sin)
    spectra = lax.all_to_all(spectra, "tx", split_axis=2, concat_axis=4, tiled=True)
    spectra = along_last(spectra, 2 * total_cols, 2 * total_cols, -1, 1.0)
    spectra = lax.all_to_all(spectra, "ty", split_axis=4, concat_axis=3, tiled=True)
    spectra = along_rows(spectra, 2 * total_rows, 2 * total_rows, -1, 1.0)
    field = apply_kernel(stray_tensor, spectra)
    field = along_rows(field, total_rows, 2 * total_rows, 1, 1.0 / (2 * total_rows))
    field = lax.all_to_all(field, "ty", split_axis=3, concat_axis=4, tiled=True)
    field = along_last(field, total_cols, 2 * total_cols, 1, 1.0 / (2 * total_cols))
    field = lax.all_to_all(field, "tx", split_axis=4, concat_axis=2, tiled=True)
    back_cos, back_sin = phase_table(double_layers, sheet_indices, double_layers)
    demag_field = (
        jnp.einsum("ckyx,kz->czyx", field[0], back_cos, precision=HIGHEST)
        - jnp.einsum("ckyx,kz->czyx", field[1], back_sin, precision=HIGHEST)
    ) * (1.0 / double_layers)
    return (warmed_state, demag_field)


def solution(mesh):
    in_specs = (
        P(None, "ty", "tx"),
        P(None, "ty", "tx"),
        P(None, None, "ty", "tx"),
        P(None, "tx", None, "ty"),
        P(),
        P(),
        P(),
        P(),
        P(),
    )
    out_specs = (P(None, "ty", "tx"), P(None, None, "ty", "tx"))
    return jax.shard_map(local, mesh=mesh, in_specs=in_specs, out_specs=out_specs, check_vma=False)
```

profile of v0, /device:TPU:24, one launch (start us, length us, event | category | flops | bytes accessed | tf_op | source)
XLA Modules:
  0.0 484.9 jit_solution(11517684766371992604)
XLA Ops:
  23.7 4.4 add_multiply_fusion.1
  30.2 4.7 collective-permute-start.1
  49.1 5.6 %collective-permute-start.5 = (f32[2,8,32,1]{3,2,1,0:T(8,128)S(1)}, f32[2,8,32,1]{3,2,1,0:T(8,128)S(1)}, u32[]{:S(2)}, u32[]{:S(2)}) collective-permute-start(f32[2,8,32,1]{3,2,1,0:T(8,128)S(1)} %get-tuple-element.48), channel_id=1, source_target_pairs={{16,0},{32,16},{48,32},{64,48},{80,64},{96,80},{112,96},{0,112},{1... | collective-permute-start | bytes 6152 | tf_op jit(solution)/shard_map/ppermute | solution.py:30
  69.0 5.2 %all-to-all-start = ((f32[2,3,16,32,128]{4,3,1,0,2:T(8,128)}), f32[2,3,16,32,128]{4,3,1,0,2:T(8,128)S(1)}, u32[]{:S(2)}, u32[]{:S(2)}) async-start(f32[2,3,16,32,128]{4,3,1,0,2:T(8,128)} %copy.229), calls=%async_computation | async-start | bytes 3145728 | tf_op jit(solution)/shard_map/all_to_all | solution.py:221
  74.3 20.2 %all-to-all-done = f32[2,3,16,32,128]{4,3,1,0,2:T(8,128)S(1)} async-done(((f32[2,3,16,32,128]{4,3,1,0,2:T(8,128)}), f32[2,3,16,32,128]{4,3,1,0,2:T(8,128)S(1)}, u32[]{:S(2)}, u32[]{:S(2)}) %all-to-all-start) | async-done | bytes 1572896 | tf_op jit(solution)/shard_map/all_to_all | solution.py:221
  109.3 5.2 %copy.234 = f32[3,2,32,128,16]{2,4,3,1,0:T(8,128)} copy(f32[3,2,32,128,16]{3,2,4,1,0:T(8,128)} %subtract_bitcast_fusion.6) | data formatting | bytes 3145728 | tf_op jit(solution)/shard_map/sub | solution.py:99
  117.5 5.3 %copy.237 = f32[3,2,32,128,16]{2,4,3,1,0:T(8,128)} copy(f32[3,2,32,128,16]{3,2,4,1,0:T(8,128)} %add_bitcast_fusion.6) | data formatting | bytes 3145728 | tf_op jit(solution)/shard_map/add | solution.py:100
  122.8 10.2 %pad_maximum_fusion = f32[2,3,2,32,2048]{3,4,2,1,0:T(8,128)} fusion(f32[1,3,2,32,2048]{3,4,2,1,0:T(8,128)} %bitcast.458, f32[1,3,2,32,2048]{3,4,2,1,0:T(8,128)} %bitcast.457), kind=kLoop, calls=%fused_computation | loop fusion | flops 786432 | bytes 6291456 | tf_op jit(solution)/shard_map/stack | solution.py:142
  133.0 22.1 %copy.373 = f32[2,3,2,32,2048]{3,2,1,0,4:T(2,128)} copy(f32[2,3,2,32,2048]{3,4,2,1,0:T(8,128)} %pad_maximum_fusion) | data formatting | bytes 6291456 | tf_op jit(solution)/shard_map/stack | solution.py:142
  155.1 17.9 %reshape.262 = f32[16,1,49152]{2,1,0:T(1,128)} reshape(f32[2048,2,3,2,32]{4,3,2,1,0:T(2,128)} %bitcast.443) | data formatting | bytes 6291456
  173.0 5.7 %all-to-all-start.1 = ((f32[16,1,49152]{2,1,0:T(1,128)}), f32[16,1,49152]{2,1,0:T(1,128)S(1)}, u32[]{:S(2)}, u32[]{:S(2)}) async-start(f32[16,1,49152]{2,1,0:T(1,128)} %reshape.262), calls=%async_computation.1 | async-start | bytes 6291456 | tf_op jit(solution)/shard_map/all_to_all | solution.py:223
  179.0 5.5 %slice_bitcast_fusion.8 = (f32[2,1024,128]{2,1,0:T(8,128)}, f32[2,1024,128]{2,1,0:T(8,128)}, f32[2,1024,128]{2,1,0:T(8,128)}, f32[2,1024,128]{2,1,0:T(8,128)}, f...) fusion(f32[6,2,1024,128]{3,2,1,0:T(8,128)} %param.12), kind=kLoop, calls=%fused_computation.95 | loop fusion | bytes 12582912 | tf_op jit(solution)/shard_map/mul | solution.py:162
  184.5 39.5 %all-to-all-done.1 = f32[16,1,49152]{2,1,0:T(1,128)S(1)} async-done(((f32[16,1,49152]{2,1,0:T(1,128)}), f32[16,1,49152]{2,1,0:T(1,128)S(1)}, u32[]{:S(2)}, u32[]{:S(2)}) %all-to-all-start.1) | async-done | bytes 3145760 | tf_op jit(solution)/shard_map/all_to_all | solution.py:223
  224.5 10.8 %reduce = f32[16,49152]{1,0:T(8,128)} reduce(f32[16,1,49152]{2,1,0:T(1,128)S(1)} %all-to-all-done.1, f32[]{:T(128)} %broadcast.988), dimensions={1}, to_apply=%all_to_all.47.reduce_sub_computation | reduce | bytes 6291460 | tf_op jit(solution)/shard_map/all_to_all | solution.py:223
  235.3 18.7 %reshape.263 = f32[2048,2,3,2,32]{4,3,2,1,0:T(2,128)} reshape(f32[16,49152]{1,0:T(8,128)} %reduce) | data formatting | bytes 6291456
  254.0 10.3 %copy.296 = f32[2,3,2,32,16,128]{5,4,3,2,1,0:T(8,128)S(1)} copy(f32[2,3,2,32,16,128]{3,2,1,0,5,4:T(2,128)} %bitcast.444) | data formatting | bytes 6291456 | tf_op jit(solution)/shard_map/all_to_all | solution.py:223
  275.8 4.6 subtract_bitcast_fusion.2
  288.0 4.2 subtract_bitcast_fusion.1
  294.0 3.8 add_bitcast_fusion.1
  303.5 4.3 fusion.10
  307.8 4.3 fusion.8
  312.2 4.6 fusion.30
  316.8 5.5 %subtract_bitcast_fusion = (f32[3,2,16,64,128]{4,2,3,1,0:T(8,128)S(1)}, f32[3,2,16,64,128]{4,2,3,1,0:T(8,128)S(1)}) fusion(f32[16,3,2,64,128]{4,0,3,2,1:T(8,128)S(1)} %fusion.30, f32[16,64]{0,1:T(8,128)S(1)} %fusion.184, f32[16,64]{0,1:T(8,128)S(1)} %get-tuple-element.92, f32[16,3,2,64,128]{4,0,3,2,1:T(8,128)S(1)} %fusion.8, ...), kind=kOutput, calls=%fused_computation.9 | convolution fusion | flops 156503552 | bytes 15736832 | tf_op jit(solution)/shard_map/...pqx,pk->...kqx/dot_general | solution.py:96
  335.4 4.1 copy.262
  339.4 5.3 %all-to-all-start.2 = ((f32[2,3,2,512,128]{4,2,1,0,3:T(2,128)}), f32[2,3,2,512,128]{4,2,1,0,3:T(2,128)S(1)}, u32[]{:S(2)}, u32[]{:S(2)}) async-start(f32[2,3,2,512,128]{4,2,1,0,3:T(2,128)} %copy.262), calls=%async_computation.2 | async-start | bytes 6291456 | tf_op jit(solution)/shard_map/all_to_all | solution.py:227
  344.8 45.1 %all-to-all-done.2 = f32[2,3,2,512,128]{4,2,1,0,3:T(2,128)S(1)} async-done(((f32[2,3,2,512,128]{4,2,1,0,3:T(2,128)}), f32[2,3,2,512,128]{4,2,1,0,3:T(2,128)S(1)}, u32[]{:S(2)}, u32[]{:S(2)}) %all-to-all-start.2) | async-done | bytes 3145760 | tf_op jit(solution)/shard_map/all_to_all | solution.py:227
  420.1 6.7 %copy.273 = f32[2,3,2,32,1024]{3,2,1,0,4:T(2,128)} copy(f32[2,3,2,32,1024]{4,3,2,1,0:T(8,128)S(1)} %maximum_multiply_fusion.1) | data formatting | bytes 3145728 | tf_op jit(solution)/shard_map/mul | solution.py:142
  426.8 8.7 %reshape.264 = f32[8,1,49152]{2,1,0:T(1,128)S(1)} reshape(f32[1024,2,3,2,32]{4,3,2,1,0:T(2,128)} %bitcast.459) | data formatting | bytes 3145728
  435.5 28.3 %all_to_all.60 = f32[8,1,49152]{2,1,0:T(1,128)S(1)} all-to-all(f32[8,1,49152]{2,1,0:T(1,128)S(1)} %reshape.264), channel_id=1, replica_groups=mesh['tx'=8,'ty'=16] {'tx'}, dimensions={0} | all-to-all | bytes 3145728 | tf_op jit(solution)/shard_map/all_to_all | solution.py:229
  463.8 4.4 reduce.1
  468.1 7.9 %reshape.265 = f32[1024,2,3,2,32]{4,3,2,1,0:T(2,128)} reshape(f32[8,49152]{1,0:T(8,128)S(1)} %reduce.1) | data formatting | bytes 3145728
  476.1 5.2 %copy.299 = f32[2,3,2,32,8,128]{5,4,3,2,1,0:T(8,128)S(1)} copy(f32[2,3,2,32,8,128]{3,2,1,0,5,4:T(2,128)} %bitcast.460) | data formatting | bytes 3145728 | tf_op jit(solution)/shard_map/all_to_all | solution.py:229
  (115 shorter events, 126.3 us)
Async XLA Ops:
  0.6 44.4 %copy-start.6 = (f32[8,32,128]{2,1,0:T(8,128)S(1)}, f32[8,32,128]{2,1,0:T(8,128)}, u32[]{:S(2)}) copy-start(f32[8,32,128]{2,1,0:T(8,128)} %param.9) | copy-start | bytes 393220
  0.6 39.9 %copy-start.9 = (s32[2]{0:T(128)S(1)}, s32[2]{0:T(128)}, u32[]{:S(2)}) copy-start(s32[2]{0:T(128)} %param.16) | copy-start | bytes 28
  0.7 40.4 %copy-start.10 = (s32[2]{0:T(128)S(1)}, s32[2]{0:T(128)}, u32[]{:S(2)}) copy-start(s32[2]{0:T(128)} %param.17) | copy-start | bytes 28
  0.7 41.0 %copy-start.8 = (f32[4]{0:T(128)S(1)}, f32[4]{0:T(128)}, u32[]{:S(2)}) copy-start(f32[4]{0:T(128)} %param.15) | copy-start | bytes 52
  28.2 16.8 %collective-permute-start = (f32[2,8,32,1]{3,2,1,0:T(8,128)S(1)}, f32[2,8,32,1]{3,2,1,0:T(8,128)S(1)}, u32[]{:S(2)}, u32[]{:S(2)}) collective-permute-start(f32[2,8,32,1]{3,2,1,0:T(8,128)S(1)} %get-tuple-element.51), channel_id=1, source_target_pairs={{0,16},{16,32},{32,48},{48,64},{64,80},{80,96},{96,112},{112,0},{1... | collective-permute-start | bytes 6152 | tf_op jit(solution)/shard_map/ppermute | solution.py:29
  30.2 14.8 %collective-permute-start.1 = (f32[2,8,32,1]{3,2,1,0:T(8,128)S(1)}, f32[2,8,32,1]{3,2,1,0:T(8,128)S(1)}, u32[]{:S(2)}, u32[]{:S(2)}) collective-permute-start(f32[2,8,32,1]{3,2,1,0:T(8,128)S(1)} %get-tuple-element.52), channel_id=1, source_target_pairs={{16,0},{32,16},{48,32},{64,48},{80,64},{96,80},{112,96},{0,112},{1... | collective-permute-start | bytes 6152 | tf_op jit(solution)/shard_map/ppermute | solution.py:30
  34.9 10.1 %collective-permute-start.2 = (f32[2,8,1,128]{3,2,1,0:T(1,128)S(1)}, f32[2,8,1,128]{3,2,1,0:T(1,128)S(1)}, u32[]{:S(2)}, u32[]{:S(2)}) collective-permute-start(f32[2,8,1,128]{3,2,1,0:T(1,128)S(1)} %get-tuple-element.53), channel_id=1, source_target_pairs={{0,1},{1,2},{2,3},{3,4},{4,5},{5,6},{6,7},{7,8},{8,9},{9,10},{10,1... | collective-permute-start | bytes 24584 | tf_op jit(solution)/shard_map/ppermute | solution.py:29
  36.8 8.2 %collective-permute-start.3 = (f32[2,8,1,128]{3,2,1,0:T(1,128)S(1)}, f32[2,8,1,128]{3,2,1,0:T(1,128)S(1)}, u32[]{:S(2)}, u32[]{:S(2)}) collective-permute-start(f32[2,8,1,128]{3,2,1,0:T(1,128)S(1)} %get-tuple-element.54), channel_id=1, source_target_pairs={{1,0},{2,1},{3,2},{4,3},{5,4},{6,5},{7,6},{8,7},{9,8},{10,9},{11,1... | collective-permute-start | bytes 24584 | tf_op jit(solution)/shard_map/ppermute | solution.py:30
  45.0 20.1 %copy-start.7 = (f32[3,8,32,128]{3,2,1,0:T(8,128)S(1)}, f32[3,8,32,128]{3,2,1,0:T(8,128)}, u32[]{:S(2)}) copy-start(f32[3,8,32,128]{3,2,1,0:T(8,128)} %param.11) | copy-start | bytes 1179652
  49.0 11.3 %collective-permute-start.4 = (f32[2,8,32,1]{3,2,1,0:T(8,128)S(1)}, f32[2,8,32,1]{3,2,1,0:T(8,128)S(1)}, u32[]{:S(2)}, u32[]{:S(2)}) collective-permute-start(f32[2,8,32,1]{3,2,1,0:T(8,128)S(1)} %get-tuple-element.47), channel_id=1, source_target_pairs={{0,16},{16,32},{32,48},{48,64},{64,80},{80,96},{96,112},{112,0},{1... | collective-permute-start | bytes 6152 | tf_op jit(solution)/shard_map/ppermute | solution.py:29
  49.1 11.2 %collective-permute-start.5 = (f32[2,8,32,1]{3,2,1,0:T(8,128)S(1)}, f32[2,8,32,1]{3,2,1,0:T(8,128)S(1)}, u32[]{:S(2)}, u32[]{:S(2)}) collective-permute-start(f32[2,8,32,1]{3,2,1,0:T(8,128)S(1)} %get-tuple-element.48), channel_id=1, source_target_pairs={{16,0},{32,16},{48,32},{64,48},{80,64},{96,80},{112,96},{0,112},{1... | collective-permute-start | bytes 6152 | tf_op jit(solution)/shard_map/ppermute | solution.py:30
  54.7 5.6 %collective-permute-start.6 = (f32[2,8,1,128]{3,2,1,0:T(1,128)S(1)}, f32[2,8,1,128]{3,2,1,0:T(1,128)S(1)}, u32[]{:S(2)}, u32[]{:S(2)}) collective-permute-start(f32[2,8,1,128]{3,2,1,0:T(1,128)S(1)} %get-tuple-element.49), channel_id=1, source_target_pairs={{0,1},{1,2},{2,3},{3,4},{4,5},{5,6},{6,7},{7,8},{8,9},{9,10},{10,1... | collective-permute-start | bytes 24584 | tf_op jit(solution)/shard_map/ppermute | solution.py:29
  56.6 5.0 %collective-permute-start.7 = (f32[2,8,1,128]{3,2,1,0:T(1,128)S(1)}, f32[2,8,1,128]{3,2,1,0:T(1,128)S(1)}, u32[]{:S(2)}, u32[]{:S(2)}) collective-permute-start(f32[2,8,1,128]{3,2,1,0:T(1,128)S(1)} %get-tuple-element.50), channel_id=1, source_target_pairs={{1,0},{2,1},{3,2},{4,3},{5,4},{6,5},{7,6},{8,7},{9,8},{10,9},{11,1... | collective-permute-start | bytes 24584 | tf_op jit(solution)/shard_map/ppermute | solution.py:30
  69.0 25.5 %all-to-all-start = ((f32[2,3,16,32,128]{4,3,1,0,2:T(8,128)}), f32[2,3,16,32,128]{4,3,1,0,2:T(8,128)S(1)}, u32[]{:S(2)}, u32[]{:S(2)}) async-start(f32[2,3,16,32,128]{4,3,1,0,2:T(8,128)} %copy.229), calls=%async_computation | async-start | bytes 3145728 | tf_op jit(solution)/shard_map/all_to_all | solution.py:221
  173.0 51.0 %all-to-all-start.1 = ((f32[16,1,49152]{2,1,0:T(1,128)}), f32[16,1,49152]{2,1,0:T(1,128)S(1)}, u32[]{:S(2)}, u32[]{:S(2)}) async-start(f32[16,1,49152]{2,1,0:T(1,128)} %reshape.262), calls=%async_computation.1 | async-start | bytes 6291456 | tf_op jit(solution)/shard_map/all_to_all | solution.py:223
  297.8 1.8 copy-start
  297.9 1.8 copy-start.1
  297.9 1.8 copy-start.5
  299.7 1.2 copy-start.2
  299.7 1.5 copy-start.3
  299.7 1.8 copy-start.4
  339.4 50.4 %all-to-all-start.2 = ((f32[2,3,2,512,128]{4,2,1,0,3:T(2,128)}), f32[2,3,2,512,128]{4,2,1,0,3:T(2,128)S(1)}, u32[]{:S(2)}, u32[]{:S(2)}) async-start(f32[2,3,2,512,128]{4,2,1,0,3:T(2,128)} %copy.262), calls=%async_computation.2 | async-start | bytes 6291456 | tf_op jit(solution)/shard_map/all_to_all | solution.py:227
where the time goes:
time: 492 us; the launch traced here: 485 us
  local copies, waits for them, and re-layouts  150 us (30%)
  waiting for transfers between devices  106 us (22%)
  matrix products  95.5 us (19%)
  other arithmetic  45.3 us (9%)
  starting transfers between devices  39.6 us (8%)
  blocking collectives  28.3 us (6%)
  between operations  20.4 us (4%)
    dot_general x32, matrix products, product(): return jnp.einsum(form, values, table, precision=HIGHEST)  92.6 us
    unnamed x27, local copies, waits for them, and re-layouts  55.4 us
    all_to_all x1, waiting for transfers between devices, local(): field = lax.all_to_all(field, 'ty', split_axis=3, concat_axis=4, tiled=True)  45.1 us
    all_to_all x1, waiting for transfers between devices, local(): lax.all_to_all(spectra, 'ty', split_axis=4, concat_axis=3, tiled=True)  39.5 us
    all_to_all x1, blocking collectives, local(): field = lax.all_to_all(field, 'tx', split_axis=4, concat_axis=2, tiled=True)  28.3 us
    another operation x3, local copies, waits for them, and re-layouts, along_last(): return jnp.stack([out_real, out_imag]) * factor  27.1 us
    all_to_all x1, waiting for transfers between devices, local(): lax.all_to_all(spectra, 'tx', split_axis=2, concat_axis=4, tiled=True)  20.2 us
    ppermute x4, starting transfers between devices, extended(): after = lax.ppermute(first, axis, down)  17.6 us
  transfers between devices with their start and end apart: 11, of which 4 were waited for; matrix products, arithmetic and copies ran while one was open for 2% of the time, Pallas kernels for 0%

commit v1 on v0

v1 whole, which is shorter than its diff:
```python
import functools
import math

import jax
import jax.numpy as jnp
import ml_dtypes
import numpy as np
from jax import lax
from jax.experimental import pallas as pl
from jax.experimental.pallas import tpu as pltpu
from jax.sharding import PartitionSpec as P

SWEEPS = 2
AMBIENT_HEAT = 0.3
STEP_RATE = 0.05
LASER_POWER = 4.0
LASER_DEPTH = 4.0
ORDERING_SPREAD = 0.08
TABLE_LOW = 0.2
TABLE_SPAN = 1.6
RADIX = 4
PAIRS = ((0, 3, 4), (3, 1, 5), (4, 5, 2))
VMEM = pl.BlockSpec(memory_space=pltpu.VMEM)
SMEM = pl.BlockSpec(memory_space=pltpu.SMEM)
PARAMS = pltpu.CompilerParams(vmem_limit_bytes=50 * 1024 * 1024)
F32 = jnp.float32
BF16 = jnp.bfloat16


def two_terms(table):
    table = np.asarray(table, np.float64)
    high = table.astype(np.float32).astype(ml_dtypes.bfloat16)
    low = (table - high.astype(np.float64)).astype(np.float32).astype(ml_dtypes.bfloat16)
    return (high, low)


def waves(products, length):
    angles = 2.0 * math.pi / length * (products % length)
    return (np.cos(angles), np.sin(angles))


def split(values):
    high = values.astype(BF16)
    low = (values - high.astype(F32)).astype(BF16)
    return (high, low)


def matmul(left, right):
    return lax.dot_general(left, right, (((1,), (0,)), ((), ())), preferred_element_type=F32)


def layer_tables(layers, strips, comps, order):
    count = 2 * layers
    owners = count // 2
    rows_in = comps * strips * layers
    if order == "whole":
        shape = (owners, 2, comps, 2, strips)
    else:
        shape = (2, owners, comps, 2, strips)
    index = np.indices(shape).reshape(5, -1)
    if order == "whole":
        owner, member, comp, part, strip = index
    else:
        member, owner, comp, part, strip = index
    freq = 2 * owner + member
    comp_in, strip_in, layer_in = np.indices((comps, strips, layers)).reshape(3, -1)
    same = (comp[:, None] == comp_in[None]) & (strip[:, None] == strip_in[None])
    cosine, sine = waves(freq[:, None] * layer_in[None], count)
    zero = part[:, None] == 0
    from_real = np.where(zero, cosine, -sine) * same
    from_imag = np.where(zero, sine, cosine) * same
    forward = np.concatenate([from_real, from_imag], 1)
    return forward, forward.T


def along_tables(points, devices):
    length = 2 * points
    span = length // RADIX
    sub = points // RADIX
    a = np.arange(sub)
    v = np.arange(span)
    forward = np.zeros((RADIX, sub, 2 * span))
    for b in range(RADIX):
        cosine, sine = waves(v[None, :] * (RADIX * a + b)[:, None], length)
        forward[b] = np.concatenate([cosine, -sine], 1)
    order = np.zeros((points, points), np.float32)
    for b in range(RADIX):
        order[RADIX * a + b, b * sub + a] = 1.0
    return forward, forward.transpose(0, 2, 1), order.astype(ml_dtypes.bfloat16)


def across_tables(points, groups, blocks, strips):
    length = 2 * points
    span = length // RADIX
    quarter, block, part, strip = np.indices((groups // RADIX, blocks, 2, strips)).reshape(4, -1)
    v = np.arange(span)
    forward = np.zeros((RADIX, 2 * span, quarter.size))
    for b in range(RADIX):
        y = groups * strips * block + groups * strip + RADIX * quarter + b
        cosine, sine = waves(v[:, None] * y[None, :], length)
        zero = part[None, :] == 0
        forward[b, :span] = np.where(zero, cosine, sine)
        forward[b, span:] = np.where(zero, -sine, cosine)
    return forward, forward.transpose(0, 2, 1)


def edges_kernel(heat, kind, factor, sides, rows):
    layers, count = 8, heat.shape[0] // 8
    lane = lax.broadcasted_iota(jnp.int32, (layers, 128), 1)
    packed = [jnp.zeros((layers, 128), F32), jnp.zeros((layers, 128), F32)]
    for y in range(count):
        theta = heat[pl.ds(y, layers, stride=count), :]
        which = kind[pl.ds(y, layers, stride=count), :]
        gain = jnp.zeros_like(theta)
        for grain in range(4):
            gain = gain + jnp.where(which == grain, factor[grain], 0.0)
        for at, value in enumerate((theta, gain)):
            turned = pltpu.roll(value, (2 + 4 * y) % 128, 1)
            packed[at] = jnp.where(lane // 4 == y, turned, packed[at])
            if y < 2:
                rows[0, at, y] = value
            if y >= count - 2:
                rows[1, at, y - count + 2] = value
    sides[0] = packed[0]
    sides[1] = packed[1]


def heat_kernel(
    heat, kind, moment, above, below, left, right, up_left, up_right, down_left, down_right,
    nodes, factor, threshold, spot_row, spot_col, place, warmed, scaled, *, total_rows, total_cols
):
    layers, count = 8, heat.shape[0] // 8
    width = 128
    col_base = place[0] * width
    row_base = place[1] * count
    lane = lax.broadcasted_iota(jnp.int32, (layers, width), 1)
    first = lane == 0
    last = lane == width - 1
    low = lane < width // 2
    depth = lax.broadcasted_iota(jnp.int32, (layers, width), 0)
    spacing = TABLE_SPAN / (nodes.shape[0] - 1)
    slopes = [(nodes[j + 1] - nodes[j]) * (1.0 / spacing) for j in range(nodes.shape[0] - 1)]

    def conductivity(theta, gain):
        absolute = theta + AMBIENT_HEAT
        total = jnp.zeros_like(theta) + nodes[0]
        for j, slope in enumerate(slopes):
            total = total + slope * jnp.clip(absolute - (TABLE_LOW + j * spacing), 0.0, spacing)
        return gain * total

    inside_top = (row_base > 0).astype(F32)
    inside_bottom = (row_base + count < total_rows).astype(F32)
    start = AMBIENT_HEAT
    main = {}
    gains = {}
    for y in range(count):
        which = kind[pl.ds(y, layers, stride=count), :]
        gain = jnp.zeros((layers, width), F32)
        for grain in range(4):
            gain = gain + jnp.where(which == grain, factor[grain], 0.0)
        gains[y] = gain
        main[y] = heat[pl.ds(y, layers, stride=count), :] - start
    for j in range(2):
        main[j - 2] = (above[0, j] - start) * inside_top
        gains[j - 2] = above[1, j] * inside_top
        main[count + j] = (below[0, j] - start) * inside_bottom
        gains[count + j] = below[1, j] * inside_bottom

    def side(at, y, to_left, to_right):
        turn = (128 - (2 + 4 * y)) % 128
        return jnp.where(low, pltpu.roll(to_right[at], turn, 1), pltpu.roll(to_left[at], turn, 1))

    flank = {}
    flank_gain = {}
    for y in range(count):
        flank[y] = side(0, y, left, right) - start
        flank_gain[y] = side(1, y, left, right)
    flank[-1] = (side(0, count - 1, up_left, up_right) - start) * inside_top
    flank_gain[-1] = side(1, count - 1, up_left, up_right) * inside_top
    flank[count] = (side(0, 0, down_left, down_right) - start) * inside_bottom
    flank_gain[count] = side(1, 0, down_left, down_right) * inside_bottom

    def heating(y, sweep, along):
        across = (row_base + y - spot_row[sweep]).astype(F32) * (1.0 / 32.0)
        across = jnp.full((layers, width), -0.5, F32) * (across * across)
        return along * jnp.exp(across)

    def along_of(columns, sweep):
        shifted = columns - spot_col[sweep] + total_cols // 2
        shifted = jnp.where(shifted < 0, shifted + total_cols, shifted)
        shifted = jnp.where(shifted >= total_cols, shifted - total_cols, shifted)
        offset = (shifted - total_cols // 2).astype(F32) * (1.0 / (0.5 * width))
        return jnp.exp(depth.astype(F32) * (-1.0 / LASER_DEPTH)) * jnp.exp(-0.5 * offset * offset)

    main_columns = col_base + lane
    flank_columns = jnp.where(low, lane + width, lane - width) + col_base
    flank_columns = jnp.where(flank_columns < 0, flank_columns + total_cols, flank_columns)
    flank_columns = jnp.where(
        flank_columns >= total_cols, flank_columns - total_cols, flank_columns
    )
    not_top = depth > 0
    not_bottom = depth < layers - 1

    def before(value, other):
        return jnp.where(first, pltpu.roll(other, 1, 1), pltpu.roll(value, 1, 1))

    def after(value, other):
        return jnp.where(last, pltpu.roll(other, width - 1, 1), pltpu.roll(value, width - 1, 1))

    def step(theta, k, sides, up, down, source):
        flux = jnp.zeros_like(theta)
        for other, other_k in sides + (up, down):
            flux = flux + (k + other_k) * (other - theta)
        below_flux = (k + pltpu.roll(k, layers - 1, 0)) * (pltpu.roll(theta, layers - 1, 0) - theta)
        above_flux = (k + pltpu.roll(k, 1, 0)) * (pltpu.roll(theta, 1, 0) - theta)
        flux = flux + jnp.where(not_bottom, below_flux, 0.0) + jnp.where(not_top, above_flux, 0.0)
        return theta + STEP_RATE * (0.5 * flux + LASER_POWER * source)

    def flanked(value, other):
        return before(value, other), after(value, other)

    for sweep in range(SWEEPS):
        reach = SWEEPS - 1 - sweep
        k_main = {y: conductivity(main[y], gains[y]) for y in range(-1 - reach, count + 1 + reach)}
        k_flank = {
            y: conductivity(flank[y], flank_gain[y]) for y in range(-reach, count + reach)
        }
        along_main = along_of(main_columns, sweep)
        along_flank = along_of(flank_columns, sweep)
        fresh = {}
        fresh_flank = {}
        for y in range(-reach, count + reach):
            lt, rt = flanked(main[y], flank[y])
            lk, rk = flanked(k_main[y], k_flank[y])
            value = step(
                main[y], k_main[y], ((lt, lk), (rt, rk)),
                (main[y - 1], k_main[y - 1]), (main[y + 1], k_main[y + 1]),
                heating(y, sweep, along_main),
            )
            if y < 0:
                value = value * inside_top
            if y >= count:
                value = value * inside_bottom
            fresh[y] = value
            if reach and 0 <= y < count:
                lt, rt = flanked(flank[y], main[y])
                lk, rk = flanked(k_flank[y], k_main[y])
                fresh_flank[y] = step(
                    flank[y], k_flank[y], ((lt, lk), (rt, rk)),
                    (flank[y - 1], k_flank[y - 1]), (flank[y + 1], k_flank[y + 1]),
                    heating(y, sweep, along_flank),
                )
        main, flank = fresh, fresh_flank

    groups = scaled.shape[0]
    for y in range(count):
        value = main[y] + AMBIENT_HEAT
        warmed[pl.ds(y, layers, stride=count), :] = value
        which = kind[pl.ds(y, layers, stride=count), :]
        limit = jnp.zeros((layers, width), F32)
        for grain in range(4):
            limit = limit + jnp.where(which == grain, threshold[grain], 0.0)
        fraction = 1.0 / (1.0 + jnp.exp((value - limit) * (1.0 / ORDERING_SPREAD)))
        strip, group = divmod(y, groups)
        for comp in range(3):
            source = moment[pl.ds(comp * layers * count + y, layers, stride=count), :]
            at = (comp * (count // groups) + strip) * layers
            scaled[group, at : at + layers, :] = source * fraction


def turns(t, sign):
    (ar, ai), (br, bi), (cr, ci), (dr, di) = t
    er, ei, fr, fi = ar + cr, ai + ci, ar - cr, ai - ci
    gr, gi, hr, hi = br + dr, bi + di, br - dr, bi - di
    minus = (fr + hi, fi - hr)
    plus = (fr - hi, fi + hr)
    one, three = (minus, plus) if sign < 0 else (plus, minus)
    return ((er + gr, ei + gi), one, (er - gr, ei - gi), three)


def rows_kernel(block, order, high, low, layer_high, layer_low, *outs):
    groups, lines, width = block.shape
    points = groups * width
    sub = points // RADIX
    span = high.shape[2] // 2
    values = jnp.concatenate([block[t] for t in range(groups)], 1)
    both = jnp.concatenate(split(values), 0)
    both = matmul(both, order[...]).astype(BF16)
    parts = []
    for b in range(RADIX):
        data = both[:, b * sub : (b + 1) * sub]
        total = matmul(data, high[b])
        total = total[:lines] + total[lines:] + matmul(data[:lines], low[b])
        parts.append((total[:, :span], total[:, span:]))
    slabs = span // width
    for u, (real, imag) in enumerate(turns(parts, -1)):
        data_high, data_low = split(jnp.concatenate([real, imag], 0))
        total = matmul(layer_high[...], data_high)
        total = total + matmul(layer_high[...], data_low)
        total = total + matmul(layer_low[...], data_high)
        each = total.shape[0] // len(outs)
        rows = each // groups
        blocks = RADIX * slabs
        for member, out in enumerate(outs):
            for t in range(groups):
                for slab in range(slabs):
                    out[t * blocks + u * slabs + slab] = total[
                        member * each + t * rows : member * each + (t + 1) * rows,
                        slab * width : (slab + 1) * width,
                    ]


def spectrum_kernel(data, tensor, high, low, back_high, back_low, out, sums, fields_high, fields_low):
    comps = 3
    senders, lines, width = data.shape
    blocks = 16
    quarters = senders // blocks // RADIX
    members = lines // (8 * comps)
    span = high.shape[1] // 2
    columns = comps * width
    for member in range(members):
        for b in range(RADIX):
            pieces = []
            for comp in range(comps):
                at = (member * comps + comp) * 8
                tall = [
                    data[(b + RADIX * q) * blocks : (b + RADIX * q + 1) * blocks, at : at + 8, :]
                    for q in range(quarters)
                ]
                pieces.append(jnp.concatenate(tall, 0).reshape(quarters * blocks * 8, width))
            data_high, data_low = split(jnp.concatenate(pieces, 1))
            total = matmul(high[b], data_high)
            total = total + matmul(high[b], data_low)
            total = total + matmul(low[b], data_high)
            sums[b] = total
        piece = 16

        def multiply(step, carry):
            at = pl.multiple_of(step * piece, piece)
            spectra = []
            for comp in range(comps):
                lanes = pl.ds(comp * width, width)
                t = [
                    (sums[b, pl.ds(at, piece), lanes], sums[b, pl.ds(span + at, piece), lanes])
                    for b in range(RADIX)
                ]
                spectra.append(turns(t, -1))
            field = [[None] * RADIX for _ in range(comps)]
            for u in range(RADIX):
                taps = [tensor[p, member, pl.ds(u * span + at, piece), :] for p in range(6)]
                for target in range(comps):
                    field[target][u] = tuple(
                        taps[PAIRS[target][0]] * spectra[0][u][part]
                        + taps[PAIRS[target][1]] * spectra[1][u][part]
                        + taps[PAIRS[target][2]] * spectra[2][u][part]
                        for part in range(2)
                    )
            for comp in range(comps):
                lanes = pl.ds(comp * width, width)
                for b, both in enumerate(turns(field[comp], 1)):
                    for part, value in enumerate(both):
                        data_high, data_low = split(value)
                        rows = pl.ds(part * span + at, piece)
                        fields_high[b, rows, lanes] = data_high
                        fields_low[b, rows, lanes] = data_low
            return carry

        lax.fori_loop(0, span // piece, multiply, 0)
        for b in range(RADIX):
            total = matmul(back_high[b], fields_high[b])
            total = total + matmul(back_high[b], fields_low[b])
            total = total + matmul(back_low[b], fields_high[b])
            for q in range(quarters):
                group = b + RADIX * q
                tall = total[q * blocks * 8 : (q + 1) * blocks * 8]
                for comp in range(comps):
                    at = (member * comps + comp) * 8
                    out[group * blocks : (group + 1) * blocks, at : at + 8, :] = tall[
                        :, comp * width : (comp + 1) * width
                    ].reshape(blocks, 8, width)


def cells_kernel(*refs, scale):
    *blocks_in, layer_high, layer_low, high, low, order, out = refs
    groups, lines, width = out.shape
    span = high.shape[1] // 2
    slabs = span // width
    blocks = RADIX * slabs
    pieces = []
    for u in range(RADIX):
        columns = []
        for slab in range(slabs):
            at = u * slabs + slab
            columns.append(
                jnp.concatenate([d[t * blocks + at] for d in blocks_in for t in range(groups)], 0)
            )
        data_high, data_low = split(jnp.concatenate(columns, 1))
        total = matmul(layer_high[...], data_high)
        total = total + matmul(layer_high[...], data_low)
        total = total + matmul(layer_low[...], data_high)
        pieces.append((total[:lines], total[lines:]))
    sorted_columns = []
    for b, both in enumerate(turns(pieces, 1)):
        data_high, data_low = split(jnp.concatenate(both, 1))
        total = matmul(data_high, high[b]) + matmul(data_low, high[b])
        sorted_columns.append(total + matmul(data_high, low[b]))
    values = jnp.concatenate(sorted_columns, 1) * scale
    data_high, data_mid = split(values)
    data_low = (values - data_high.astype(F32) - data_mid.astype(F32)).astype(BF16)
    total = matmul(jnp.concatenate([data_high, data_mid, data_low], 0), order[...])
    values = total[:lines] + total[lines : 2 * lines] + total[2 * lines :]
    for t in range(groups):
        out[t] = values[:, t * width : (t + 1) * width]


def place_kernel(block, out):
    groups, lines, width = block.shape
    layers = 8
    count = out.shape[0] // (3 * layers)
    strips = count // groups
    for comp in range(3):
        for y in range(count):
            strip, group = divmod(y, groups)
            at = (comp * strips + strip) * layers
            out[pl.ds(comp * layers * count + y, layers, stride=count), :] = block[
                group, at : at + layers, :
            ]


def call(kernel, out_shape, in_specs, scratch=(), flops=0, bytes_accessed=0):
    many = isinstance(out_shape, (list, tuple))
    return pl.pallas_call(
        kernel,
        out_shape=out_shape,
        in_specs=in_specs,
        out_specs=[VMEM] * len(out_shape) if many else VMEM,
        scratch_shapes=list(scratch),
        compiler_params=PARAMS,
        cost_estimate=pl.CostEstimate(
            flops=flops, bytes_accessed=bytes_accessed, transcendentals=0
        ),
    )


def local(
    tx, ty, order, heat, kind, moment, tensor, nodes, factor, threshold, spot_row, spot_col
):
    layers, count, width = heat.shape
    strips = count // tx
    comps = 3
    lines = comps * strips * layers
    points_x, points_y = tx * width, ty * count
    members = 2

    heat = heat.reshape(layers * count, width)
    kind = kind.reshape(layers * count, width)
    moment = moment.reshape(comps * layers * count, width)
    sides, rows = call(
        edges_kernel,
        [
            jax.ShapeDtypeStruct((2, layers, width), F32),
            jax.ShapeDtypeStruct((2, 2, 2, layers, width), F32),
        ],
        [VMEM, VMEM, SMEM],
    )(heat, kind, factor)

    def moved(value, step_x, step_y):
        pairs = []
        for x in range(tx):
            for y in range(ty):
                if 0 <= y + step_y < ty:
                    pairs.append((x * ty + y, (x + step_x) % tx * ty + y + step_y))
        return lax.ppermute(value, ("tx", "ty"), pairs)

    left = moved(sides, 1, 0)
    right = moved(sides, -1, 0)
    above = moved(rows[1], 0, 1)
    below = moved(rows[0], 0, -1)
    up_left = moved(sides, 1, 1)
    up_right = moved(sides, -1, 1)
    down_left = moved(sides, 1, -1)
    down_right = moved(sides, -1, -1)
    place = jnp.stack([lax.axis_index("tx"), lax.axis_index("ty")]).astype(jnp.int32)
    warmed, scaled = call(
        functools.partial(heat_kernel, total_rows=points_y, total_cols=points_x),
        [
            jax.ShapeDtypeStruct((layers * count, width), F32),
            jax.ShapeDtypeStruct((tx, lines, width), F32),
        ],
        [VMEM] * 11 + [SMEM] * 6,
    )(
        heat, kind, moment, above, below, left, right, up_left, up_right, down_left, down_right,
        nodes, factor, threshold, spot_row, spot_col, place,
    )
    block = lax.all_to_all(scaled, "tx", split_axis=0, concat_axis=0, tiled=True)

    layer, layer_back = layer_tables(layers, strips, comps, order)
    along, along_back, sort = along_tables(points_x, tx)
    across, across_back = across_tables(points_y, tx, ty, strips)
    senders = tx * ty
    chunks = 1 if order == "whole" else members
    message = members // chunks * comps * 2 * strips
    spectra = call(
        rows_kernel,
        [jax.ShapeDtypeStruct((senders, message, width), F32)] * chunks,
        [VMEM] * 6,
    )(block, sort, *two_terms(along), *two_terms(layer))
    fields = []
    for chunk, data in enumerate(spectra):
        data = lax.all_to_all(data, ("tx", "ty"), split_axis=0, concat_axis=0, tiled=True)
        taps = tensor if chunks == 1 else tensor[:, chunk : chunk + 1]
        span = 2 * points_y // RADIX
        field = call(
            spectrum_kernel,
            jax.ShapeDtypeStruct(data.shape, F32),
            [VMEM] * 6,
            [
                pltpu.VMEM((RADIX, 2 * span, comps * width), F32),
                pltpu.VMEM((RADIX, 2 * span, comps * width), BF16),
                pltpu.VMEM((RADIX, 2 * span, comps * width), BF16),
            ],
        )(data, taps, *two_terms(across), *two_terms(across_back))
        fields.append(
            lax.all_to_all(field, ("tx", "ty"), split_axis=0, concat_axis=0, tiled=True)
        )
    scale = -1.0 / (2 * layers * 2 * points_y * 2 * points_x)
    cells = call(
        functools.partial(cells_kernel, scale=scale),
        jax.ShapeDtypeStruct((tx, lines, width), F32),
        [VMEM] * (chunks + 5),
    )(
        *fields, *two_terms(layer_back), *two_terms(along_back), np.ascontiguousarray(sort.T)
    )
    cells = lax.all_to_all(cells, "tx", split_axis=0, concat_axis=0, tiled=True)
    demag = call(
        place_kernel, jax.ShapeDtypeStruct((comps * layers * count, width), F32), [VMEM]
    )(cells)
    return (
        warmed.reshape(layers, count, width),
        demag.reshape(comps, layers, count, width),
    )


def solution(mesh):
    in_specs = (
        P(None, "ty", "tx"),
        P(None, "ty", "tx"),
        P(None, None, "ty", "tx"),
        P(None, "tx", None, "ty"),
        P(),
        P(),
        P(),
        P(),
        P(),
    )
    out_specs = (P(None, "ty", "tx"), P(None, None, "ty", "tx"))
    body = functools.partial(local, mesh.shape["tx"], mesh.shape["ty"], "whole")
    return jax.shard_map(body, mesh=mesh, in_specs=in_specs, out_specs=out_specs, check_vma=False)
```

time: 492 us -> 206 us (0.42); the launches traced: 485 us -> 205 us
  local copies, waits for them, and re-layouts: 150 us -> 12 us
  waiting for transfers between devices: 106 us -> 2.83 us
  matrix products: 95.5 us -> 0 us
  blocking collectives: 28.3 us -> 123 us
  other arithmetic: 45.3 us -> 0.08 us
  Pallas kernels: 0 us -> 34.9 us
  between operations: 20.4 us -> 0.75 us
  starting transfers between devices: 39.6 us -> 31.1 us
    all_to_all x3 -> x0, waiting for transfers between devices: 105 us -> none  [the longest x1 45.1 us: local(): field = lax.all_to_all(field, 'ty', split_axis=3, concat_axis=4, tiled=True)]
    dot_general x36 -> x0, matrix products: 95.5 us -> none  [the longest x32 92.6 us: product(): return jnp.einsum(form, values, table, precision=HIGHEST)]
    all_to_all x1 -> x4, blocking collectives: 28.3 us -> 123 us  [the longest x1 47.5 us: local(): lax.all_to_all(field, ('tx', 'ty'), split_axis=0, concat_axis=0, tiled=True)]
    unnamed x27 -> x40, local copies, waits for them, and re-layouts: 55.4 us -> 12 us
    pallas_call x0 -> x6, Pallas kernels: none -> 34.9 us  [the longest x1 16.1 us: local(): call(spectrum_kernel, jax.ShapeDtypeStruct(data.shape, F32), [VMEM] * 6,...]
    another operation x4 -> x0, local copies, waits for them, and re-layouts: 28.7 us -> none  [the longest x3 27.1 us: along_last(): return jnp.stack([out_real, out_imag]) * factor]
    all_to_all x5 -> x0, local copies, waits for them, and re-layouts: 18.9 us -> none  [the longest x2 10.8 us: local(): lax.all_to_all(spectra, 'ty', split_axis=4, concat_axis=3, tiled=True)]
    mul x3 -> x0, local copies, waits for them, and re-layouts: 16.2 us -> none  [the longest x1 6.65 us: along_last(): return jnp.stack([out_real, out_imag]) * factor]
  transfers between devices with their start and end apart: 11 -> 8, of which waited for: 4 -> 1; matrix products, arithmetic and copies ran while one was open for 2% -> 0% of each run, Pallas kernels for 0% -> 0%
where the time goes in v1:
time: 206 us; the launch traced here: 205 us
  blocking collectives  123 us (60%)
  Pallas kernels  34.9 us (17%)
  starting transfers between devices  31.1 us (15%)
  local copies, waits for them, and re-layouts  12 us (6%)
  waiting for transfers between devices  2.83 us (1%)
    all_to_all x1, blocking collectives, local(): lax.all_to_all(field, ('tx', 'ty'), split_axis=0, concat_axis=0, tiled=True)  47.5 us
    all_to_all x1, blocking collectives, local(): lax.all_to_all(data, ('tx', 'ty'), split_axis=0, concat_axis=0, tiled=True)  43.3 us
    ppermute x8, starting transfers between devices, moved(): return lax.ppermute(value, ('tx', 'ty'), pairs)  31.1 us
    all_to_all x1, blocking collectives, local(): lax.all_to_all(scaled, 'tx', split_axis=0, concat_axis=0, tiled=True)  16.4 us
    pallas_call x1, Pallas kernels, local(): call(spectrum_kernel, jax.ShapeDtypeStruct(data.shape, F32), [VMEM] * 6,...  16.1 us
    all_to_all x1, blocking collectives, local(): cells = lax.all_to_all(cells, 'tx', split_axis=0, concat_axis=0, tiled=True)  15.7 us
    unnamed x40, local copies, waits for them, and re-layouts  12 us
    pallas_call x1, Pallas kernels, local(): call(rows_kernel, [jax.ShapeDtypeStruct((senders, message, width), F32)]...  6.64 us
  transfers between devices with their start and end apart: 8, of which 1 were waited for; matrix products, arithmetic and copies ran while one was open for 0% of the time, Pallas kernels for 0%

profile of v1, /device:TPU:24, one launch (start us, length us, event | category | flops | bytes accessed | tf_op | source)
XLA Modules:
  0.0 204.5 jit_solution(15611648306116069269)
XLA Ops:
  0.6 0.9 copy-done.5
  1.5 0.9 copy-done.7
  2.4 0.7 copy-done.14
  3.1 0.8 shard_map.230
  3.9 8.0 %collective-permute-start.7 = (f32[2,8,128]{2,1,0:T(8,128)S(1)}, f32[2,8,128]{2,1,0:T(8,128)S(1)}, u32[]{:S(2)}, u32[]{:S(2)}) collective-permute-start(f32[2,8,128]{2,1,0:T(8,128)S(1)} %get-tuple-element.7), channel_id=1, source_target_pairs={{1,112},{2,113},{3,114},{4,115},{5,116},{6,117},{7,118},{8,119},{9... | collective-permute-start | bytes 24584 | tf_op jit(solution)/shard_map/ppermute | solution.py:473
  11.9 1.9 collective-permute-start.6
  13.8 7.3 %collective-permute-start.5 = (f32[2,8,128]{2,1,0:T(8,128)S(1)}, f32[2,8,128]{2,1,0:T(8,128)S(1)}, u32[]{:S(2)}, u32[]{:S(2)}) collective-permute-start(f32[2,8,128]{2,1,0:T(8,128)S(1)} %get-tuple-element.7), channel_id=1, source_target_pairs={{0,113},{1,114},{2,115},{3,116},{4,117},{5,118},{6,119},{7,120},{8... | collective-permute-start | bytes 24584 | tf_op jit(solution)/shard_map/ppermute | solution.py:473
  21.1 1.9 collective-permute-start.4
  23.0 7.6 %collective-permute-start.3 = (f32[2,8,128]{2,1,0:T(8,128)S(1)}, f32[2,8,128]{2,1,0:T(8,128)S(1)}, u32[]{:S(2)}, u32[]{:S(2)}) collective-permute-start(f32[2,8,128]{2,1,0:T(8,128)S(1)} %get-tuple-element.7), channel_id=1, source_target_pairs={{0,112},{1,113},{2,114},{3,115},{4,116},{5,117},{6,118},{7,119},{8... | collective-permute-start | bytes 24584 | tf_op jit(solution)/shard_map/ppermute | solution.py:473
  30.7 1.9 collective-permute-start.1
  32.6 2.4 %collective-permute-start = (f32[2,2,8,128]{3,2,1,0:T(8,128)S(1)}, f32[2,2,8,128]{3,2,1,0:T(8,128)S(1)}, u32[]{:S(2)}, u32[]{:S(2)}) collective-permute-start(f32[2,2,8,128]{3,2,1,0:T(8,128)S(1)} %get-tuple-element.11), channel_id=1, source_target_pairs={{0,1},{1,2},{2,3},{3,4},{4,5},{5,6},{6,7},{7,8},{8,9},{9,10},{10,1... | collective-permute-start | bytes 49160 | tf_op jit(solution)/shard_map/ppermute | solution.py:473
  35.1 2.8 %collective-permute-done.2.left = f32[2,8,128]{2,1,0:T(8,128)S(1)} collective-permute-done((f32[2,8,128]{2,1,0:T(8,128)S(1)}, f32[2,8,128]{2,1,0:T(8,128)S(1)}, u32[]{:S(2)}, u32[]{:S(2)}) %collective-permute-start.2) | collective-permute-done | bytes 8224 | tf_op jit(solution)/shard_map/ppermute | solution.py:473
  37.9 0.9 copy-done.6
  38.8 0.9 copy-done.8
  39.7 1.0 copy-done.9
  40.7 0.7 copy-done.15
  41.4 0.7 copy-done.16
  42.0 0.7 copy-done.17
  42.7 0.7 copy-done.18
  43.3 0.7 copy-done.19
  44.0 3.9 %shard_map.231 = (f32[256,128]{1,0:T(8,128)}, f32[8,96,128]{2,1,0:T(8,128)S(1)}) custom-call(f32[256,128]{1,0:T(8,128)S(1)} %bitcast.12, s32[256,128]{1,0:T(8,128)S(1)} %bitcast.14, f32[768,128]{1,0:T(8,128)S(1)} %bitcast.15, f32[2,2,8,128]{3,2,1,0:T(8,128)S(1)} %collective-permute-done.above, f32[2,2,8,128]{3,2,1,0:T(8,128)S(1)} %collective-permute-done.1.below, ...), custom_call_target="tpu_custom_call" | custom-call | tf_op jit(solution)/shard_map/pallas_call | solution.py:484
  47.9 16.4 %all_to_all.20.block = f32[8,96,128]{2,1,0:T(8,128)S(1)} all-to-all(f32[8,96,128]{2,1,0:T(8,128)S(1)} %get-tuple-element.9), channel_id=1, replica_groups=mesh['tx'=8,'ty'=16] {'tx'}, dimensions={0} | all-to-all | bytes 786432 | tf_op jit(solution)/shard_map/all_to_all | solution.py:495
  64.3 1.6 copy-done.1
  65.9 0.9 copy-done.10
  66.8 0.9 copy-done.11
  67.7 6.6 %shard_map.232 = f32[128,48,128]{2,1,0:T(8,128)} custom-call(f32[8,96,128]{2,1,0:T(8,128)S(1)} %all_to_all.20.block, bf16[1024,1024]{1,0:T(8,128)(2,1)S(1)} %copy-done.1, bf16[4,256,1024]{2,1,0:T(8,128)(2,1)} %constant.38.clone.high, bf16[4,256,1024]{2,1,0:T(8,128)(2,1)} %constant.39.clone.low, bf16[384,192]{1,0:T(8,128)(2,1)S(1)} %copy-done.11, ...), custom_call_target="tpu_custom_call" | custom-call | tf_op jit(solution)/shard_map/pallas_call | solution.py:503
  74.3 43.3 %all_to_all.21.data = f32[128,48,128]{2,1,0:T(8,128)} all-to-all(f32[128,48,128]{2,1,0:T(8,128)} %shard_map.232), channel_id=1, replica_groups=mesh['tx'=8,'ty'=16] {'tx','ty'}, dimensions={0} | all-to-all | bytes 6291456 | tf_op jit(solution)/shard_map/all_to_all | solution.py:510
  117.7 16.1 %shard_map.233 = f32[128,48,128]{2,1,0:T(8,128)} custom-call(f32[128,48,128]{2,1,0:T(8,128)} %all_to_all.21.data, f32[6,2,1024,128]{3,2,1,0:T(8,128)} %tensor.1, bf16[4,512,256]{2,1,0:T(8,128)(2,1)S(1)} %copy-done.4, bf16[4,512,256]{2,1,0:T(8,128)(2,1)S(1)} %copy-done.3, bf16[4,256,512]{2,1,0:T(8,128)(2,1)S(1)} %copy-done.2, ...), custom_call_target="tpu_custom_call" | custom-call | tf_op jit(solution)/shard_map/pallas_call | solution.py:513
  133.8 47.5 %all_to_all.22.refs_0_ = f32[128,48,128]{2,1,0:T(8,128)} all-to-all(f32[128,48,128]{2,1,0:T(8,128)} %shard_map.233), channel_id=1, replica_groups=mesh['tx'=8,'ty'=16] {'tx','ty'}, dimensions={0} | all-to-all | bytes 6291456 | tf_op jit(solution)/shard_map/all_to_all | solution.py:524
  181.3 6.5 %shard_map.234 = f32[8,96,128]{2,1,0:T(8,128)S(1)} custom-call(f32[128,48,128]{2,1,0:T(8,128)} %all_to_all.22.refs_0_, bf16[192,384]{1,0:T(8,128)(2,1)S(1)} %copy-done.13, bf16[192,384]{1,0:T(8,128)(2,1)S(1)} %copy-done.12, bf16[4,1024,256]{2,1,0:T(8,128)(2,1)S(1)} %copy-done, bf16[4,1024,256]{2,1,0:T(8,128)(2,1)} %constant.49.clone.refs_4_, ...), custom_call_target="tpu_custom_call" | custom-call | tf_op jit(solution)/shard_map/pallas_call | solution.py:527
  187.8 15.7 %all_to_all.23.block = f32[8,96,128]{2,1,0:T(8,128)S(1)} all-to-all(f32[8,96,128]{2,1,0:T(8,128)S(1)} %shard_map.234), channel_id=1, replica_groups=mesh['tx'=8,'ty'=16] {'tx'}, dimensions={0} | all-to-all | bytes 786432 | tf_op jit(solution)/shard_map/all_to_all | solution.py:534
  203.5 1.0 shard_map.235
  (36 shorter events, 0.1 us)
Async XLA Ops:
  0.6 0.9 copy-start.5
  1.5 0.9 copy-start.7
  2.4 0.7 copy-start.14
  3.9 26.8 %collective-permute-start.7 = (f32[2,8,128]{2,1,0:T(8,128)S(1)}, f32[2,8,128]{2,1,0:T(8,128)S(1)}, u32[]{:S(2)}, u32[]{:S(2)}) collective-permute-start(f32[2,8,128]{2,1,0:T(8,128)S(1)} %get-tuple-element.7), channel_id=1, source_target_pairs={{1,112},{2,113},{3,114},{4,115},{5,116},{6,117},{7,118},{8,119},{9... | collective-permute-start | bytes 24584 | tf_op jit(solution)/shard_map/ppermute | solution.py:473
  11.9 18.8 %collective-permute-start.6 = (f32[2,8,128]{2,1,0:T(8,128)S(1)}, f32[2,8,128]{2,1,0:T(8,128)S(1)}, u32[]{:S(2)}, u32[]{:S(2)}) collective-permute-start(f32[2,8,128]{2,1,0:T(8,128)S(1)} %get-tuple-element.7), channel_id=1, source_target_pairs={{1,16},{2,17},{3,18},{4,19},{5,20},{6,21},{7,22},{8,23},{9,24},{10... | collective-permute-start | bytes 24584 | tf_op jit(solution)/shard_map/ppermute | solution.py:473
  13.8 18.8 %collective-permute-start.5 = (f32[2,8,128]{2,1,0:T(8,128)S(1)}, f32[2,8,128]{2,1,0:T(8,128)S(1)}, u32[]{:S(2)}, u32[]{:S(2)}) collective-permute-start(f32[2,8,128]{2,1,0:T(8,128)S(1)} %get-tuple-element.7), channel_id=1, source_target_pairs={{0,113},{1,114},{2,115},{3,116},{4,117},{5,118},{6,119},{7,120},{8... | collective-permute-start | bytes 24584 | tf_op jit(solution)/shard_map/ppermute | solution.py:473
  21.1 14.0 %collective-permute-start.4 = (f32[2,8,128]{2,1,0:T(8,128)S(1)}, f32[2,8,128]{2,1,0:T(8,128)S(1)}, u32[]{:S(2)}, u32[]{:S(2)}) collective-permute-start(f32[2,8,128]{2,1,0:T(8,128)S(1)} %get-tuple-element.7), channel_id=1, source_target_pairs={{0,17},{1,18},{2,19},{3,20},{4,21},{5,22},{6,23},{7,24},{8,25},{9,... | collective-permute-start | bytes 24584 | tf_op jit(solution)/shard_map/ppermute | solution.py:473
  23.0 12.1 %collective-permute-start.3 = (f32[2,8,128]{2,1,0:T(8,128)S(1)}, f32[2,8,128]{2,1,0:T(8,128)S(1)}, u32[]{:S(2)}, u32[]{:S(2)}) collective-permute-start(f32[2,8,128]{2,1,0:T(8,128)S(1)} %get-tuple-element.7), channel_id=1, source_target_pairs={{0,112},{1,113},{2,114},{3,115},{4,116},{5,117},{6,118},{7,119},{8... | collective-permute-start | bytes 24584 | tf_op jit(solution)/shard_map/ppermute | solution.py:473
  30.6 7.3 %collective-permute-start.2 = (f32[2,8,128]{2,1,0:T(8,128)S(1)}, f32[2,8,128]{2,1,0:T(8,128)S(1)}, u32[]{:S(2)}, u32[]{:S(2)}) collective-permute-start(f32[2,8,128]{2,1,0:T(8,128)S(1)} %get-tuple-element.7), channel_id=1, source_target_pairs={{0,16},{1,17},{2,18},{3,19},{4,20},{5,21},{6,22},{7,23},{8,24},{9,... | collective-permute-start | bytes 24584 | tf_op jit(solution)/shard_map/ppermute | solution.py:473
  30.7 7.2 %collective-permute-start.1 = (f32[2,2,8,128]{3,2,1,0:T(8,128)S(1)}, f32[2,2,8,128]{3,2,1,0:T(8,128)S(1)}, u32[]{:S(2)}, u32[]{:S(2)}) collective-permute-start(f32[2,2,8,128]{3,2,1,0:T(8,128)S(1)} %get-tuple-element.10), channel_id=1, source_target_pairs={{1,0},{2,1},{3,2},{4,3},{5,4},{6,5},{7,6},{8,7},{9,8},{10,9},{11,1... | collective-permute-start | bytes 49160 | tf_op jit(solution)/shard_map/ppermute | solution.py:473
  32.6 5.3 %collective-permute-start = (f32[2,2,8,128]{3,2,1,0:T(8,128)S(1)}, f32[2,2,8,128]{3,2,1,0:T(8,128)S(1)}, u32[]{:S(2)}, u32[]{:S(2)}) collective-permute-start(f32[2,2,8,128]{3,2,1,0:T(8,128)S(1)} %get-tuple-element.11), channel_id=1, source_target_pairs={{0,1},{1,2},{2,3},{3,4},{4,5},{5,6},{6,7},{7,8},{8,9},{9,10},{10,1... | collective-permute-start | bytes 49160 | tf_op jit(solution)/shard_map/ppermute | solution.py:473
  37.9 0.9 copy-start.6
  38.8 0.9 copy-start.8
  39.7 1.0 copy-start.9
  40.7 0.7 copy-start.15
  41.4 0.7 copy-start.16
  42.0 0.7 copy-start.17
  42.7 0.7 copy-start.18
  43.3 0.7 copy-start.19
  64.3 1.6 copy-start.1
  65.8 0.9 copy-start.10
  66.8 0.9 copy-start.11
  74.3 43.3 %copy-start.2 = (bf16[4,256,512]{2,1,0:T(8,128)(2,1)S(1)}, bf16[4,256,512]{2,1,0:T(8,128)(2,1)}, u32[]{:S(2)}) copy-start(bf16[4,256,512]{2,1,0:T(8,128)(2,1)} %constant.44.clone.back_high) | copy-start | bytes 3145732
  74.3 43.3 %copy-start.3 = (bf16[4,512,256]{2,1,0:T(8,128)(2,1)S(1)}, bf16[4,512,256]{2,1,0:T(8,128)(2,1)}, u32[]{:S(2)}) copy-start(bf16[4,512,256]{2,1,0:T(8,128)(2,1)} %constant.43.clone.low) | copy-start | bytes 3145732
  74.3 43.3 %copy-start.4 = (bf16[4,512,256]{2,1,0:T(8,128)(2,1)S(1)}, bf16[4,512,256]{2,1,0:T(8,128)(2,1)}, u32[]{:S(2)}) copy-start(bf16[4,512,256]{2,1,0:T(8,128)(2,1)} %constant.42.clone.high) | copy-start | bytes 3145732
  133.8 47.5 %copy-start = (bf16[4,1024,256]{2,1,0:T(8,128)(2,1)S(1)}, bf16[4,1024,256]{2,1,0:T(8,128)(2,1)}, u32[]{:S(2)}) copy-start(bf16[4,1024,256]{2,1,0:T(8,128)(2,1)} %constant.48.clone.refs_3_) | copy-start | bytes 6291460
  133.8 47.5 %copy-start.12 = (bf16[192,384]{1,0:T(8,128)(2,1)S(1)}, bf16[192,384]{1,0:T(8,128)(2,1)}, u32[]{:S(2)}) copy-start(bf16[192,384]{1,0:T(8,128)(2,1)} %constant.47.clone.refs_2_) | copy-start | bytes 442372
  133.8 47.5 %copy-start.13 = (bf16[192,384]{1,0:T(8,128)(2,1)S(1)}, bf16[192,384]{1,0:T(8,128)(2,1)}, u32[]{:S(2)}) copy-start(bf16[192,384]{1,0:T(8,128)(2,1)} %constant.46.clone.refs_1_) | copy-start | bytes 442372

commit v2 on v1

v2 whole, which is shorter than its diff:
```python
import functools
import math

import jax
import jax.numpy as jnp
import ml_dtypes
import numpy as np
from jax import lax
from jax.experimental import pallas as pl
from jax.experimental.pallas import tpu as pltpu
from jax.sharding import PartitionSpec as P

SWEEPS = 2
AMBIENT_HEAT = 0.3
STEP_RATE = 0.05
LASER_POWER = 4.0
LASER_DEPTH = 4.0
ORDERING_SPREAD = 0.08
TABLE_LOW = 0.2
TABLE_SPAN = 1.6
RADIX = 4
PAIRS = ((0, 3, 4), (3, 1, 5), (4, 5, 2))
VMEM = pl.BlockSpec(memory_space=pltpu.VMEM)
ANY = pl.BlockSpec(memory_space=pl.ANY)
F32 = jnp.float32
BF16 = jnp.bfloat16


def two_terms(table):
    table = np.asarray(table, np.float64)
    high = table.astype(np.float32).astype(ml_dtypes.bfloat16)
    low = (table - high.astype(np.float64)).astype(np.float32).astype(ml_dtypes.bfloat16)
    return (high, low)


def waves(products, length):
    angles = 2.0 * math.pi / length * (products % length)
    return (np.cos(angles), np.sin(angles))


def split(values):
    high = values.astype(BF16)
    low = (values - high.astype(F32)).astype(BF16)
    return (high, low)


def matmul(left, right):
    return lax.dot_general(left, right, (((1,), (0,)), ((), ())), preferred_element_type=F32)


def layer_tables(layers, strips, comps, order):
    count = 2 * layers
    owners = count // 2
    rows_in = comps * strips * layers
    if order == "whole":
        shape = (owners, 2, comps, 2, strips)
    else:
        shape = (2, owners, comps, 2, strips)
    index = np.indices(shape).reshape(5, -1)
    if order == "whole":
        owner, member, comp, part, strip = index
    else:
        member, owner, comp, part, strip = index
    freq = 2 * owner + member
    comp_in, strip_in, layer_in = np.indices((comps, strips, layers)).reshape(3, -1)
    same = (comp[:, None] == comp_in[None]) & (strip[:, None] == strip_in[None])
    cosine, sine = waves(freq[:, None] * layer_in[None], count)
    zero = part[:, None] == 0
    from_real = np.where(zero, cosine, -sine) * same
    from_imag = np.where(zero, sine, cosine) * same
    forward = np.concatenate([from_real, from_imag], 1)
    return forward, forward.T


def along_tables(points, devices):
    length = 2 * points
    span = length // RADIX
    sub = points // RADIX
    a = np.arange(sub)
    v = np.arange(span)
    forward = np.zeros((RADIX, sub, 2 * span))
    for b in range(RADIX):
        cosine, sine = waves(v[None, :] * (RADIX * a + b)[:, None], length)
        forward[b] = np.concatenate([cosine, -sine], 1)
    order = np.zeros((points, points), np.float32)
    for b in range(RADIX):
        order[RADIX * a + b, b * sub + a] = 1.0
    return forward, forward.transpose(0, 2, 1), order.astype(ml_dtypes.bfloat16)


def across_tables(points, groups, blocks, strips):
    length = 2 * points
    span = length // RADIX
    quarter, block, part, strip = np.indices((groups // RADIX, blocks, 2, strips)).reshape(4, -1)
    v = np.arange(span)
    forward = np.zeros((RADIX, 2 * span, quarter.size))
    for b in range(RADIX):
        y = groups * strips * block + groups * strip + RADIX * quarter + b
        cosine, sine = waves(v[:, None] * y[None, :], length)
        zero = part[None, :] == 0
        forward[b, :span] = np.where(zero, cosine, sine)
        forward[b, span:] = np.where(zero, -sine, cosine)
    return forward, forward.transpose(0, 2, 1)


def fetch(pairs, sems):
    copies = [
        pltpu.make_async_copy(source, target, sems.at[at])
        for at, (source, target) in enumerate(pairs)
    ]
    for copy in copies:
        copy.start()
    return copies


def chosen(which, values):
    total = jnp.zeros(which.shape, F32)
    for grain in range(values.shape[0]):
        total = total + jnp.where(which == grain, values[grain], 0.0)
    return total


def edges_kernel(
    heat_in, kind_in, factor_in, threshold_in, heat, gains, limits, sides, rows,
    kind, factor, threshold, sems
):
    copies = fetch(
        [(factor_in, factor), (threshold_in, threshold), (kind_in, kind), (heat_in, heat)], sems
    )
    for copy in copies:
        copy.wait()
    layers, count = 8, heat.shape[0] // 8
    lane = lax.broadcasted_iota(jnp.int32, (layers, 128), 1)
    packed = [jnp.zeros((layers, 128), F32), jnp.zeros((layers, 128), F32)]
    for y in range(count):
        at_rows = pl.ds(y, layers, stride=count)
        theta = heat[at_rows, :]
        which = kind[at_rows, :]
        gain = chosen(which, factor)
        gains[at_rows, :] = gain
        limits[at_rows, :] = chosen(which, threshold)
        for at, value in enumerate((theta, gain)):
            turned = pltpu.roll(value, (2 + 4 * y) % 128, 1)
            packed[at] = jnp.where(lane // 4 == y, turned, packed[at])
            if y < 2:
                rows[0, 2 * at + y] = value
            if y >= count - 2:
                rows[1, 2 * at + y - count + 2] = value
    sides[0] = packed[0]
    sides[1] = packed[1]


def join_kernel(rows, left, right, upward, downward):
    for at, out in enumerate((upward, downward)):
        out[0:4] = rows[at]
        out[4:6] = left[...]
        out[6:8] = right[...]


def heat_kernel(
    heat, gains_in, limits, moment_in, above, below, left, right, nodes_in, spot_row_in, spot_col_in,
    warmed, scaled, moment, nodes, spot_row, spot_col, sems, *, total_rows, total_cols
):
    copies = fetch(
        [(nodes_in, nodes), (spot_row_in, spot_row), (spot_col_in, spot_col), (moment_in, moment)],
        sems,
    )
    layers, count = 8, heat.shape[0] // 8
    width = 128
    col_base = lax.axis_index("tx") * width
    row_base = lax.axis_index("ty") * count
    for copy in copies[:3]:
        copy.wait()
    lane = lax.broadcasted_iota(jnp.int32, (layers, width), 1)
    first = lane == 0
    last = lane == width - 1
    low = lane < width // 2
    depth = lax.broadcasted_iota(jnp.int32, (layers, width), 0)
    spacing = TABLE_SPAN / (nodes.shape[0] - 1)
    slopes = [(nodes[j + 1] - nodes[j]) * (1.0 / spacing) for j in range(nodes.shape[0] - 1)]

    def conductivity(theta, gain):
        absolute = theta + AMBIENT_HEAT
        total = jnp.zeros_like(theta) + nodes[0]
        for j, slope in enumerate(slopes):
            total = total + slope * jnp.clip(absolute - (TABLE_LOW + j * spacing), 0.0, spacing)
        return gain * total

    inside_top = jnp.where(row_base > 0, 1.0, 0.0)
    inside_bottom = jnp.where(row_base + count < total_rows, 1.0, 0.0)
    start = AMBIENT_HEAT
    main = {}
    gains = {}
    for y in range(count):
        gains[y] = gains_in[pl.ds(y, layers, stride=count), :]
        main[y] = heat[pl.ds(y, layers, stride=count), :] - start
    for j in range(2):
        main[j - 2] = (above[j] - start) * inside_top
        gains[j - 2] = above[2 + j] * inside_top
        main[count + j] = (below[j] - start) * inside_bottom
        gains[count + j] = below[2 + j] * inside_bottom

    def side(at, y, to_left, to_right, skip=(0, 0)):
        turn = (128 - (2 + 4 * y)) % 128
        return jnp.where(
            low,
            pltpu.roll(to_right[skip[1] + at], turn, 1),
            pltpu.roll(to_left[skip[0] + at], turn, 1),
        )

    flank = {}
    flank_gain = {}
    for y in range(count):
        flank[y] = side(0, y, left, right) - start
        flank_gain[y] = side(1, y, left, right)
    flank[-1] = (side(0, count - 1, above, above, (4, 6)) - start) * inside_top
    flank_gain[-1] = side(1, count - 1, above, above, (4, 6)) * inside_top
    flank[count] = (side(0, 0, below, below, (4, 6)) - start) * inside_bottom
    flank_gain[count] = side(1, 0, below, below, (4, 6)) * inside_bottom

    def heating(y, sweep, along):
        across = (row_base + y - spot_row[sweep]).astype(F32) * (1.0 / 32.0)
        across = jnp.full((layers, width), -0.5, F32) * (across * across)
        return along * jnp.exp(across)

    def along_of(columns, sweep):
        shifted = columns - spot_col[sweep] + total_cols // 2
        shifted = jnp.where(shifted < 0, shifted + total_cols, shifted)
        shifted = jnp.where(shifted >= total_cols, shifted - total_cols, shifted)
        offset = (shifted - total_cols // 2).astype(F32) * (1.0 / (0.5 * width))
        return jnp.exp(depth.astype(F32) * (-1.0 / LASER_DEPTH)) * jnp.exp(-0.5 * offset * offset)

    main_columns = col_base + lane
    flank_columns = jnp.where(low, lane + width, lane - width) + col_base
    flank_columns = jnp.where(flank_columns < 0, flank_columns + total_cols, flank_columns)
    flank_columns = jnp.where(
        flank_columns >= total_cols, flank_columns - total_cols, flank_columns
    )
    not_top = depth > 0
    not_bottom = depth < layers - 1

    def before(value, other):
        return jnp.where(first, pltpu.roll(other, 1, 1), pltpu.roll(value, 1, 1))

    def after(value, other):
        return jnp.where(last, pltpu.roll(other, width - 1, 1), pltpu.roll(value, width - 1, 1))

    def step(theta, k, sides, up, down, source):
        flux = jnp.zeros_like(theta)
        for other, other_k in sides + (up, down):
            flux = flux + (k + other_k) * (other - theta)
        below_flux = (k + pltpu.roll(k, layers - 1, 0)) * (pltpu.roll(theta, layers - 1, 0) - theta)
        above_flux = (k + pltpu.roll(k, 1, 0)) * (pltpu.roll(theta, 1, 0) - theta)
        flux = flux + jnp.where(not_bottom, below_flux, 0.0) + jnp.where(not_top, above_flux, 0.0)
        return theta + STEP_RATE * (0.5 * flux + LASER_POWER * source)

    def flanked(value, other):
        return before(value, other), after(value, other)

    for sweep in range(SWEEPS):
        reach = SWEEPS - 1 - sweep
        k_main = {y: conductivity(main[y], gains[y]) for y in range(-1 - reach, count + 1 + reach)}
        k_flank = {
            y: conductivity(flank[y], flank_gain[y]) for y in range(-reach, count + reach)
        }
        along_main = along_of(main_columns, sweep)
        along_flank = along_of(flank_columns, sweep)
        fresh = {}
        fresh_flank = {}
        for y in range(-reach, count + reach):
            lt, rt = flanked(main[y], flank[y])
            lk, rk = flanked(k_main[y], k_flank[y])
            value = step(
                main[y], k_main[y], ((lt, lk), (rt, rk)),
                (main[y - 1], k_main[y - 1]), (main[y + 1], k_main[y + 1]),
                heating(y, sweep, along_main),
            )
            if y < 0:
                value = value * inside_top
            if y >= count:
                value = value * inside_bottom
            fresh[y] = value
            if reach and 0 <= y < count:
                lt, rt = flanked(flank[y], main[y])
                lk, rk = flanked(k_flank[y], k_main[y])
                fresh_flank[y] = step(
                    flank[y], k_flank[y], ((lt, lk), (rt, rk)),
                    (flank[y - 1], k_flank[y - 1]), (flank[y + 1], k_flank[y + 1]),
                    heating(y, sweep, along_flank),
                )
        main, flank = fresh, fresh_flank

    groups = scaled.shape[0]
    copies[3].wait()
    for y in range(count):
        value = main[y] + AMBIENT_HEAT
        warmed[pl.ds(y, layers, stride=count), :] = value
        limit = limits[pl.ds(y, layers, stride=count), :]
        fraction = 1.0 / (1.0 + jnp.exp((value - limit) * (1.0 / ORDERING_SPREAD)))
        strip, group = divmod(y, groups)
        for comp in range(3):
            source = moment[pl.ds(comp * layers * count + y, layers, stride=count), :]
            at = (comp * (count // groups) + strip) * layers
            scaled[group, at : at + layers, :] = source * fraction


def turns(t, sign):
    (ar, ai), (br, bi), (cr, ci), (dr, di) = t
    er, ei, fr, fi = ar + cr, ai + ci, ar - cr, ai - ci
    gr, gi, hr, hi = br + dr, bi + di, br - dr, bi - di
    minus = (fr + hi, fi - hr)
    plus = (fr - hi, fi + hr)
    one, three = (minus, plus) if sign < 0 else (plus, minus)
    return ((er + gr, ei + gi), one, (er - gr, ei - gi), three)


def matmul_terms(left, right):
    left_high, left_low = left
    right_high, right_low = right
    return matmul(
        jnp.concatenate([left_high, left_high, left_low], 1),
        jnp.concatenate([right_high, right_low, right_high], 0),
    )


def rows_kernel(block, order_in, high_in, low_in, layer_in, out, order, high, low, layer, sems):
    copies = fetch(
        [(order_in, order)]
        + [pair for b in range(RADIX) for pair in ((high_in.at[b], high.at[b]), (low_in.at[b], low.at[b]))]
        + [(layer_in, layer)],
        sems,
    )
    groups, lines, width = block.shape
    points = groups * width
    sub = points // RADIX
    span = high.shape[2] // 2
    values = jnp.concatenate([block[t] for t in range(groups)], 1)
    both = jnp.concatenate(split(values), 0)
    copies[0].wait()
    both = matmul(both, order[...]).astype(BF16)
    parts = []
    for b in range(RADIX):
        data = both[:, b * sub : (b + 1) * sub]
        copies[1 + 2 * b].wait()
        copies[2 + 2 * b].wait()
        total = matmul_terms((data[:lines], data[lines:]), (high[b], low[b]))
        parts.append((total[:, :span], total[:, span:]))
    copies[-1].wait()
    slabs = span // width
    blocks = RADIX * slabs
    for u, (real, imag) in enumerate(turns(parts, -1)):
        data_high, data_low = split(jnp.concatenate([real, imag], 0))
        total = matmul(layer[...], jnp.concatenate([data_high, data_low, data_high], 0))
        rows = total.shape[0] // groups
        for t in range(groups):
            for slab in range(slabs):
                out[t * blocks + u * slabs + slab] = total[
                    t * rows : (t + 1) * rows, slab * width : (slab + 1) * width
                ]


def spectrum_kernel(
    data, tensor_in, high_in, low_in, back_high_in, back_low_in, out,
    tensor, high, low, back_high, back_low, sums, fields_high, fields_low, sems
):
    comps = 3
    senders, lines, width = data.shape
    blocks = 16
    quarters = senders // blocks // RADIX
    units = lines // 8
    members = units // comps
    span = high.shape[1] // 2
    pairs = []
    for b in range(RADIX):
        pairs += [(high_in.at[b], high.at[b]), (low_in.at[b], low.at[b])]
    pairs += [(tensor_in, tensor)]
    for b in range(RADIX):
        pairs += [(back_high_in.at[b], back_high.at[b]), (back_low_in.at[b], back_low.at[b])]
    copies = fetch(pairs, sems)
    for b in range(RADIX):
        pieces = []
        for unit in range(units):
            tall = [
                data[(b + RADIX * q) * blocks : (b + RADIX * q + 1) * blocks, unit * 8 : unit * 8 + 8, :]
                for q in range(quarters)
            ]
            pieces.append(jnp.concatenate(tall, 0).reshape(quarters * blocks * 8, width))
        copies[2 * b].wait()
        copies[2 * b + 1].wait()
        sums[b] = matmul_terms((high[b], low[b]), split(jnp.concatenate(pieces, 1)))
    copies[2 * RADIX].wait()
    piece = 16

    def multiply(step, carry):
        at = pl.multiple_of(step * piece, piece)
        for member in range(members):
            spectra = []
            for comp in range(comps):
                lanes = pl.ds((member * comps + comp) * width, width)
                t = [
                    (sums[b, pl.ds(at, piece), lanes], sums[b, pl.ds(span + at, piece), lanes])
                    for b in range(RADIX)
                ]
                spectra.append(turns(t, -1))
            field = [[None] * RADIX for _ in range(comps)]
            for u in range(RADIX):
                taps = [tensor[p, member, pl.ds(u * span + at, piece), :] for p in range(6)]
                for target in range(comps):
                    field[target][u] = tuple(
                        taps[PAIRS[target][0]] * spectra[0][u][part]
                        + taps[PAIRS[target][1]] * spectra[1][u][part]
                        + taps[PAIRS[target][2]] * spectra[2][u][part]
                        for part in range(2)
                    )
            for comp in range(comps):
                lanes = pl.ds((member * comps + comp) * width, width)
                for b, both in enumerate(turns(field[comp], 1)):
                    for part, value in enumerate(both):
                        data_high, data_low = split(value)
                        rows = pl.ds(part * span + at, piece)
                        fields_high[b, rows, lanes] = data_high
                        fields_low[b, rows, lanes] = data_low
        return carry

    lax.fori_loop(0, span // piece, multiply, 0)
    for b in range(RADIX):
        copies[2 * RADIX + 1 + 2 * b].wait()
        copies[2 * RADIX + 2 + 2 * b].wait()
        total = matmul_terms((back_high[b], back_low[b]), (fields_high[b], fields_low[b]))
        for q in range(quarters):
            group = b + RADIX * q
            tall = total[q * blocks * 8 : (q + 1) * blocks * 8]
            for unit in range(units):
                out[group * blocks : (group + 1) * blocks, unit * 8 : unit * 8 + 8, :] = tall[
                    :, unit * width : (unit + 1) * width
                ].reshape(blocks, 8, width)


def cells_kernel(data, layer_in, high_in, low_in, order_in, out, layer, high, low, order, sems, *, scale):
    copies = fetch(
        [(layer_in, layer)]
        + [pair for b in range(RADIX) for pair in ((high_in.at[b], high.at[b]), (low_in.at[b], low.at[b]))]
        + [(order_in, order)],
        sems,
    )
    groups, lines, width = out.shape
    span = high.shape[1] // 2
    slabs = span // width
    blocks = RADIX * slabs
    pieces = []
    copies[0].wait()
    for u in range(RADIX):
        columns = []
        for slab in range(slabs):
            at = u * slabs + slab
            columns.append(jnp.concatenate([data[t * blocks + at] for t in range(groups)], 0))
        data_high, data_low = split(jnp.concatenate(columns, 1))
        total = matmul(layer[...], jnp.concatenate([data_high, data_low, data_high], 0))
        pieces.append((total[:lines], total[lines:]))
    sorted_columns = []
    for b, both in enumerate(turns(pieces, 1)):
        copies[1 + 2 * b].wait()
        copies[2 + 2 * b].wait()
        sorted_columns.append(matmul_terms(split(jnp.concatenate(both, 1)), (high[b], low[b])))
    values = jnp.concatenate(sorted_columns, 1) * scale
    data_high, data_mid = split(values)
    data_low = (values - data_high.astype(F32) - data_mid.astype(F32)).astype(BF16)
    copies[-1].wait()
    total = matmul(jnp.concatenate([data_high, data_mid, data_low], 0), order[...])
    values = total[:lines] + total[lines : 2 * lines] + total[2 * lines :]
    for t in range(groups):
        out[t] = values[:, t * width : (t + 1) * width]


def place_kernel(block, out):
    groups, lines, width = block.shape
    layers = 8
    count = out.shape[0] // (3 * layers)
    strips = count // groups
    for comp in range(3):
        for y in range(count):
            strip, group = divmod(y, groups)
            at = (comp * strips + strip) * layers
            out[pl.ds(comp * layers * count + y, layers, stride=count), :] = block[
                group, at : at + layers, :
            ]


def near(shape, dtype):
    return pltpu.VMEM(shape, dtype)


def call(kernel, out_shape, in_specs, scratch=(), megabytes=16, flops=0, bytes_accessed=0):
    many = isinstance(out_shape, (list, tuple))
    return pl.pallas_call(
        kernel,
        out_shape=out_shape,
        in_specs=in_specs,
        out_specs=[VMEM] * len(out_shape) if many else VMEM,
        scratch_shapes=list(scratch),
        compiler_params=pltpu.CompilerParams(vmem_limit_bytes=megabytes * 1024 * 1024),
        cost_estimate=pl.CostEstimate(
            flops=flops, bytes_accessed=bytes_accessed, transcendentals=0
        ),
    )


def far(value):
    return pltpu.with_memory_space_constraint(value, pltpu.HBM)


def with_tables(kernel, out_shape, operand, tables, scratch=(), copies=0, megabytes=32):
    tables = [jnp.asarray(a) for a in tables]
    return call(
        kernel,
        out_shape,
        [VMEM] + [ANY] * len(tables),
        [pltpu.VMEM(a.shape, a.dtype) for a in tables]
        + list(scratch)
        + [pltpu.SemaphoreType.DMA((copies,))],
        megabytes=megabytes,
    )(operand, *[far(a) for a in tables])


def local(
    tx, ty, order, heat, kind, moment, tensor, nodes, factor, threshold, spot_row, spot_col
):
    layers, count, width = heat.shape
    strips = count // tx
    comps = 3
    lines = comps * strips * layers
    points_x, points_y = tx * width, ty * count
    members = 2
    cells = layers * count

    heat = heat.reshape(cells, width)
    kind = kind.reshape(cells, width)
    moment = moment.reshape(comps * cells, width)
    heat, gains, limits, sides, rows = call(
        edges_kernel,
        [near((cells, width), F32)] * 3
        + [near((2, layers, width), F32), near((2, 4, layers, width), F32)],
        [ANY] * 4,
        [
            pltpu.VMEM((cells, width), jnp.int32),
            pltpu.SMEM(factor.shape, F32),
            pltpu.SMEM(threshold.shape, F32),
            pltpu.SemaphoreType.DMA((4,)),
        ],
    )(far(heat), far(kind), far(factor), far(threshold))

    def moved(value, axis, step, wrap):
        size = tx if axis == "tx" else ty
        pairs = [(i, (i + step) % size) for i in range(size) if wrap or 0 <= i + step < size]
        return lax.ppermute(value, axis, pairs)

    left = moved(sides, "tx", 1, True)
    right = moved(sides, "tx", -1, True)
    upward, downward = call(join_kernel, [near((8, layers, width), F32)] * 2, [VMEM] * 3)(
        rows, left, right
    )
    above = moved(downward, "ty", 1, False)
    below = moved(upward, "ty", -1, False)
    warmed, scaled = call(
        functools.partial(heat_kernel, total_rows=points_y, total_cols=points_x),
        [
            jax.ShapeDtypeStruct((cells, width), F32),
            near((tx, lines, width), F32),
        ],
        [VMEM] * 3 + [ANY] + [VMEM] * 4 + [ANY] * 3,
        [
            pltpu.VMEM((comps * cells, width), F32),
            pltpu.SMEM(nodes.shape, F32),
            pltpu.SMEM(spot_row.shape, jnp.int32),
            pltpu.SMEM(spot_col.shape, jnp.int32),
            pltpu.SemaphoreType.DMA((4,)),
        ],
    )(
        heat, gains, limits, far(moment), above, below, left, right,
        far(nodes), far(spot_row), far(spot_col),
    )

    layer, layer_back = layer_tables(layers, strips, comps, order)
    along, along_back, sort = along_tables(points_x, tx)
    across, across_back = across_tables(points_y, tx, ty, strips)
    senders = tx * ty
    message = members * comps * 2 * strips
    span = 2 * points_y // RADIX

    def tripled(table):
        high, low = two_terms(table)
        return np.concatenate([high, high, low], 1)

    block = lax.all_to_all(scaled, "tx", split_axis=0, concat_axis=0, tiled=True)
    spectra = with_tables(
        rows_kernel,
        jax.ShapeDtypeStruct((senders, message, width), F32),
        block,
        [sort, *two_terms(along), tripled(layer)],
        copies=2 + 2 * RADIX,
    )
    data = lax.all_to_all(spectra, ("tx", "ty"), split_axis=0, concat_axis=0, tiled=True)
    columns = members * comps * width
    field = with_tables(
        spectrum_kernel,
        jax.ShapeDtypeStruct(data.shape, F32),
        data,
        [tensor, *two_terms(across), *two_terms(across_back)],
        [
            pltpu.VMEM((RADIX, 2 * span, columns), F32),
            pltpu.VMEM((RADIX, 2 * span, columns), BF16),
            pltpu.VMEM((RADIX, 2 * span, columns), BF16),
        ],
        copies=1 + 4 * RADIX,
        megabytes=44,
    )
    data = lax.all_to_all(field, ("tx", "ty"), split_axis=0, concat_axis=0, tiled=True)
    scale = -1.0 / (2 * layers * 2 * points_y * 2 * points_x)
    block = with_tables(
        functools.partial(cells_kernel, scale=scale),
        near((tx, lines, width), F32),
        data,
        [tripled(layer_back), *two_terms(along_back), np.ascontiguousarray(sort.T)],
        copies=2 + 2 * RADIX,
    )
    block = lax.all_to_all(block, "tx", split_axis=0, concat_axis=0, tiled=True)
    demag = call(place_kernel, jax.ShapeDtypeStruct((comps * cells, width), F32), [VMEM])(block)
    return (
        warmed.reshape(layers, count, width),
        demag.reshape(comps, layers, count, width),
    )


def solution(mesh):
    in_specs = (
        P(None, "ty", "tx"),
        P(None, "ty", "tx"),
        P(None, None, "ty", "tx"),
        P(None, "tx", None, "ty"),
        P(),
        P(),
        P(),
        P(),
        P(),
    )
    out_specs = (P(None, "ty", "tx"), P(None, None, "ty", "tx"))
    body = functools.partial(local, mesh.shape["tx"], mesh.shape["ty"], "whole")
    return jax.shard_map(body, mesh=mesh, in_specs=in_specs, out_specs=out_specs, check_vma=False)
```

time: 206 us -> 172 us (0.83)
  starting transfers between devices: 31.1 us -> 12.1 us
  local copies, waits for them, and re-layouts: 12 us -> 0 us
  waiting for transfers between devices: 2.83 us -> 8.83 us
  Pallas kernels: 34.9 us -> 29.1 us
  blocking collectives: 123 us -> 119 us
    ppermute x8 -> x4, starting transfers between devices: 31.1 us -> 12.1 us  [moved(): return lax.ppermute(value, axis, pairs)]
    unnamed x40 -> x0, local copies, waits for them, and re-layouts: 12 us -> none
    ppermute x8 -> x4, waiting for transfers between devices: 2.83 us -> 8.83 us  [moved(): return lax.ppermute(value, axis, pairs)]
    pallas_call x5 -> x6, Pallas kernels: 31 us -> 25.3 us  [the longest x3 22.9 us: with_tables(): call(kernel, out_shape, [VMEM] + [ANY] * len(tables), [pltpu.VMEM(a.shape...]
    all_to_all x1, blocking collectives: 16.4 us -> 11.9 us  [local(): lax.all_to_all(scaled, 'tx', split_axis=0, concat_axis=0, tiled=True)]
  transfers between devices with their start and end apart: 8 -> 4, of which waited for: 1 -> 3; matrix products, arithmetic and copies ran while one was open for 0% -> 0% of each run, Pallas kernels for 0% -> 0%
where the time goes in v2:
time: 172 us; the launch traced here: 170 us
  blocking collectives  119 us (69%)
  Pallas kernels  29.1 us (17%)
  starting transfers between devices  12.1 us (7%)
  waiting for transfers between devices  8.83 us (5%)
    all_to_all x1, blocking collectives, local(): lax.all_to_all(field, ('tx', 'ty'), split_axis=0, concat_axis=0, tiled=True)  46.5 us
    all_to_all x1, blocking collectives, local(): lax.all_to_all(spectra, ('tx', 'ty'), split_axis=0, concat_axis=0, tiled=...  45.3 us
    pallas_call x3, Pallas kernels, with_tables(): call(kernel, out_shape, [VMEM] + [ANY] * len(tables), [pltpu.VMEM(a.shape...  22.9 us
    all_to_all x1, blocking collectives, local(): block = lax.all_to_all(block, 'tx', split_axis=0, concat_axis=0, tiled=True)  15.7 us
    ppermute x4, starting transfers between devices, moved(): return lax.ppermute(value, axis, pairs)  12.1 us
    all_to_all x1, blocking collectives, local(): lax.all_to_all(scaled, 'tx', split_axis=0, concat_axis=0, tiled=True)  11.9 us
    ppermute x4, waiting for transfers between devices, moved(): return lax.ppermute(value, axis, pairs)  8.83 us
    pallas_call x1, Pallas kernels, local(): call(functools.partial(heat_kernel, total_rows=points_y, total_cols=point...  3.74 us
  transfers between devices with their start and end apart: 4, of which 3 were waited for; matrix products, arithmetic and copies ran while one was open for 0% of the time, Pallas kernels for 0%

profile of v2, /device:TPU:24, one launch (start us, length us, event | category | flops | bytes accessed | tf_op | source)
XLA Modules:
  0.0 170.1 jit_solution(4104359240150717616)
XLA Ops:
  0.6 1.5 shard_map.212
  2.1 6.6 %collective-permute-start.1 = (f32[2,8,128]{2,1,0:T(8,128)S(1)}, f32[2,8,128]{2,1,0:T(8,128)S(1)}, u32[]{:S(2)}, u32[]{:S(2)}) collective-permute-start(f32[2,8,128]{2,1,0:T(8,128)S(1)} %get-tuple-element.15), channel_id=1, source_target_pairs={{0,112},{16,0},{32,16},{48,32},{64,48},{80,64},{96,80},{112,96},{1... | collective-permute-start | bytes 24584 | tf_op jit(solution)/shard_map/ppermute | solution.py:555
  8.7 0.0 collective-permute-start
  8.7 1.4 collective-permute-done.1.right
  10.0 5.9 %collective-permute-done.left = f32[2,8,128]{2,1,0:T(8,128)S(1)} collective-permute-done((f32[2,8,128]{2,1,0:T(8,128)S(1)}, f32[2,8,128]{2,1,0:T(8,128)S(1)}, u32[]{:S(2)}, u32[]{:S(2)}) %collective-permute-start) | collective-permute-done | bytes 8224 | tf_op jit(solution)/shard_map/ppermute | solution.py:555
  15.9 1.9 %collective-permute-start.2 = (f32[8,8,128]{2,1,0:T(8,128)S(1)}, f32[8,8,128]{2,1,0:T(8,128)S(1)}, u32[]{:S(2)}, u32[]{:S(2)}) collective-permute-start(f32[8,8,128]{2,1,0:T(8,128)S(1)} %get-tuple-element.16), channel_id=1, source_target_pairs={{0,1},{1,2},{2,3},{3,4},{4,5},{5,6},{6,7},{7,8},{8,9},{9,10},{10,1... | collective-permute-start | bytes 98312 | tf_op jit(solution)/shard_map/ppermute | solution.py:555
  17.9 3.6 %collective-permute-start.3 = (f32[8,8,128]{2,1,0:T(8,128)S(1)}, f32[8,8,128]{2,1,0:T(8,128)S(1)}, u32[]{:S(2)}, u32[]{:S(2)}) collective-permute-start(f32[8,8,128]{2,1,0:T(8,128)S(1)} %get-tuple-element.17), channel_id=1, source_target_pairs={{1,0},{2,1},{3,2},{4,3},{5,4},{6,5},{7,6},{8,7},{9,8},{10,9},{11,1... | collective-permute-start | bytes 98312 | tf_op jit(solution)/shard_map/ppermute | solution.py:555
  21.5 0.0 collective-permute-done.2.above
  21.5 1.6 collective-permute-done.3.below
  23.1 3.7 %shard_map.214 = (f32[256,128]{1,0:T(8,128)}, f32[8,96,128]{2,1,0:T(8,128)S(1)}) custom-call(f32[256,128]{1,0:T(8,128)S(1)} %get-tuple-element.11.heat, f32[256,128]{1,0:T(8,128)S(1)} %get-tuple-element.12.gains_in, f32[256,128]{1,0:T(8,128)S(1)} %get-tuple-element.13.limits, f32[768,128]{1,0:T(8,128)} %bitcast.5, ...), custom_call_target="tpu_custom_call" | custom-call | tf_op jit(solution)/shard_map/pallas_call | solution.py:564
  26.8 11.9 %all_to_all.20.block = f32[8,96,128]{2,1,0:T(8,128)S(1)} all-to-all(f32[8,96,128]{2,1,0:T(8,128)S(1)} %get-tuple-element.19), channel_id=1, replica_groups=mesh['tx'=8,'ty'=16] {'tx'}, dimensions={0} | all-to-all | bytes 786432 | tf_op jit(solution)/shard_map/all_to_all | solution.py:594
  38.7 5.3 %shard_map.215 = f32[128,48,128]{2,1,0:T(8,128)S(1)} custom-call(f32[8,96,128]{2,1,0:T(8,128)S(1)} %all_to_all.20.block, bf16[1024,1024]{1,0:T(8,128)(2,1)} %constant.24.clone.order_in, bf16[4,256,1024]{2,1,0:T(8,128)(2,1)} %constant.25.clone.high_in, bf16[4,256,1024]{2,1,0:T(8,128)(2,1)} %constant.26.clone.low_in, bf16[384,576]{1,0:T(8,128)(2,1)} %constant.27.clone.layer_in), custom_call_target="tpu_custom_call" | custom-call | tf_op jit(solution)/shard_map/pallas_call | solution.py:514
  44.1 45.3 %all_to_all.21.data = f32[128,48,128]{2,1,0:T(8,128)S(1)} all-to-all(f32[128,48,128]{2,1,0:T(8,128)S(1)} %shard_map.215), channel_id=1, replica_groups=mesh['tx'=8,'ty'=16] {'tx','ty'}, dimensions={0} | all-to-all | bytes 6291456 | tf_op jit(solution)/shard_map/all_to_all | solution.py:602
  89.3 12.1 %shard_map.216 = f32[128,48,128]{2,1,0:T(8,128)S(1)} custom-call(f32[128,48,128]{2,1,0:T(8,128)S(1)} %all_to_all.21.data, f32[6,2,1024,128]{3,2,1,0:T(8,128)} %tensor_in.1, bf16[4,512,256]{2,1,0:T(8,128)(2,1)} %constant.28.clone.high_in, bf16[4,512,256]{2,1,0:T(8,128)(2,1)} %constant.29.clone.low_in, bf16[4,256,512]{2,1,0:T(8,128)(2,1)} %constant.30.clone.back_high_in, ...), custom_call_target="tpu_custom_call" | custom-call | tf_op jit(solution)/shard_map/pallas_call | solution.py:514
  101.5 46.5 %all_to_all.22.data = f32[128,48,128]{2,1,0:T(8,128)S(1)} all-to-all(f32[128,48,128]{2,1,0:T(8,128)S(1)} %shard_map.216), channel_id=1, replica_groups=mesh['tx'=8,'ty'=16] {'tx','ty'}, dimensions={0} | all-to-all | bytes 6291456 | tf_op jit(solution)/shard_map/all_to_all | solution.py:617
  148.0 5.4 %shard_map.217 = f32[8,96,128]{2,1,0:T(8,128)S(1)} custom-call(f32[128,48,128]{2,1,0:T(8,128)S(1)} %all_to_all.22.data, bf16[192,1152]{1,0:T(8,128)(2,1)} %constant.32.clone.layer_in, bf16[4,1024,256]{2,1,0:T(8,128)(2,1)} %constant.33.clone.high_in, bf16[4,1024,256]{2,1,0:T(8,128)(2,1)} %constant.34.clone.low_in, bf16[1024,1024]{1,0:T(8,128)(2,1)} %constant.35.clone.order_in), custom_call_target="tpu_custom_call" | custom-call | tf_op jit(solution)/shard_map/pallas_call | solution.py:514
  153.4 15.7 %all_to_all.23.block = f32[8,96,128]{2,1,0:T(8,128)S(1)} all-to-all(f32[8,96,128]{2,1,0:T(8,128)S(1)} %shard_map.217), channel_id=1, replica_groups=mesh['tx'=8,'ty'=16] {'tx'}, dimensions={0} | all-to-all | bytes 786432 | tf_op jit(solution)/shard_map/all_to_all | solution.py:626
  169.1 1.0 shard_map.218
  (1 shorter events, 0.0 us)
Async XLA Ops:
  2.1 7.9 %collective-permute-start.1 = (f32[2,8,128]{2,1,0:T(8,128)S(1)}, f32[2,8,128]{2,1,0:T(8,128)S(1)}, u32[]{:S(2)}, u32[]{:S(2)}) collective-permute-start(f32[2,8,128]{2,1,0:T(8,128)S(1)} %get-tuple-element.15), channel_id=1, source_target_pairs={{0,112},{16,0},{32,16},{48,32},{64,48},{80,64},{96,80},{112,96},{1... | collective-permute-start | bytes 24584 | tf_op jit(solution)/shard_map/ppermute | solution.py:555
  8.7 7.3 %collective-permute-start = (f32[2,8,128]{2,1,0:T(8,128)S(1)}, f32[2,8,128]{2,1,0:T(8,128)S(1)}, u32[]{:S(2)}, u32[]{:S(2)}) collective-permute-start(f32[2,8,128]{2,1,0:T(8,128)S(1)} %get-tuple-element.15), channel_id=1, source_target_pairs={{0,16},{16,32},{32,48},{48,64},{64,80},{80,96},{96,112},{112,0},{1... | collective-permute-start | bytes 24584 | tf_op jit(solution)/shard_map/ppermute | solution.py:555
  15.9 5.6 %collective-permute-start.2 = (f32[8,8,128]{2,1,0:T(8,128)S(1)}, f32[8,8,128]{2,1,0:T(8,128)S(1)}, u32[]{:S(2)}, u32[]{:S(2)}) collective-permute-start(f32[8,8,128]{2,1,0:T(8,128)S(1)} %get-tuple-element.16), channel_id=1, source_target_pairs={{0,1},{1,2},{2,3},{3,4},{4,5},{5,6},{6,7},{7,8},{8,9},{9,10},{10,1... | collective-permute-start | bytes 98312 | tf_op jit(solution)/shard_map/ppermute | solution.py:555
  17.9 5.2 %collective-permute-start.3 = (f32[8,8,128]{2,1,0:T(8,128)S(1)}, f32[8,8,128]{2,1,0:T(8,128)S(1)}, u32[]{:S(2)}, u32[]{:S(2)}) collective-permute-start(f32[8,8,128]{2,1,0:T(8,128)S(1)} %get-tuple-element.17), channel_id=1, source_target_pairs={{1,0},{2,1},{3,2},{4,3},{5,4},{6,5},{7,6},{8,7},{9,8},{10,9},{11,1... | collective-permute-start | bytes 98312 | tf_op jit(solution)/shard_map/ppermute | solution.py:555

commit v3 on v2

v3 whole, which is shorter than its diff:
```python
import functools
import math

import jax
import jax.numpy as jnp
import ml_dtypes
import numpy as np
from jax import lax
from jax.experimental import pallas as pl
from jax.experimental.pallas import tpu as pltpu
from jax.sharding import PartitionSpec as P

SWEEPS = 2
AMBIENT_HEAT = 0.3
STEP_RATE = 0.05
LASER_POWER = 4.0
LASER_DEPTH = 4.0
ORDERING_SPREAD = 0.08
TABLE_LOW = 0.2
TABLE_SPAN = 1.6
RADIX = 4
REACH = SWEEPS
PAIRS = ((0, 3, 4), (3, 1, 5), (4, 5, 2))
VMEM = pl.BlockSpec(memory_space=pltpu.VMEM)
ANY = pl.BlockSpec(memory_space=pl.ANY)
F32 = jnp.float32
BF16 = jnp.bfloat16


def two_terms(table):
    table = np.asarray(table, np.float64)
    high = table.astype(np.float32).astype(ml_dtypes.bfloat16)
    low = (table - high.astype(np.float64)).astype(np.float32).astype(ml_dtypes.bfloat16)
    return (high, low)


def waves(products, length):
    angles = 2.0 * math.pi / length * (products % length)
    return (np.cos(angles), np.sin(angles))


def split(values):
    high = values.astype(BF16)
    low = (values - high.astype(F32)).astype(BF16)
    return (high, low)


def matmul(left, right):
    return lax.dot_general(left, right, (((1,), (0,)), ((), ())), preferred_element_type=F32)


def layer_tables(layers, strips, comps, order):
    count = 2 * layers
    owners = count // 2
    rows_in = comps * strips * layers
    if order == "whole":
        shape = (owners, 2, comps, 2, strips)
    else:
        shape = (2, owners, comps, 2, strips)
    index = np.indices(shape).reshape(5, -1)
    if order == "whole":
        owner, member, comp, part, strip = index
    else:
        member, owner, comp, part, strip = index
    freq = 2 * owner + member
    comp_in, strip_in, layer_in = np.indices((comps, strips, layers)).reshape(3, -1)
    same = (comp[:, None] == comp_in[None]) & (strip[:, None] == strip_in[None])
    cosine, sine = waves(freq[:, None] * layer_in[None], count)
    zero = part[:, None] == 0
    from_real = np.where(zero, cosine, -sine) * same
    from_imag = np.where(zero, sine, cosine) * same
    forward = np.concatenate([from_real, from_imag], 1)
    return forward, forward.T


def along_tables(points, devices):
    length = 2 * points
    span = length // RADIX
    sub = points // RADIX
    a = np.arange(sub)
    v = np.arange(span)
    forward = np.zeros((RADIX, sub, 2 * span))
    for b in range(RADIX):
        cosine, sine = waves(v[None, :] * (RADIX * a + b)[:, None], length)
        forward[b] = np.concatenate([cosine, -sine], 1)
    order = np.zeros((points, points), np.float32)
    for b in range(RADIX):
        order[RADIX * a + b, b * sub + a] = 1.0
    return forward, forward.transpose(0, 2, 1), order.astype(ml_dtypes.bfloat16)


def across_tables(points, groups, blocks, strips):
    length = 2 * points
    span = length // RADIX
    part, group, block = np.indices((2, groups, blocks)).reshape(3, -1)
    v = np.arange(span)
    forward = np.zeros((RADIX, 2 * span, part.size))
    for b in range(RADIX):
        y = strips * (groups * block + group) + b
        cosine, sine = waves(v[:, None] * y[None, :], length)
        zero = part[None, :] == 0
        forward[b, :span] = np.where(zero, cosine, sine)
        forward[b, span:] = np.where(zero, -sine, cosine)
    return forward, forward.transpose(0, 2, 1)


def fetch(pairs, sems):
    copies = [
        pltpu.make_async_copy(source, target, sems.at[at])
        for at, (source, target) in enumerate(pairs)
    ]
    for copy in copies:
        copy.start()
    return copies


def chosen(which, values):
    total = jnp.zeros(which.shape, F32)
    for grain in range(values.shape[0]):
        total = total + jnp.where(which == grain, values[grain], 0.0)
    return total


def edges_kernel(heat_in, kind_in, moment_in, heat, kind, moment, rows, sems):
    copies = fetch([(heat_in, heat), (kind_in, kind), (moment_in, moment)], sems)
    layers, count = 8, heat.shape[0] // 8
    copies[0].wait()
    copies[1].wait()
    for side, first in enumerate((0, count - REACH)):
        for j in range(REACH):
            at = pl.ds(first + j, layers, stride=count)
            rows[side, j] = heat[at, :]
            rows[side, REACH + j] = kind[at, :].astype(F32)
    copies[2].wait()


def send_kernel(heat, kind, moment, above, below, out):
    layers, count = 8, heat.shape[0] // 8
    groups = out.shape[0]
    strips = count // groups
    tall = strips + 2 * REACH
    for group in range(groups):
        for i in range(tall):
            y = group * strips - REACH + i
            if y < 0:
                pair = (above[y + REACH], above[y + 2 * REACH])
            elif y >= count:
                pair = (below[y - count], below[y - count + REACH])
            else:
                at = pl.ds(y, layers, stride=count)
                pair = (heat[at, :], kind[at, :].astype(F32))
            for which, value in enumerate(pair):
                out[group, (which * tall + i) * layers : (which * tall + i + 1) * layers, :] = value
        for comp in range(3):
            for strip in range(strips):
                at = pl.ds(comp * layers * count + group * strips + strip, layers, stride=count)
                to = (2 * tall + comp * strips + strip) * layers
                out[group, to : to + layers, :] = moment[at, :]


def heat_rows(block, nodes, factor, threshold, spot_row, spot_col, total_rows):
    layers = 8
    groups, lines, width = block.shape
    total_cols = groups * width
    strips = (lines // layers - 4 * REACH) // 5
    tall = strips + 2 * REACH
    row_base = (lax.axis_index("ty") * groups + lax.axis_index("tx")) * strips - REACH
    shape = (layers, total_cols)
    column = lax.broadcasted_iota(jnp.int32, shape, 1)
    depth = lax.broadcasted_iota(jnp.int32, shape, 0)
    spacing = TABLE_SPAN / (nodes.shape[0] - 1)
    slopes = [(nodes[j + 1] - nodes[j]) * (1.0 / spacing) for j in range(nodes.shape[0] - 1)]

    def whole(index):
        at = index * layers
        return jnp.concatenate([block[t, at : at + layers, :] for t in range(groups)], 1)

    def chosen(which, values):
        total = jnp.zeros(which.shape, F32)
        for grain in range(values.shape[0]):
            total = total + jnp.where(which == float(grain), values[grain], 0.0)
        return total

    def conductivity(theta, gain):
        absolute = theta + AMBIENT_HEAT
        total = jnp.zeros_like(theta) + nodes[0]
        for j, slope in enumerate(slopes):
            total = total + slope * jnp.clip(absolute - (TABLE_LOW + j * spacing), 0.0, spacing)
        return gain * total

    inside = {}
    thetas = {}
    gains = {}
    for i in range(tall):
        y = row_base + i
        inside[i] = jnp.where((y >= 0) & (y < total_rows), 1.0, 0.0)
        thetas[i] = (whole(i) - AMBIENT_HEAT) * inside[i]
        gains[i] = chosen(whole(tall + i), factor) * inside[i]
    not_top = depth > 0
    not_bottom = depth < layers - 1
    for sweep in range(SWEEPS):
        shifted = column - spot_col[sweep] + total_cols // 2
        shifted = jnp.where(shifted < 0, shifted + total_cols, shifted)
        shifted = jnp.where(shifted >= total_cols, shifted - total_cols, shifted)
        offset = (shifted - total_cols // 2).astype(F32) * (1.0 / (0.5 * width))
        along = jnp.exp(depth.astype(F32) * (-1.0 / LASER_DEPTH)) * jnp.exp(-0.5 * offset * offset)
        k = {i: conductivity(thetas[i], gains[i]) for i in range(sweep, tall - sweep)}
        fresh = {}
        for i in range(sweep + 1, tall - sweep - 1):
            theta, own = thetas[i], k[i]
            flux = (own + k[i - 1]) * (thetas[i - 1] - theta)
            flux = flux + (own + k[i + 1]) * (thetas[i + 1] - theta)
            for turn in (1, total_cols - 1):
                flux = flux + (own + pltpu.roll(own, turn, 1)) * (pltpu.roll(theta, turn, 1) - theta)
            for turn, valid in ((1, not_top), (layers - 1, not_bottom)):
                part = (own + pltpu.roll(own, turn, 0)) * (pltpu.roll(theta, turn, 0) - theta)
                flux = flux + jnp.where(valid, part, 0.0)
            across = (row_base + i - spot_row[sweep]).astype(F32) * (1.0 / 32.0)
            across = jnp.exp(jnp.full((layers, width), -0.5, F32) * (across * across))
            source = along * jnp.concatenate([across] * groups, 1)
            value = theta + STEP_RATE * (0.5 * flux + LASER_POWER * source)
            fresh[i] = value * inside[i]
        thetas = fresh
    warmed = []
    fractions = []
    for strip in range(strips):
        value = thetas[REACH + strip] + AMBIENT_HEAT
        limit = chosen(whole(tall + REACH + strip), threshold)
        warmed.append(value)
        fractions.append(1.0 / (1.0 + jnp.exp((value - limit) * (1.0 / ORDERING_SPREAD))))
    scaled = []
    for comp in range(3):
        for strip in range(strips):
            scaled.append(whole(2 * tall + comp * strips + strip) * fractions[strip])
    return warmed, jnp.concatenate(scaled, 0)


def turns(t, sign):
    (ar, ai), (br, bi), (cr, ci), (dr, di) = t
    er, ei, fr, fi = ar + cr, ai + ci, ar - cr, ai - ci
    gr, gi, hr, hi = br + dr, bi + di, br - dr, bi - di
    minus = (fr + hi, fi - hr)
    plus = (fr - hi, fi + hr)
    one, three = (minus, plus) if sign < 0 else (plus, minus)
    return ((er + gr, ei + gi), one, (er - gr, ei - gi), three)


def matmul_terms(left, right):
    left_high, left_low = left
    right_high, right_low = right
    return matmul(
        jnp.concatenate([left_high, left_high, left_low], 1),
        jnp.concatenate([right_high, right_low, right_high], 0),
    )


def rows_kernel(
    block, order_in, high_in, low_in, layer_in, nodes_in, factor_in, threshold_in, spot_row_in, spot_col_in,
    out, warmed, order, high, low, layer, nodes, factor, threshold, spot_row, spot_col, sems, *, total_rows
):
    copies = fetch(
        [
            (nodes_in, nodes), (factor_in, factor), (threshold_in, threshold),
            (spot_row_in, spot_row), (spot_col_in, spot_col), (order_in, order),
        ]
        + [pair for b in range(RADIX) for pair in ((high_in.at[b], high.at[b]), (low_in.at[b], low.at[b]))]
        + [(layer_in, layer)],
        sems,
    )
    for copy in copies[:5]:
        copy.wait()
    copies = copies[5:]
    groups, _, width = block.shape
    points = groups * width
    sub = points // RADIX
    span = high.shape[2] // 2
    kept, values = heat_rows(block, nodes, factor, threshold, spot_row, spot_col, total_rows)
    lines = values.shape[0]
    for strip, value in enumerate(kept):
        for t in range(groups):
            warmed[t, strip * 8 : strip * 8 + 8, :] = value[:, t * width : (t + 1) * width]
    both = jnp.concatenate(split(values), 0)
    copies[0].wait()
    both = matmul(both, order[...]).astype(BF16)
    parts = []
    for b in range(RADIX):
        data = both[:, b * sub : (b + 1) * sub]
        copies[1 + 2 * b].wait()
        copies[2 + 2 * b].wait()
        total = matmul_terms((data[:lines], data[lines:]), (high[b], low[b]))
        parts.append((total[:, :span], total[:, span:]))
    copies[-1].wait()
    slabs = span // width
    blocks = RADIX * slabs
    for u, (real, imag) in enumerate(turns(parts, -1)):
        data_high, data_low = split(jnp.concatenate([real, imag], 0))
        total = matmul(layer[...], jnp.concatenate([data_high, data_low, data_high], 0))
        rows = total.shape[0] // groups
        for t in range(groups):
            for slab in range(slabs):
                out[t * blocks + u * slabs + slab] = total[
                    t * rows : (t + 1) * rows, slab * width : (slab + 1) * width
                ]


def spectrum_kernel(
    data, tensor_in, high_in, low_in, back_high_in, back_low_in, out,
    tensor, high, low, back_high, back_low, sums, fields_high, fields_low, sems
):
    comps = 3
    width = data.shape[1]
    senders = high.shape[2] // 2
    lines = data.shape[0] // senders
    units = lines // 8
    members = units // comps
    span = high.shape[1] // 2
    pairs = []
    for b in range(RADIX):
        pairs += [(high_in.at[b], high.at[b]), (low_in.at[b], low.at[b])]
    pairs += [(tensor_in, tensor)]
    for b in range(RADIX):
        pairs += [(back_high_in.at[b], back_high.at[b]), (back_low_in.at[b], back_low.at[b])]
    copies = fetch(pairs, sems)
    for b in range(RADIX):
        pieces = []
        for unit in range(units):
            both = [
                data[pl.ds(unit * 8 + part * RADIX + b, senders, stride=lines), :]
                for part in range(2)
            ]
            pieces.append(jnp.concatenate(both, 0))
        copies[2 * b].wait()
        copies[2 * b + 1].wait()
        sums[b] = matmul_terms((high[b], low[b]), split(jnp.concatenate(pieces, 1)))
    copies[2 * RADIX].wait()
    piece = 16

    def multiply(step, carry):
        at = pl.multiple_of(step * piece, piece)
        for member in range(members):
            spectra = []
            for comp in range(comps):
                lanes = pl.ds((member * comps + comp) * width, width)
                t = [
                    (sums[b, pl.ds(at, piece), lanes], sums[b, pl.ds(span + at, piece), lanes])
                    for b in range(RADIX)
                ]
                spectra.append(turns(t, -1))
            field = [[None] * RADIX for _ in range(comps)]
            for u in range(RADIX):
                taps = [tensor[p, member, pl.ds(u * span + at, piece), :] for p in range(6)]
                for target in range(comps):
                    field[target][u] = tuple(
                        taps[PAIRS[target][0]] * spectra[0][u][part]
                        + taps[PAIRS[target][1]] * spectra[1][u][part]
                        + taps[PAIRS[target][2]] * spectra[2][u][part]
                        for part in range(2)
                    )
            for comp in range(comps):
                lanes = pl.ds((member * comps + comp) * width, width)
                for b, both in enumerate(turns(field[comp], 1)):
                    for part, value in enumerate(both):
                        data_high, data_low = split(value)
                        rows = pl.ds(part * span + at, piece)
                        fields_high[b, rows, lanes] = data_high
                        fields_low[b, rows, lanes] = data_low
        return carry

    lax.fori_loop(0, span // piece, multiply, 0)
    for b in range(RADIX):
        copies[2 * RADIX + 1 + 2 * b].wait()
        copies[2 * RADIX + 2 + 2 * b].wait()
        total = matmul_terms((back_high[b], back_low[b]), (fields_high[b], fields_low[b]))
        for unit in range(units):
            for part in range(2):
                out[pl.ds(unit * 8 + part * RADIX + b, senders, stride=lines), :] = total[
                    part * senders : (part + 1) * senders, unit * width : (unit + 1) * width
                ]


def cells_kernel(data, kept, layer_in, high_in, low_in, order_in, out, layer, high, low, order, sems, *, scale):
    copies = fetch(
        [(layer_in, layer)]
        + [pair for b in range(RADIX) for pair in ((high_in.at[b], high.at[b]), (low_in.at[b], low.at[b]))]
        + [(order_in, order)],
        sems,
    )
    groups, _, width = out.shape
    lines = layer.shape[0] // 2
    span = high.shape[1] // 2
    slabs = span // width
    blocks = RADIX * slabs
    pieces = []
    copies[0].wait()
    for u in range(RADIX):
        columns = []
        for slab in range(slabs):
            at = u * slabs + slab
            columns.append(jnp.concatenate([data[t * blocks + at] for t in range(groups)], 0))
        data_high, data_low = split(jnp.concatenate(columns, 1))
        total = matmul(layer[...], jnp.concatenate([data_high, data_low, data_high], 0))
        pieces.append((total[:lines], total[lines:]))
    sorted_columns = []
    for b, both in enumerate(turns(pieces, 1)):
        copies[1 + 2 * b].wait()
        copies[2 + 2 * b].wait()
        sorted_columns.append(matmul_terms(split(jnp.concatenate(both, 1)), (high[b], low[b])))
    values = jnp.concatenate(sorted_columns, 1) * scale
    data_high, data_mid = split(values)
    data_low = (values - data_high.astype(F32) - data_mid.astype(F32)).astype(BF16)
    copies[-1].wait()
    total = matmul(jnp.concatenate([data_high, data_mid, data_low], 0), order[...])
    values = total[:lines] + total[lines : 2 * lines] + total[2 * lines :]
    for t in range(groups):
        out[t, :lines] = values[:, t * width : (t + 1) * width]
        out[t, lines:] = kept[t]


def place_kernel(block, field, warmed):
    groups, lines, width = block.shape
    layers = 8
    count = warmed.shape[0] // layers
    strips = count // groups
    for y in range(count):
        group, strip = divmod(y, strips)
        for comp in range(4):
            at = (comp * strips + strip) * layers
            value = block[group, at : at + layers, :]
            if comp < 3:
                field[pl.ds(comp * layers * count + y, layers, stride=count), :] = value
            else:
                warmed[pl.ds(y, layers, stride=count), :] = value


def near(shape, dtype):
    return pltpu.VMEM(shape, dtype)


def call(kernel, out_shape, in_specs, scratch=(), megabytes=16, flops=0, bytes_accessed=0):
    many = isinstance(out_shape, (list, tuple))
    return pl.pallas_call(
        kernel,
        out_shape=out_shape,
        in_specs=in_specs,
        out_specs=[VMEM] * len(out_shape) if many else VMEM,
        scratch_shapes=list(scratch),
        compiler_params=pltpu.CompilerParams(vmem_limit_bytes=megabytes * 1024 * 1024),
        cost_estimate=pl.CostEstimate(
            flops=flops, bytes_accessed=bytes_accessed, transcendentals=0
        ),
    )


def far(value):
    return pltpu.with_memory_space_constraint(value, pltpu.HBM)


def with_tables(
    kernel, out_shape, operands, tables, scalars=(), scratch=(), copies=0, megabytes=32
):
    tables = [jnp.asarray(a) for a in tables]
    return call(
        kernel,
        out_shape,
        [VMEM] * len(operands) + [ANY] * (len(tables) + len(scalars)),
        [pltpu.VMEM(a.shape, a.dtype) for a in tables]
        + [pltpu.SMEM(a.shape, a.dtype) for a in scalars]
        + list(scratch)
        + [pltpu.SemaphoreType.DMA((copies,))],
        megabytes=megabytes,
    )(*operands, *[far(a) for a in tables], *[far(a) for a in scalars])


def local(
    tx, ty, order, heat, kind, moment, tensor, nodes, factor, threshold, spot_row, spot_col
):
    layers, count, width = heat.shape
    strips = count // tx
    comps = 3
    lines = comps * strips * layers
    points_x, points_y = tx * width, ty * count
    members = 2
    cells = layers * count

    heat = heat.reshape(cells, width)
    kind = kind.reshape(cells, width)
    moment = moment.reshape(comps * cells, width)
    heat, kind, moment, rows = call(
        edges_kernel,
        [
            near((cells, width), F32),
            near((cells, width), jnp.int32),
            near((comps * cells, width), F32),
            near((2, 2 * REACH, layers, width), F32),
        ],
        [ANY] * 3,
        [pltpu.SemaphoreType.DMA((3,))],
    )(far(heat), far(kind), far(moment))

    def moved(value, step):
        pairs = [(i, i + step) for i in range(ty) if 0 <= i + step < ty]
        return lax.ppermute(value, "ty", pairs)

    above = moved(rows[1], 1)
    below = moved(rows[0], -1)
    tall = 2 * (strips + 2 * REACH) + comps * strips
    block = call(send_kernel, near((tx, tall * layers, width), F32), [VMEM] * 5)(
        heat, kind, moment, above, below
    )
    block = lax.all_to_all(block, "tx", split_axis=0, concat_axis=0, tiled=True)

    layer, layer_back = layer_tables(layers, strips, comps, order)
    along, along_back, sort = along_tables(points_x, tx)
    across, across_back = across_tables(points_y, tx, ty, strips)
    senders = tx * ty
    message = members * comps * 2 * strips
    span = 2 * points_y // RADIX

    def tripled(table):
        high, low = two_terms(table)
        return np.concatenate([high, high, low], 1)

    spectra, warmed = with_tables(
        functools.partial(rows_kernel, total_rows=points_y),
        [
            jax.ShapeDtypeStruct((senders, message, width), F32),
            near((tx, strips * layers, width), F32),
        ],
        [block],
        [sort, *two_terms(along), tripled(layer)],
        [nodes, factor, threshold, spot_row, spot_col],
        copies=7 + 2 * RADIX,
    )
    data = lax.all_to_all(spectra, ("tx", "ty"), split_axis=0, concat_axis=0, tiled=True)
    columns = members * comps * width
    field = with_tables(
        spectrum_kernel,
        jax.ShapeDtypeStruct((senders * message, width), F32),
        [data.reshape(senders * message, width)],
        [tensor, *two_terms(across), *two_terms(across_back)],
        (),
        [
            pltpu.VMEM((RADIX, 2 * span, columns), F32),
            pltpu.VMEM((RADIX, 2 * span, columns), BF16),
            pltpu.VMEM((RADIX, 2 * span, columns), BF16),
        ],
        copies=1 + 4 * RADIX,
        megabytes=44,
    )
    field = field.reshape(senders, message, width)
    data = lax.all_to_all(field, ("tx", "ty"), split_axis=0, concat_axis=0, tiled=True)
    scale = -1.0 / (2 * layers * 2 * points_y * 2 * points_x)
    block = with_tables(
        functools.partial(cells_kernel, scale=scale),
        near((tx, lines + strips * layers, width), F32),
        [data, warmed],
        [tripled(layer_back), *two_terms(along_back), np.ascontiguousarray(sort.T)],
        copies=2 + 2 * RADIX,
    )
    block = lax.all_to_all(block, "tx", split_axis=0, concat_axis=0, tiled=True)
    demag, warmed = call(
        place_kernel,
        [jax.ShapeDtypeStruct((comps * cells, width), F32), jax.ShapeDtypeStruct((cells, width), F32)],
        [VMEM],
    )(block)
    return (
        warmed.reshape(layers, count, width),
        demag.reshape(comps, layers, count, width),
    )


def solution(mesh):
    in_specs = (
        P(None, "ty", "tx"),
        P(None, "ty", "tx"),
        P(None, None, "ty", "tx"),
        P(None, "tx", None, "ty"),
        P(),
        P(),
        P(),
        P(),
        P(),
    )
    out_specs = (P(None, "ty", "tx"), P(None, None, "ty", "tx"))
    body = functools.partial(local, mesh.shape["tx"], mesh.shape["ty"], "whole")
    return jax.shard_map(body, mesh=mesh, in_specs=in_specs, out_specs=out_specs, check_vma=False)
```

time: 172 us -> 169 us (0.983)
  blocking collectives: 119 us -> 131 us
  starting transfers between devices: 12.1 us -> 4.33 us
  waiting for transfers between devices: 8.83 us -> 2.81 us
    all_to_all x1 -> x2, blocking collectives: 15.7 us -> 41.7 us  [local(): block = lax.all_to_all(block, 'tx', split_axis=0, concat_axis=0, tiled=True)]
    all_to_all x1 -> x0, blocking collectives: 11.9 us -> none  [local(): lax.all_to_all(scaled, 'tx', split_axis=0, concat_axis=0, tiled=True)]
    ppermute x4 -> x2, starting transfers between devices: 12.1 us -> 4.33 us  [moved(): return lax.ppermute(value, 'ty', pairs)]
    ppermute x4 -> x2, waiting for transfers between devices: 8.83 us -> 2.81 us  [moved(): return lax.ppermute(value, 'ty', pairs)]
    all_to_all x1, blocking collectives: 45.3 us -> 43.1 us  [local(): lax.all_to_all(spectra, ('tx', 'ty'), split_axis=0, concat_axis=0, tiled=...]
    pallas_call x7 -> x6, Pallas kernels: 29.1 us -> 28.3 us  [the longest x3 25.5 us: with_tables(): call(kernel, out_shape, [VMEM] * len(operands) + [ANY] * (len(tables) + l...]
  transfers between devices with their start and end apart: 4 -> 2, of which waited for: 3 -> 1; matrix products, arithmetic and copies ran while one was open for 0% -> 0% of each run, Pallas kernels for 0% -> 0%
where the time goes in v3:
time: 169 us; the launch traced here: 167 us
  blocking collectives  131 us (78%)
  Pallas kernels  28.3 us (17%)
  starting transfers between devices  4.33 us (3%)
  waiting for transfers between devices  2.81 us (2%)
    all_to_all x1, blocking collectives, local(): lax.all_to_all(field, ('tx', 'ty'), split_axis=0, concat_axis=0, tiled=True)  46.5 us
    all_to_all x1, blocking collectives, local(): lax.all_to_all(spectra, ('tx', 'ty'), split_axis=0, concat_axis=0, tiled=...  43.1 us
    all_to_all x2, blocking collectives, local(): block = lax.all_to_all(block, 'tx', split_axis=0, concat_axis=0, tiled=True)  41.7 us
    pallas_call x3, Pallas kernels, with_tables(): call(kernel, out_shape, [VMEM] * len(operands) + [ANY] * (len(tables) + l...  25.5 us
    ppermute x2, starting transfers between devices, moved(): return lax.ppermute(value, 'ty', pairs)  4.33 us
  transfers between devices with their start and end apart: 2, of which 1 were waited for; matrix products, arithmetic and copies ran while one was open for 0% of the time, Pallas kernels for 0%

profile of v3, /device:TPU:24, one launch (start us, length us, event | category | flops | bytes accessed | tf_op | source)
XLA Modules:
  0.0 167.5 jit_solution(15608593868574836695)
XLA Ops:
  0.6 1.2 shard_map.212
  1.8 2.1 %collective-permute-start.1 = (f32[4,8,128]{2,1,0:T(8,128)S(1)}, f32[4,8,128]{2,1,0:T(8,128)S(1)}, u32[]{:S(2)}, u32[]{:S(2)}) collective-permute-start(f32[4,8,128]{2,1,0:T(8,128)S(1)} %get-tuple-element.18), channel_id=1, source_target_pairs={{1,0},{2,1},{3,2},{4,3},{5,4},{6,5},{7,6},{8,7},{9,8},{10,9},{11,1... | collective-permute-start | bytes 49160 | tf_op jit(solution)/shard_map/ppermute | solution.py:502
  3.9 2.2 %collective-permute-start = (f32[4,8,128]{2,1,0:T(8,128)S(1)}, f32[4,8,128]{2,1,0:T(8,128)S(1)}, u32[]{:S(2)}, u32[]{:S(2)}) collective-permute-start(f32[4,8,128]{2,1,0:T(8,128)S(1)} %get-tuple-element.19), channel_id=1, source_target_pairs={{0,1},{1,2},{2,3},{3,4},{4,5},{5,6},{6,7},{7,8},{8,9},{9,10},{10,1... | collective-permute-start | bytes 49160 | tf_op jit(solution)/shard_map/ppermute | solution.py:502
  6.2 0.0 collective-permute-done.1.below
  6.2 2.8 %collective-permute-done.above = f32[4,8,128]{2,1,0:T(8,128)S(1)} collective-permute-done((f32[4,8,128]{2,1,0:T(8,128)S(1)}, f32[4,8,128]{2,1,0:T(8,128)S(1)}, u32[]{:S(2)}, u32[]{:S(2)}) %collective-permute-start) | collective-permute-done | bytes 16416 | tf_op jit(solution)/shard_map/ppermute | solution.py:502
  9.0 0.4 shard_map.213
  9.4 24.7 %all_to_all.20.block = f32[8,224,128]{2,1,0:T(8,128)S(1)} all-to-all(f32[8,224,128]{2,1,0:T(8,128)S(1)} %shard_map.213), channel_id=1, replica_groups=mesh['tx'=8,'ty'=16] {'tx'}, dimensions={0} | all-to-all | bytes 1835008 | tf_op jit(solution)/shard_map/all_to_all | solution.py:510
  34.0 6.5 %shard_map.214 = (f32[128,48,128]{2,1,0:T(8,128)S(1)}, f32[8,32,128]{2,1,0:T(8,128)S(1)}) custom-call(f32[8,224,128]{2,1,0:T(8,128)S(1)} %all_to_all.20.block, bf16[1024,1024]{1,0:T(8,128)(2,1)} %constant.24.clone.order_in, bf16[4,256,1024]{2,1,0:T(8,128)(2,1)} %constant.25.clone.high_in, bf16[4,256,1024]{2,1,0:T(8,128)(2,1)} %constant.26.clone.low_in, ...), custom_call_target="tpu_custom_call" | custom-call | tf_op jit(solution)/shard_map/pallas_call | solution.py:462
  40.5 43.1 %all_to_all.21 = f32[128,48,128]{2,1,0:T(8,128)S(1)} all-to-all(f32[128,48,128]{2,1,0:T(8,128)S(1)} %get-tuple-element.14), channel_id=1, replica_groups=mesh['tx'=8,'ty'=16] {'tx','ty'}, dimensions={0} | all-to-all | bytes 6291456 | tf_op jit(solution)/shard_map/all_to_all | solution.py:534
  83.6 13.6 %shard_map.215 = f32[6144,128]{1,0:T(8,128)S(1)} custom-call(f32[6144,128]{1,0:T(8,128)S(1)} %bitcast.11, f32[6,2,1024,128]{3,2,1,0:T(8,128)} %tensor_in.1, bf16[4,512,256]{2,1,0:T(8,128)(2,1)} %constant.28.clone.high_in, bf16[4,512,256]{2,1,0:T(8,128)(2,1)} %constant.29.clone.low_in, bf16[4,256,512]{2,1,0:T(8,128)(2,1)} %constant.30.clone.back_high_in, ...), custom_call_target="tpu_custom_call" | custom-call | tf_op jit(solution)/shard_map/pallas_call | solution.py:462
  97.2 46.5 %all_to_all.22.data = f32[128,48,128]{2,1,0:T(8,128)S(1)} all-to-all(f32[128,48,128]{2,1,0:T(8,128)S(1)} %bitcast.12), channel_id=1, replica_groups=mesh['tx'=8,'ty'=16] {'tx','ty'}, dimensions={0} | all-to-all | bytes 6291456 | tf_op jit(solution)/shard_map/all_to_all | solution.py:551
  143.7 5.4 %shard_map.216 = f32[8,128,128]{2,1,0:T(8,128)S(1)} custom-call(f32[128,48,128]{2,1,0:T(8,128)S(1)} %all_to_all.22.data, f32[8,32,128]{2,1,0:T(8,128)S(1)} %get-tuple-element.15.kept, bf16[192,1152]{1,0:T(8,128)(2,1)} %constant.32.clone.layer_in, bf16[4,1024,256]{2,1,0:T(8,128)(2,1)} %constant.33.clone.high_in, bf16[4,1024,256]{2,1,0:T(8,128)(2,1)} %constant.34.clone.low_in, ...), custom_call_target="tpu_custom_call" | custom-call | tf_op jit(solution)/shard_map/pallas_call | solution.py:462
  149.1 17.1 %all_to_all.23.block = f32[8,128,128]{2,1,0:T(8,128)S(1)} all-to-all(f32[8,128,128]{2,1,0:T(8,128)S(1)} %shard_map.216), channel_id=1, replica_groups=mesh['tx'=8,'ty'=16] {'tx'}, dimensions={0} | all-to-all | bytes 1048576 | tf_op jit(solution)/shard_map/all_to_all | solution.py:560
  166.2 1.3 shard_map.217
  (1 shorter events, 0.0 us)
Async XLA Ops:
  1.8 4.3 %collective-permute-start.1 = (f32[4,8,128]{2,1,0:T(8,128)S(1)}, f32[4,8,128]{2,1,0:T(8,128)S(1)}, u32[]{:S(2)}, u32[]{:S(2)}) collective-permute-start(f32[4,8,128]{2,1,0:T(8,128)S(1)} %get-tuple-element.18), channel_id=1, source_target_pairs={{1,0},{2,1},{3,2},{4,3},{5,4},{6,5},{7,6},{8,7},{9,8},{10,9},{11,1... | collective-permute-start | bytes 49160 | tf_op jit(solution)/shard_map/ppermute | solution.py:502
  3.9 5.1 %collective-permute-start = (f32[4,8,128]{2,1,0:T(8,128)S(1)}, f32[4,8,128]{2,1,0:T(8,128)S(1)}, u32[]{:S(2)}, u32[]{:S(2)}) collective-permute-start(f32[4,8,128]{2,1,0:T(8,128)S(1)} %get-tuple-element.19), channel_id=1, source_target_pairs={{0,1},{1,2},{2,3},{3,4},{4,5},{5,6},{6,7},{7,8},{8,9},{9,10},{10,1... | collective-permute-start | bytes 49160 | tf_op jit(solution)/shard_map/ppermute | solution.py:502

commit v4 on v3

--- a/solution.py
+++ b/solution.py
@@ -283,13 +283,12 @@
     copies[0].wait()
     both = matmul(both, order[...]).astype(BF16)
     parts = []
+    for copy in copies[1:]:
+        copy.wait()
     for b in range(RADIX):
         data = both[:, b * sub : (b + 1) * sub]
-        copies[1 + 2 * b].wait()
-        copies[2 + 2 * b].wait()
         total = matmul_terms((data[:lines], data[lines:]), (high[b], low[b]))
         parts.append((total[:, :span], total[:, span:]))
-    copies[-1].wait()
     slabs = span // width
     blocks = RADIX * slabs
     for u, (real, imag) in enumerate(turns(parts, -1)):
@@ -321,6 +320,8 @@
     for b in range(RADIX):
         pairs += [(back_high_in.at[b], back_high.at[b]), (back_low_in.at[b], back_low.at[b])]
     copies = fetch(pairs, sems)
+    for copy in copies[: 2 * RADIX]:
+        copy.wait()
     for b in range(RADIX):
         pieces = []
         for unit in range(units):
@@ -329,8 +330,6 @@
                 for part in range(2)
             ]
             pieces.append(jnp.concatenate(both, 0))
-        copies[2 * b].wait()
-        copies[2 * b + 1].wait()
         sums[b] = matmul_terms((high[b], low[b]), split(jnp.concatenate(pieces, 1)))
     copies[2 * RADIX].wait()
     piece = 16
@@ -366,10 +365,10 @@
                         fields_low[b, rows, lanes] = data_low
         return carry
 
-    lax.fori_loop(0, span // piece, multiply, 0)
-    for b in range(RADIX):
-        copies[2 * RADIX + 1 + 2 * b].wait()
-        copies[2 * RADIX + 2 + 2 * b].wait()
+    lax.fori_loop(0, span // piece, multiply, 0, unroll=4)
+    for copy in copies[2 * RADIX + 1 :]:
+        copy.wait()
+    for b in range(RADIX):
         total = matmul_terms((back_high[b], back_low[b]), (fields_high[b], fields_low[b]))
         for unit in range(units):
             for part in range(2):
@@ -401,14 +400,13 @@
         total = matmul(layer[...], jnp.concatenate([data_high, data_low, data_high], 0))
         pieces.append((total[:lines], total[lines:]))
     sorted_columns = []
+    for copy in copies[1:]:
+        copy.wait()
     for b, both in enumerate(turns(pieces, 1)):
-        copies[1 + 2 * b].wait()
-        copies[2 + 2 * b].wait()
         sorted_columns.append(matmul_terms(split(jnp.concatenate(both, 1)), (high[b], low[b])))
     values = jnp.concatenate(sorted_columns, 1) * scale
     data_high, data_mid = split(values)
     data_low = (values - data_high.astype(F32) - data_mid.astype(F32)).astype(BF16)
-    copies[-1].wait()
     total = matmul(jnp.concatenate([data_high, data_mid, data_low], 0), order[...])
     values = total[:lines] + total[lines : 2 * lines] + total[2 * lines :]
     for t in range(groups):
@@ -498,8 +496,7 @@
     )(far(heat), far(kind), far(moment))
 
     def moved(value, step):
-        pairs = [(i, i + step) for i in range(ty) if 0 <= i + step < ty]
-        return lax.ppermute(value, "ty", pairs)
+        return lax.ppermute(value, "ty", [(i, (i + step) % ty) for i in range(ty)])
 
     above = moved(rows[1], 1)
     below = moved(rows[0], -1)

time: 169 us -> 162 us (0.959)
  starting transfers between devices: 4.33 us -> 0.58 us
  Pallas kernels: 28.3 us -> 24.6 us
    ppermute x2, starting transfers between devices: 4.33 us -> 0.58 us  [moved(): return lax.ppermute(value, 'ty', [(i, (i + step) % ty) for i in range(ty)])]
    pallas_call x3, Pallas kernels: 25.5 us -> 21.8 us  [with_tables(): call(kernel, out_shape, [VMEM] * len(operands) + [ANY] * (len(tables) + l...]
  transfers between devices with their start and end apart: 2 -> 2, of which waited for: 1 -> 2; matrix products, arithmetic and copies ran while one was open for 0% -> 0% of each run, Pallas kernels for 0% -> 0%
where the time goes in v4:
time: 162 us; the launch traced here: 160 us
  blocking collectives  131 us (81%)
  Pallas kernels  24.6 us (15%)
  waiting for transfers between devices  2.84 us (2%)
    all_to_all x1, blocking collectives, local(): lax.all_to_all(field, ('tx', 'ty'), split_axis=0, concat_axis=0, tiled=True)  46.5 us
    all_to_all x1, blocking collectives, local(): lax.all_to_all(spectra, ('tx', 'ty'), split_axis=0, concat_axis=0, tiled=...  43.8 us
    all_to_all x2, blocking collectives, local(): block = lax.all_to_all(block, 'tx', split_axis=0, concat_axis=0, tiled=True)  41 us
    pallas_call x3, Pallas kernels, with_tables(): call(kernel, out_shape, [VMEM] * len(operands) + [ANY] * (len(tables) + l...  21.8 us
  transfers between devices with their start and end apart: 2, of which 2 were waited for; matrix products, arithmetic and copies ran while one was open for 0% of the time, Pallas kernels for 0%

profile of v4, /device:TPU:24, one launch (start us, length us, event | category | flops | bytes accessed | tf_op | source)
XLA Modules:
  0.0 160.1 jit_solution(943381825653618166)
XLA Ops:
  0.6 1.2 shard_map.212
  1.8 0.3 collective-permute-start.1
  2.1 0.3 collective-permute-start
  2.4 1.1 collective-permute-done.1.below
  3.5 1.7 %collective-permute-done.above = f32[4,8,128]{2,1,0:T(8,128)S(1)} collective-permute-done((f32[4,8,128]{2,1,0:T(8,128)S(1)}, f32[4,8,128]{2,1,0:T(8,128)S(1)}, u32[]{:S(2)}, u32[]{:S(2)}) %collective-permute-start) | collective-permute-done | bytes 16416 | tf_op jit(solution)/shard_map/ppermute | solution.py:499
  5.2 0.4 shard_map.213
  5.6 24.0 %all_to_all.20.block = f32[8,224,128]{2,1,0:T(8,128)S(1)} all-to-all(f32[8,224,128]{2,1,0:T(8,128)S(1)} %shard_map.213), channel_id=1, replica_groups=mesh['tx'=8,'ty'=16] {'tx'}, dimensions={0} | all-to-all | bytes 1835008 | tf_op jit(solution)/shard_map/all_to_all | solution.py:507
  29.6 6.0 %shard_map.214 = (f32[128,48,128]{2,1,0:T(8,128)S(1)}, f32[8,32,128]{2,1,0:T(8,128)S(1)}) custom-call(f32[8,224,128]{2,1,0:T(8,128)S(1)} %all_to_all.20.block, bf16[1024,1024]{1,0:T(8,128)(2,1)} %constant.24.clone.order_in, bf16[4,256,1024]{2,1,0:T(8,128)(2,1)} %constant.25.clone.high_in, bf16[4,256,1024]{2,1,0:T(8,128)(2,1)} %constant.26.clone.low_in, ...), custom_call_target="tpu_custom_call" | custom-call | tf_op jit(solution)/shard_map/pallas_call | solution.py:460
  35.6 43.8 %all_to_all.21 = f32[128,48,128]{2,1,0:T(8,128)S(1)} all-to-all(f32[128,48,128]{2,1,0:T(8,128)S(1)} %get-tuple-element.14), channel_id=1, replica_groups=mesh['tx'=8,'ty'=16] {'tx','ty'}, dimensions={0} | all-to-all | bytes 6291456 | tf_op jit(solution)/shard_map/all_to_all | solution.py:531
  79.4 10.9 %shard_map.215 = f32[6144,128]{1,0:T(8,128)S(1)} custom-call(f32[6144,128]{1,0:T(8,128)S(1)} %bitcast.11, f32[6,2,1024,128]{3,2,1,0:T(8,128)} %tensor_in.1, bf16[4,512,256]{2,1,0:T(8,128)(2,1)} %constant.28.clone.high_in, bf16[4,512,256]{2,1,0:T(8,128)(2,1)} %constant.29.clone.low_in, bf16[4,256,512]{2,1,0:T(8,128)(2,1)} %constant.30.clone.back_high_in, ...), custom_call_target="tpu_custom_call" | custom-call | tf_op jit(solution)/shard_map/pallas_call | solution.py:460
  90.3 46.5 %all_to_all.22.data = f32[128,48,128]{2,1,0:T(8,128)S(1)} all-to-all(f32[128,48,128]{2,1,0:T(8,128)S(1)} %bitcast.12), channel_id=1, replica_groups=mesh['tx'=8,'ty'=16] {'tx','ty'}, dimensions={0} | all-to-all | bytes 6291456 | tf_op jit(solution)/shard_map/all_to_all | solution.py:548
  136.8 4.9 %shard_map.216 = f32[8,128,128]{2,1,0:T(8,128)S(1)} custom-call(f32[128,48,128]{2,1,0:T(8,128)S(1)} %all_to_all.22.data, f32[8,32,128]{2,1,0:T(8,128)S(1)} %get-tuple-element.15.kept, bf16[192,1152]{1,0:T(8,128)(2,1)} %constant.32.clone.layer_in, bf16[4,1024,256]{2,1,0:T(8,128)(2,1)} %constant.33.clone.high_in, bf16[4,1024,256]{2,1,0:T(8,128)(2,1)} %constant.34.clone.low_in, ...), custom_call_target="tpu_custom_call" | custom-call | tf_op jit(solution)/shard_map/pallas_call | solution.py:460
  141.7 17.1 %all_to_all.23.block = f32[8,128,128]{2,1,0:T(8,128)S(1)} all-to-all(f32[8,128,128]{2,1,0:T(8,128)S(1)} %shard_map.216), channel_id=1, replica_groups=mesh['tx'=8,'ty'=16] {'tx'}, dimensions={0} | all-to-all | bytes 1048576 | tf_op jit(solution)/shard_map/all_to_all | solution.py:557
  158.8 1.3 shard_map.217
  (1 shorter events, 0.0 us)
Async XLA Ops:
  1.8 1.7 %collective-permute-start.1 = (f32[4,8,128]{2,1,0:T(8,128)S(1)}, f32[4,8,128]{2,1,0:T(8,128)S(1)}, u32[]{:S(2)}, u32[]{:S(2)}) collective-permute-start(f32[4,8,128]{2,1,0:T(8,128)S(1)} %get-tuple-element.18), channel_id=1, source_target_pairs={{0,15},{1,0},{2,1},{3,2},{4,3},{5,4},{6,5},{7,6},{8,7},{9,8},{10,9... | collective-permute-start | bytes 49160 | tf_op jit(solution)/shard_map/ppermute | solution.py:499
  2.1 3.2 %collective-permute-start = (f32[4,8,128]{2,1,0:T(8,128)S(1)}, f32[4,8,128]{2,1,0:T(8,128)S(1)}, u32[]{:S(2)}, u32[]{:S(2)}) collective-permute-start(f32[4,8,128]{2,1,0:T(8,128)S(1)} %get-tuple-element.19), channel_id=1, source_target_pairs={{0,1},{1,2},{2,3},{3,4},{4,5},{5,6},{6,7},{7,8},{8,9},{9,10},{10,1... | collective-permute-start | bytes 49160 | tf_op jit(solution)/shard_map/ppermute | solution.py:499

commit v5 on v4

--- a/solution.py
+++ b/solution.py
@@ -49,44 +49,20 @@
     return lax.dot_general(left, right, (((1,), (0,)), ((), ())), preferred_element_type=F32)
 
 
-def layer_tables(layers, strips, comps, order):
-    count = 2 * layers
-    owners = count // 2
-    rows_in = comps * strips * layers
-    if order == "whole":
-        shape = (owners, 2, comps, 2, strips)
-    else:
-        shape = (2, owners, comps, 2, strips)
-    index = np.indices(shape).reshape(5, -1)
-    if order == "whole":
-        owner, member, comp, part, strip = index
-    else:
-        member, owner, comp, part, strip = index
-    freq = 2 * owner + member
-    comp_in, strip_in, layer_in = np.indices((comps, strips, layers)).reshape(3, -1)
-    same = (comp[:, None] == comp_in[None]) & (strip[:, None] == strip_in[None])
-    cosine, sine = waves(freq[:, None] * layer_in[None], count)
-    zero = part[:, None] == 0
-    from_real = np.where(zero, cosine, -sine) * same
-    from_imag = np.where(zero, sine, cosine) * same
-    forward = np.concatenate([from_real, from_imag], 1)
-    return forward, forward.T
-
-
-def along_tables(points, devices):
+def along_tables(points):
     length = 2 * points
     span = length // RADIX
-    sub = points // RADIX
-    a = np.arange(sub)
+    a = np.arange(points // RADIX)
+    b = np.arange(RADIX)
     v = np.arange(span)
-    forward = np.zeros((RADIX, sub, 2 * span))
-    for b in range(RADIX):
-        cosine, sine = waves(v[None, :] * (RADIX * a + b)[:, None], length)
-        forward[b] = np.concatenate([cosine, -sine], 1)
-    order = np.zeros((points, points), np.float32)
-    for b in range(RADIX):
-        order[RADIX * a + b, b * sub + a] = 1.0
-    return forward, forward.transpose(0, 2, 1), order.astype(ml_dtypes.bfloat16)
+    cosine, sine = waves(v[None, :] * (RADIX * a)[:, None], length)
+    forward = np.concatenate([cosine, -sine], 1)
+    turn = np.stack(waves(v[None, :] * b[:, None], length), 1).reshape(2 * RADIX, span)
+    half = points // 2
+    order = np.zeros((half, half), np.float32)
+    x = np.arange(half)
+    order[x, x % RADIX * (half // RADIX) + x // RADIX] = 1.0
+    return forward, turn.astype(np.float32), order.astype(ml_dtypes.bfloat16)
 
 
 def across_tables(points, groups, blocks, strips):
@@ -101,7 +77,7 @@
         zero = part[None, :] == 0
         forward[b, :span] = np.where(zero, cosine, sine)
         forward[b, span:] = np.where(zero, -sine, cosine)
-    return forward, forward.transpose(0, 2, 1)
+    return forward[:, :span], forward.transpose(0, 2, 1)[:, : part.size // 2]
 
 
 def fetch(pairs, sems):
@@ -254,52 +230,125 @@
     )
 
 
+def eight(x, sign):
+    even, odd = turns(x[0::2], sign), turns(x[1::2], sign)
+    root = math.sqrt(0.5)
+    first, second = [], []
+    for k in range(4):
+        (er, ei), (ar, ai) = even[k], odd[k]
+        if k == 1:
+            ar, ai = (ar - sign * ai) * root, (ai + sign * ar) * root
+        elif k == 2:
+            ar, ai = -sign * ai, sign * ar
+        elif k == 3:
+            ar, ai = (-ar - sign * ai) * root, (-ai + sign * ar) * root
+        first.append((er + ar, ei + ai))
+        second.append((er - ar, ei - ai))
+    return first + second
+
+
+def layer_turn(value, layer, layers, high_half, sign):
+    if layer == 0:
+        return value
+    real, imag = value
+    angle = math.pi * layer / layers
+    cosine = jnp.where(high_half, math.cos(angle), 1.0)
+    sine = jnp.where(high_half, sign * math.sin(angle), 0.0)
+    return real * cosine - imag * sine, imag * cosine + real * sine
+
+
+def halves(values):
+    middle = values.shape[1] // 2
+    return values[:, :middle], values[:, middle:]
+
+
 def rows_kernel(
-    block, order_in, high_in, low_in, layer_in, nodes_in, factor_in, threshold_in, spot_row_in, spot_col_in,
-    out, warmed, order, high, low, layer, nodes, factor, threshold, spot_row, spot_col, sems, *, total_rows
+    block, order_in, high_in, low_in, turn_in, nodes_in, factor_in, threshold_in, spot_row_in, spot_col_in,
+    out, warmed, order, high, low, turn, nodes, factor, threshold, spot_row, spot_col, scaled, sems, *, total_rows
 ):
     copies = fetch(
         [
             (nodes_in, nodes), (factor_in, factor), (threshold_in, threshold),
-            (spot_row_in, spot_row), (spot_col_in, spot_col), (order_in, order),
-        ]
-        + [pair for b in range(RADIX) for pair in ((high_in.at[b], high.at[b]), (low_in.at[b], low.at[b]))]
-        + [(layer_in, layer)],
+            (spot_row_in, spot_row), (spot_col_in, spot_col),
+            (order_in, order), (high_in, high), (low_in, low), (turn_in, turn),
+        ],
         sems,
     )
     for copy in copies[:5]:
         copy.wait()
-    copies = copies[5:]
     groups, _, width = block.shape
-    points = groups * width
-    sub = points // RADIX
-    span = high.shape[2] // 2
+    span = high.shape[1] // 2
     kept, values = heat_rows(block, nodes, factor, threshold, spot_row, spot_col, total_rows)
+    layers = 8
     lines = values.shape[0]
+    strips = len(kept)
+    columns = []
+    for t in range(groups):
+        scaled[t] = values[:, t * width : (t + 1) * width]
+        rows = [
+            scaled[t, pl.ds(comp * strips * layers + layer, strips, stride=layers), :]
+            for comp in range(3)
+            for layer in range(layers)
+        ]
+        columns.append(jnp.concatenate(rows, 0))
+    values = jnp.concatenate(columns, 1)
     for strip, value in enumerate(kept):
         for t in range(groups):
             warmed[t, strip * 8 : strip * 8 + 8, :] = value[:, t * width : (t + 1) * width]
+    for copy in copies[5:]:
+        copy.wait()
     both = jnp.concatenate(split(values), 0)
-    copies[0].wait()
-    both = matmul(both, order[...]).astype(BF16)
+    both = [matmul(half, order[...]).astype(BF16) for half in halves(both)]
+    piece = both[0].shape[1] // RADIX
+    sorted_rows = [
+        jnp.concatenate(
+            [
+                jnp.concatenate([half[term, b * piece : (b + 1) * piece] for half in both], 1)
+                for b in range(RADIX)
+            ],
+            0,
+        )
+        for term in (slice(0, lines), slice(lines, 2 * lines))
+    ]
+    total = matmul_terms(sorted_rows, (high[...], low[...]))
     parts = []
-    for copy in copies[1:]:
-        copy.wait()
     for b in range(RADIX):
-        data = both[:, b * sub : (b + 1) * sub]
-        total = matmul_terms((data[:lines], data[lines:]), (high[b], low[b]))
-        parts.append((total[:, :span], total[:, span:]))
+        real, imag = halves(total[b * lines : (b + 1) * lines])
+        if b:
+            cosine, sine = turn[2 * b : 2 * b + 1, :], turn[2 * b + 1 : 2 * b + 2, :]
+            real, imag = real * cosine + imag * sine, imag * cosine - real * sine
+        parts.append((real, imag))
     slabs = span // width
     blocks = RADIX * slabs
-    for u, (real, imag) in enumerate(turns(parts, -1)):
-        data_high, data_low = split(jnp.concatenate([real, imag], 0))
-        total = matmul(layer[...], jnp.concatenate([data_high, data_low, data_high], 0))
-        rows = total.shape[0] // groups
-        for t in range(groups):
-            for slab in range(slabs):
-                out[t * blocks + u * slabs + slab] = total[
-                    t * rows : (t + 1) * rows, slab * width : (slab + 1) * width
+    wide = slabs * width
+    high_half = lax.broadcasted_iota(jnp.int32, (2 * strips, wide), 0) >= strips
+    for u, spectra in enumerate(turns(parts, -1)):
+        for comp in range(3):
+            layered = []
+            for layer in range(layers):
+                at = (comp * layers + layer // 2 * 2) * strips
+                tiles = [value[at : at + 2 * strips] for value in spectra]
+                moved = [pltpu.roll(tile, strips, 0) for tile in tiles]
+                if layer % 2:
+                    tiles, moved = moved, tiles
+                both = [
+                    jnp.where(high_half, other, tile)
+                    for tile, other in zip(tiles, moved, strict=True)
                 ]
+                layered.append(layer_turn(both, layer, layers, high_half, -1))
+            for t, value in enumerate(eight(layered, -1)):
+                for part in range(2):
+                    at = (comp * 2 + part) * 2 * strips
+                    for slab in range(slabs):
+                        out[t * blocks + u * slabs + slab, at : at + 2 * strips, :] = value[part][
+                            :, slab * width : (slab + 1) * width
+                        ]
+
+
+def complex_table(half):
+    split_at = half.shape[1] // 2
+    turned = jnp.concatenate([-half[:, split_at:], half[:, :split_at]], 1)
+    return jnp.concatenate([half, turned], 0)
 
 
 def spectrum_kernel(
@@ -312,26 +361,36 @@
     lines = data.shape[0] // senders
     units = lines // 8
     members = units // comps
-    span = high.shape[1] // 2
-    pairs = []
+    span = high.shape[1]
+
+    def row_of(unit, part, b):
+        member, comp = divmod(unit, comps)
+        return ((comp * 2 + part) * members + member) * RADIX + b
+
+    copies = fetch(
+        [
+            (high_in, high), (low_in, low), (tensor_in, tensor),
+            (back_high_in, back_high), (back_low_in, back_low),
+        ],
+        sems,
+    )
     for b in range(RADIX):
-        pairs += [(high_in.at[b], high.at[b]), (low_in.at[b], low.at[b])]
-    pairs += [(tensor_in, tensor)]
-    for b in range(RADIX):
-        pairs += [(back_high_in.at[b], back_high.at[b]), (back_low_in.at[b], back_low.at[b])]
-    copies = fetch(pairs, sems)
-    for copy in copies[: 2 * RADIX]:
-        copy.wait()
-    for b in range(RADIX):
-        pieces = []
         for unit in range(units):
             both = [
-                data[pl.ds(unit * 8 + part * RADIX + b, senders, stride=lines), :]
-                for part in range(2)
+                data[pl.ds(row_of(unit, part, b), senders, stride=lines), :] for part in range(2)
             ]
-            pieces.append(jnp.concatenate(both, 0))
-        sums[b] = matmul_terms((high[b], low[b]), split(jnp.concatenate(pieces, 1)))
-    copies[2 * RADIX].wait()
+            data_high, data_low = split(jnp.concatenate(both, 0))
+            lanes = slice(unit * width, (unit + 1) * width)
+            fields_high[b, : 2 * senders, lanes] = data_high
+            fields_low[b, : 2 * senders, lanes] = data_low
+    copies[0].wait()
+    copies[1].wait()
+    for b in range(RADIX):
+        sums[b] = matmul_terms(
+            (complex_table(high[b]), complex_table(low[b])),
+            (fields_high[b, : 2 * senders], fields_low[b, : 2 * senders]),
+        )
+    copies[2].wait()
     piece = 16
 
     def multiply(step, carry):
@@ -366,49 +425,83 @@
         return carry
 
     lax.fori_loop(0, span // piece, multiply, 0, unroll=4)
-    for copy in copies[2 * RADIX + 1 :]:
-        copy.wait()
+    copies[3].wait()
+    copies[4].wait()
     for b in range(RADIX):
-        total = matmul_terms((back_high[b], back_low[b]), (fields_high[b], fields_low[b]))
+        total = matmul_terms(
+            (complex_table(back_high[b]), complex_table(back_low[b])),
+            (fields_high[b], fields_low[b]),
+        )
         for unit in range(units):
             for part in range(2):
-                out[pl.ds(unit * 8 + part * RADIX + b, senders, stride=lines), :] = total[
+                out[pl.ds(row_of(unit, part, b), senders, stride=lines), :] = total[
                     part * senders : (part + 1) * senders, unit * width : (unit + 1) * width
                 ]
 
 
-def cells_kernel(data, kept, layer_in, high_in, low_in, order_in, out, layer, high, low, order, sems, *, scale):
+def cells_kernel(
+    data, kept, high_in, low_in, turn_in, order_in, out, high, low, turn, order, sems, *, scale
+):
     copies = fetch(
-        [(layer_in, layer)]
-        + [pair for b in range(RADIX) for pair in ((high_in.at[b], high.at[b]), (low_in.at[b], low.at[b]))]
-        + [(order_in, order)],
+        [(high_in, high), (low_in, low), (turn_in, turn), (order_in, order)],
         sems,
     )
     groups, _, width = out.shape
-    lines = layer.shape[0] // 2
-    span = high.shape[1] // 2
+    layers = 8
+    strips = kept.shape[1] // layers
+    lines = 3 * layers * strips
+    span = high.shape[0] // 2
     slabs = span // width
     blocks = RADIX * slabs
     pieces = []
-    copies[0].wait()
+    high_half = lax.broadcasted_iota(jnp.int32, (2 * strips, slabs * width), 0) >= strips
     for u in range(RADIX):
         columns = []
-        for slab in range(slabs):
-            at = u * slabs + slab
-            columns.append(jnp.concatenate([data[t * blocks + at] for t in range(groups)], 0))
-        data_high, data_low = split(jnp.concatenate(columns, 1))
-        total = matmul(layer[...], jnp.concatenate([data_high, data_low, data_high], 0))
-        pieces.append((total[:lines], total[lines:]))
-    sorted_columns = []
-    for copy in copies[1:]:
+        for comp in range(3):
+            spectra = []
+            for t in range(groups):
+                both = []
+                for part in range(2):
+                    at = (comp * 2 + part) * 2 * strips
+                    both.append(
+                        jnp.concatenate(
+                            [
+                                data[t * blocks + u * slabs + slab, at : at + 2 * strips, :]
+                                for slab in range(slabs)
+                            ],
+                            1,
+                        )
+                    )
+                spectra.append(both)
+            layered = []
+            for layer, value in enumerate(eight(spectra, 1)):
+                value = layer_turn(value, layer, layers, high_half, 1)
+                layered.append([part + pltpu.roll(part, strips, 0) for part in value])
+            for layer in range(0, layers, 2):
+                columns.append(
+                    [
+                        jnp.where(high_half, other, own)
+                        for own, other in zip(layered[layer], layered[layer + 1], strict=True)
+                    ]
+                )
+        pieces.append(tuple(jnp.concatenate([c[part] for c in columns], 0) for part in range(2)))
+    for copy in copies:
         copy.wait()
-    for b, both in enumerate(turns(pieces, 1)):
-        sorted_columns.append(matmul_terms(split(jnp.concatenate(both, 1)), (high[b], low[b])))
-    values = jnp.concatenate(sorted_columns, 1) * scale
-    data_high, data_mid = split(values)
-    data_low = (values - data_high.astype(F32) - data_mid.astype(F32)).astype(BF16)
-    total = matmul(jnp.concatenate([data_high, data_mid, data_low], 0), order[...])
-    values = total[:lines] + total[lines : 2 * lines] + total[2 * lines :]
+    rows = []
+    for b, (real, imag) in enumerate(turns(pieces, 1)):
+        if b:
+            cosine, sine = turn[2 * b : 2 * b + 1, :], turn[2 * b + 1 : 2 * b + 2, :]
+            real, imag = real * cosine - imag * sine, imag * cosine + real * sine
+        rows.append(jnp.concatenate([real, imag], 1))
+    total = matmul_terms(split(jnp.concatenate(rows, 0)), (high[...], low[...])) * scale
+    sorted_halves = []
+    for half in halves(total):
+        values = jnp.concatenate([half[b * lines : (b + 1) * lines] for b in range(RADIX)], 1)
+        data_high, data_mid = split(values)
+        data_low = (values - data_high.astype(F32) - data_mid.astype(F32)).astype(BF16)
+        values = matmul(jnp.concatenate([data_high, data_mid, data_low], 0), order[...])
+        sorted_halves.append(values[:lines] + values[lines : 2 * lines] + values[2 * lines :])
+    values = jnp.concatenate(sorted_halves, 1)
     for t in range(groups):
         out[t, :lines] = values[:, t * width : (t + 1) * width]
         out[t, lines:] = kept[t]
@@ -422,12 +515,12 @@
     for y in range(count):
         group, strip = divmod(y, strips)
         for comp in range(4):
-            at = (comp * strips + strip) * layers
-            value = block[group, at : at + layers, :]
             if comp < 3:
-                field[pl.ds(comp * layers * count + y, layers, stride=count), :] = value
+                at = pl.ds(comp * strips * layers + strip, layers, stride=strips)
+                field[pl.ds(comp * layers * count + y, layers, stride=count), :] = block[group, at, :]
             else:
-                warmed[pl.ds(y, layers, stride=count), :] = value
+                at = (comp * strips + strip) * layers
+                warmed[pl.ds(y, layers, stride=count), :] = block[group, at : at + layers, :]
 
 
 def near(shape, dtype):
@@ -470,7 +563,7 @@
 
 
 def local(
-    tx, ty, order, heat, kind, moment, tensor, nodes, factor, threshold, spot_row, spot_col
+    tx, ty, heat, kind, moment, tensor, nodes, factor, threshold, spot_row, spot_col
 ):
     layers, count, width = heat.shape
     strips = count // tx
@@ -506,16 +599,11 @@
     )
     block = lax.all_to_all(block, "tx", split_axis=0, concat_axis=0, tiled=True)
 
-    layer, layer_back = layer_tables(layers, strips, comps, order)
-    along, along_back, sort = along_tables(points_x, tx)
+    along, turn, sort = along_tables(points_x)
     across, across_back = across_tables(points_y, tx, ty, strips)
     senders = tx * ty
     message = members * comps * 2 * strips
     span = 2 * points_y // RADIX
-
-    def tripled(table):
-        high, low = two_terms(table)
-        return np.concatenate([high, high, low], 1)
 
     spectra, warmed = with_tables(
         functools.partial(rows_kernel, total_rows=points_y),
@@ -524,9 +612,10 @@
             near((tx, strips * layers, width), F32),
         ],
         [block],
-        [sort, *two_terms(along), tripled(layer)],
+        [sort, *two_terms(along), turn],
         [nodes, factor, threshold, spot_row, spot_col],
-        copies=7 + 2 * RADIX,
+        [pltpu.VMEM((tx, lines, width), F32)],
+        copies=9,
     )
     data = lax.all_to_all(spectra, ("tx", "ty"), split_axis=0, concat_axis=0, tiled=True)
     columns = members * comps * width
@@ -541,7 +630,7 @@
             pltpu.VMEM((RADIX, 2 * span, columns), BF16),
             pltpu.VMEM((RADIX, 2 * span, columns), BF16),
         ],
-        copies=1 + 4 * RADIX,
+        copies=5,
         megabytes=44,
     )
     field = field.reshape(senders, message, width)
@@ -551,8 +640,8 @@
         functools.partial(cells_kernel, scale=scale),
         near((tx, lines + strips * layers, width), F32),
         [data, warmed],
-        [tripled(layer_back), *two_terms(along_back), np.ascontiguousarray(sort.T)],
-        copies=2 + 2 * RADIX,
+        [*two_terms(along.T), turn, np.ascontiguousarray(sort.T)],
+        copies=4,
     )
     block = lax.all_to_all(block, "tx", split_axis=0, concat_axis=0, tiled=True)
     demag, warmed = call(
@@ -579,5 +668,5 @@
         P(),
     )
     out_specs = (P(None, "ty", "tx"), P(None, None, "ty", "tx"))
-    body = functools.partial(local, mesh.shape["tx"], mesh.shape["ty"], "whole")
+    body = functools.partial(local, mesh.shape["tx"], mesh.shape["ty"])
     return jax.shard_map(body, mesh=mesh, in_specs=in_specs, out_specs=out_specs, check_vma=False)

time: 162 us -> 158 us (0.975)
  Pallas kernels: 24.6 us -> 21.4 us
    pallas_call x3, Pallas kernels: 21.8 us -> 18.6 us  [with_tables(): call(kernel, out_shape, [VMEM] * len(operands) + [ANY] * (len(tables) + l...]
where the time goes in v5:
time: 158 us; the launch traced here: 157 us
  blocking collectives  131 us (83%)
  Pallas kernels  21.4 us (14%)
  waiting for transfers between devices  2.84 us (2%)
    all_to_all x1, blocking collectives, local(): lax.all_to_all(field, ('tx', 'ty'), split_axis=0, concat_axis=0, tiled=True)  46.5 us
    all_to_all x1, blocking collectives, local(): lax.all_to_all(spectra, ('tx', 'ty'), split_axis=0, concat_axis=0, tiled=...  43.8 us
    all_to_all x2, blocking collectives, local(): block = lax.all_to_all(block, 'tx', split_axis=0, concat_axis=0, tiled=True)  41 us
    pallas_call x3, Pallas kernels, with_tables(): call(kernel, out_shape, [VMEM] * len(operands) + [ANY] * (len(tables) + l...  18.6 us
  transfers between devices with their start and end apart: 2, of which 2 were waited for; matrix products, arithmetic and copies ran while one was open for 0% of the time, Pallas kernels for 0%

profile of v5, /device:TPU:24, one launch (start us, length us, event | category | flops | bytes accessed | tf_op | source)
XLA Modules:
  0.0 156.9 jit_solution(4668357253426375490)
XLA Ops:
  0.6 1.2 shard_map.203
  1.8 0.3 collective-permute-start.1
  2.1 0.3 collective-permute-start
  2.4 1.1 collective-permute-done.1.below
  3.5 1.7 %collective-permute-done.above = f32[4,8,128]{2,1,0:T(8,128)S(1)} collective-permute-done((f32[4,8,128]{2,1,0:T(8,128)S(1)}, f32[4,8,128]{2,1,0:T(8,128)S(1)}, u32[]{:S(2)}, u32[]{:S(2)}) %collective-permute-start) | collective-permute-done | bytes 16416 | tf_op jit(solution)/shard_map/ppermute | solution.py:592
  5.2 0.4 shard_map.204
  5.6 24.0 %all_to_all.20.block = f32[8,224,128]{2,1,0:T(8,128)S(1)} all-to-all(f32[8,224,128]{2,1,0:T(8,128)S(1)} %shard_map.204), channel_id=1, replica_groups=mesh['tx'=8,'ty'=16] {'tx'}, dimensions={0} | all-to-all | bytes 1835008 | tf_op jit(solution)/shard_map/all_to_all | solution.py:600
  29.6 4.9 %shard_map.205 = (f32[128,48,128]{2,1,0:T(8,128)S(1)}, f32[8,32,128]{2,1,0:T(8,128)S(1)}) custom-call(f32[8,224,128]{2,1,0:T(8,128)S(1)} %all_to_all.20.block, bf16[512,512]{1,0:T(8,128)(2,1)} %constant.22.clone.order_in, bf16[256,1024]{1,0:T(8,128)(2,1)} %constant.23.clone.high_in, bf16[256,1024]{1,0:T(8,128)(2,1)} %constant.24.clone.low_in, ...), custom_call_target="tpu_custom_call" | custom-call | tf_op jit(solution)/shard_map/pallas_call | solution.py:553
  34.6 43.8 %all_to_all.21 = f32[128,48,128]{2,1,0:T(8,128)S(1)} all-to-all(f32[128,48,128]{2,1,0:T(8,128)S(1)} %get-tuple-element.14), channel_id=1, replica_groups=mesh['tx'=8,'ty'=16] {'tx','ty'}, dimensions={0} | all-to-all | bytes 6291456 | tf_op jit(solution)/shard_map/all_to_all | solution.py:620
  78.3 10.4 %shard_map.206 = f32[6144,128]{1,0:T(8,128)S(1)} custom-call(f32[6144,128]{1,0:T(8,128)S(1)} %bitcast.11, f32[6,2,1024,128]{3,2,1,0:T(8,128)} %tensor_in.1, bf16[4,256,256]{2,1,0:T(8,128)(2,1)} %constant.26.clone.high_in, bf16[4,256,256]{2,1,0:T(8,128)(2,1)} %constant.27.clone.low_in, bf16[4,128,512]{2,1,0:T(8,128)(2,1)} %constant.28.clone.back_high_in, ...), custom_call_target="tpu_custom_call" | custom-call | tf_op jit(solution)/shard_map/pallas_call | solution.py:553
  88.8 46.5 %all_to_all.22.data = f32[128,48,128]{2,1,0:T(8,128)S(1)} all-to-all(f32[128,48,128]{2,1,0:T(8,128)S(1)} %bitcast.12), channel_id=1, replica_groups=mesh['tx'=8,'ty'=16] {'tx','ty'}, dimensions={0} | all-to-all | bytes 6291456 | tf_op jit(solution)/shard_map/all_to_all | solution.py:637
  135.3 3.2 %shard_map.207 = f32[8,128,128]{2,1,0:T(8,128)S(1)} custom-call(f32[128,48,128]{2,1,0:T(8,128)S(1)} %all_to_all.22.data, f32[8,32,128]{2,1,0:T(8,128)S(1)} %get-tuple-element.15.kept, bf16[1024,256]{1,0:T(8,128)(2,1)} %constant.30.clone.high_in, bf16[1024,256]{1,0:T(8,128)(2,1)} %constant.31.clone.low_in, f32[8,512]{1,0:T(8,128)} %constant.25.clone.turn_in, ...), custom_call_target="tpu_custom_call" | custom-call | tf_op jit(solution)/shard_map/pallas_call | solution.py:553
  138.5 17.1 %all_to_all.23.block = f32[8,128,128]{2,1,0:T(8,128)S(1)} all-to-all(f32[8,128,128]{2,1,0:T(8,128)S(1)} %shard_map.207), channel_id=1, replica_groups=mesh['tx'=8,'ty'=16] {'tx'}, dimensions={0} | all-to-all | bytes 1048576 | tf_op jit(solution)/shard_map/all_to_all | solution.py:646
  155.6 1.3 shard_map.208
  (1 shorter events, 0.0 us)
Async XLA Ops:
  1.8 1.7 %collective-permute-start.1 = (f32[4,8,128]{2,1,0:T(8,128)S(1)}, f32[4,8,128]{2,1,0:T(8,128)S(1)}, u32[]{:S(2)}, u32[]{:S(2)}) collective-permute-start(f32[4,8,128]{2,1,0:T(8,128)S(1)} %get-tuple-element.18), channel_id=1, source_target_pairs={{0,15},{1,0},{2,1},{3,2},{4,3},{5,4},{6,5},{7,6},{8,7},{9,8},{10,9... | collective-permute-start | bytes 49160 | tf_op jit(solution)/shard_map/ppermute | solution.py:592
  2.1 3.2 %collective-permute-start = (f32[4,8,128]{2,1,0:T(8,128)S(1)}, f32[4,8,128]{2,1,0:T(8,128)S(1)}, u32[]{:S(2)}, u32[]{:S(2)}) collective-permute-start(f32[4,8,128]{2,1,0:T(8,128)S(1)} %get-tuple-element.19), channel_id=1, source_target_pairs={{0,1},{1,2},{2,3},{3,4},{4,5},{5,6},{6,7},{7,8},{8,9},{9,10},{10,1... | collective-permute-start | bytes 49160 | tf_op jit(solution)/shard_map/ppermute | solution.py:592

commit v6 on v5

--- a/solution.py
+++ b/solution.py
@@ -20,6 +20,8 @@
 TABLE_SPAN = 1.6
 RADIX = 4
 REACH = SWEEPS
+OUTER, INNER = 2, 4
+TX = ("tx_outer", "tx_inner")
 PAIRS = ((0, 3, 4), (3, 1, 5), (4, 5, 2))
 VMEM = pl.BlockSpec(memory_space=pltpu.VMEM)
 ANY = pl.BlockSpec(memory_space=pl.ANY)
@@ -68,7 +70,7 @@
 def across_tables(points, groups, blocks, strips):
     length = 2 * points
     span = length // RADIX
-    part, group, block = np.indices((2, groups, blocks)).reshape(3, -1)
+    part, block, group = np.indices((2, blocks, groups)).reshape(3, -1)
     v = np.arange(span)
     forward = np.zeros((RADIX, 2 * span, part.size))
     for b in range(RADIX):
@@ -95,6 +97,11 @@
     for grain in range(values.shape[0]):
         total = total + jnp.where(which == grain, values[grain], 0.0)
     return total
+
+
+def rank(t):
+    outer, inner = divmod(t, INNER)
+    return inner * OUTER + outer
 
 
 def edges_kernel(heat_in, kind_in, moment_in, heat, kind, moment, rows, sems):
@@ -126,12 +133,13 @@
                 at = pl.ds(y, layers, stride=count)
                 pair = (heat[at, :], kind[at, :].astype(F32))
             for which, value in enumerate(pair):
-                out[group, (which * tall + i) * layers : (which * tall + i + 1) * layers, :] = value
+                at = (which * tall + i) * layers
+                out[rank(group), at : at + layers, :] = value
         for comp in range(3):
             for strip in range(strips):
                 at = pl.ds(comp * layers * count + group * strips + strip, layers, stride=count)
                 to = (2 * tall + comp * strips + strip) * layers
-                out[group, to : to + layers, :] = moment[at, :]
+                out[rank(group), to : to + layers, :] = moment[at, :]
 
 
 def heat_rows(block, nodes, factor, threshold, spot_row, spot_col, total_rows):
@@ -140,7 +148,8 @@
     total_cols = groups * width
     strips = (lines // layers - 4 * REACH) // 5
     tall = strips + 2 * REACH
-    row_base = (lax.axis_index("ty") * groups + lax.axis_index("tx")) * strips - REACH
+    place = lax.axis_index("ty") * groups + lax.axis_index(TX[0]) * INNER + lax.axis_index(TX[1])
+    row_base = place * strips - REACH
     shape = (layers, total_cols)
     column = lax.broadcasted_iota(jnp.int32, shape, 1)
     depth = lax.broadcasted_iota(jnp.int32, shape, 0)
@@ -149,7 +158,9 @@
 
     def whole(index):
         at = index * layers
-        return jnp.concatenate([block[t, at : at + layers, :] for t in range(groups)], 1)
+        return jnp.concatenate(
+            [block[rank(t), at : at + layers, :] for t in range(groups)], 1
+        )
 
     def chosen(which, values):
         total = jnp.zeros(which.shape, F32)
@@ -319,7 +330,6 @@
             real, imag = real * cosine + imag * sine, imag * cosine - real * sine
         parts.append((real, imag))
     slabs = span // width
-    blocks = RADIX * slabs
     wide = slabs * width
     high_half = lax.broadcasted_iota(jnp.int32, (2 * strips, wide), 0) >= strips
     for u, spectra in enumerate(turns(parts, -1)):
@@ -340,7 +350,7 @@
                 for part in range(2):
                     at = (comp * 2 + part) * 2 * strips
                     for slab in range(slabs):
-                        out[t * blocks + u * slabs + slab, at : at + 2 * strips, :] = value[part][
+                        out[(u * slabs + slab) * groups + t, at : at + 2 * strips, :] = value[part][
                             :, slab * width : (slab + 1) * width
                         ]
 
@@ -452,7 +462,6 @@
     lines = 3 * layers * strips
     span = high.shape[0] // 2
     slabs = span // width
-    blocks = RADIX * slabs
     pieces = []
     high_half = lax.broadcasted_iota(jnp.int32, (2 * strips, slabs * width), 0) >= strips
     for u in range(RADIX):
@@ -466,7 +475,7 @@
                     both.append(
                         jnp.concatenate(
                             [
-                                data[t * blocks + u * slabs + slab, at : at + 2 * strips, :]
+                                data[(u * slabs + slab) * groups + t, at : at + 2 * strips, :]
                                 for slab in range(slabs)
                             ],
                             1,
@@ -597,7 +606,7 @@
     block = call(send_kernel, near((tx, tall * layers, width), F32), [VMEM] * 5)(
         heat, kind, moment, above, below
     )
-    block = lax.all_to_all(block, "tx", split_axis=0, concat_axis=0, tiled=True)
+    block = lax.all_to_all(block, TX[::-1], split_axis=0, concat_axis=0, tiled=True)
 
     along, turn, sort = along_tables(points_x)
     across, across_back = across_tables(points_y, tx, ty, strips)
@@ -617,7 +626,7 @@
         [pltpu.VMEM((tx, lines, width), F32)],
         copies=9,
     )
-    data = lax.all_to_all(spectra, ("tx", "ty"), split_axis=0, concat_axis=0, tiled=True)
+    data = lax.all_to_all(spectra, ("ty", *TX), split_axis=0, concat_axis=0, tiled=True)
     columns = members * comps * width
     field = with_tables(
         spectrum_kernel,
@@ -634,7 +643,7 @@
         megabytes=44,
     )
     field = field.reshape(senders, message, width)
-    data = lax.all_to_all(field, ("tx", "ty"), split_axis=0, concat_axis=0, tiled=True)
+    data = lax.all_to_all(field, ("ty", *TX), split_axis=0, concat_axis=0, tiled=True)
     scale = -1.0 / (2 * layers * 2 * points_y * 2 * points_x)
     block = with_tables(
         functools.partial(cells_kernel, scale=scale),
@@ -643,7 +652,7 @@
         [*two_terms(along.T), turn, np.ascontiguousarray(sort.T)],
         copies=4,
     )
-    block = lax.all_to_all(block, "tx", split_axis=0, concat_axis=0, tiled=True)
+    block = lax.all_to_all(block, TX, split_axis=0, concat_axis=0, tiled=True)
     demag, warmed = call(
         place_kernel,
         [jax.ShapeDtypeStruct((comps * cells, width), F32), jax.ShapeDtypeStruct((cells, width), F32)],
@@ -656,17 +665,19 @@
 
 
 def solution(mesh):
+    tx, ty = mesh.shape["tx"], mesh.shape["ty"]
+    parts = jax.sharding.Mesh(mesh.devices.reshape(OUTER, tx // OUTER, ty), (*TX, "ty"))
     in_specs = (
-        P(None, "ty", "tx"),
-        P(None, "ty", "tx"),
-        P(None, None, "ty", "tx"),
-        P(None, "tx", None, "ty"),
+        P(None, "ty", TX),
+        P(None, "ty", TX),
+        P(None, None, "ty", TX),
+        P(None, TX, None, "ty"),
         P(),
         P(),
         P(),
         P(),
         P(),
     )
-    out_specs = (P(None, "ty", "tx"), P(None, None, "ty", "tx"))
-    body = functools.partial(local, mesh.shape["tx"], mesh.shape["ty"])
-    return jax.shard_map(body, mesh=mesh, in_specs=in_specs, out_specs=out_specs, check_vma=False)
+    out_specs = (P(None, "ty", TX), P(None, None, "ty", TX))
+    body = functools.partial(local, tx, ty)
+    return jax.shard_map(body, mesh=parts, in_specs=in_specs, out_specs=out_specs, check_vma=False)

time: 158 us -> 157 us (level)
  blocking collectives: 131 us -> 129 us
    all_to_all x4, blocking collectives: 131 us -> 129 us  [the longest x1 45.3 us: local(): lax.all_to_all(field, ('ty', *TX), split_axis=0, concat_axis=0, tiled=True)]
where the time goes in v6:
time: 157 us; the launch traced here: 155 us
  blocking collectives  129 us (82%)
  Pallas kernels  21.4 us (14%)
  waiting for transfers between devices  2.84 us (2%)
    all_to_all x1, blocking collectives, local(): lax.all_to_all(field, ('ty', *TX), split_axis=0, concat_axis=0, tiled=True)  45.3 us
    all_to_all x1, blocking collectives, local(): lax.all_to_all(spectra, ('ty', *TX), split_axis=0, concat_axis=0, tiled=T...  44.7 us
    all_to_all x1, blocking collectives, local(): lax.all_to_all(block, TX[::-1], split_axis=0, concat_axis=0, tiled=True)  24.3 us
    pallas_call x3, Pallas kernels, with_tables(): call(kernel, out_shape, [VMEM] * len(operands) + [ANY] * (len(tables) + l...  18.6 us
    all_to_all x1, blocking collectives, local(): block = lax.all_to_all(block, TX, split_axis=0, concat_axis=0, tiled=True)  14.7 us
  transfers between devices with their start and end apart: 2, of which 2 were waited for; matrix products, arithmetic and copies ran while one was open for 0% of the time, Pallas kernels for 0%

profile of v6, /device:TPU:24, one launch (start us, length us, event | category | flops | bytes accessed | tf_op | source)
XLA Modules:
  0.0 154.6 jit_solution(10080367987445758455)
XLA Ops:
  0.6 1.2 shard_map.203
  1.8 0.3 collective-permute-start.1
  2.1 0.3 collective-permute-start
  2.4 1.1 collective-permute-done.1.below
  3.5 1.7 %collective-permute-done.above = f32[4,8,128]{2,1,0:T(8,128)S(1)} collective-permute-done((f32[4,8,128]{2,1,0:T(8,128)S(1)}, f32[4,8,128]{2,1,0:T(8,128)S(1)}, u32[]{:S(2)}, u32[]{:S(2)}) %collective-permute-start) | collective-permute-done | bytes 16416 | tf_op jit(solution)/shard_map/ppermute | solution.py:601
  5.2 0.4 shard_map.204
  5.6 24.3 %all_to_all.20.block = f32[8,224,128]{2,1,0:T(8,128)S(1)} all-to-all(f32[8,224,128]{2,1,0:T(8,128)S(1)} %shard_map.204), channel_id=1, replica_groups=mesh['tx_outer'=2,'tx_inner'=4,'ty'=16] {'tx_inner','tx_outer'}, dimensions={0} | all-to-all | bytes 1835008 | tf_op jit(solution)/shard_map/all_to_all | solution.py:609
  30.0 4.9 %shard_map.205 = (f32[128,48,128]{2,1,0:T(8,128)S(1)}, f32[8,32,128]{2,1,0:T(8,128)S(1)}) custom-call(f32[8,224,128]{2,1,0:T(8,128)S(1)} %all_to_all.20.block, bf16[512,512]{1,0:T(8,128)(2,1)} %constant.22.clone.order_in, bf16[256,1024]{1,0:T(8,128)(2,1)} %constant.23.clone.high_in, bf16[256,1024]{1,0:T(8,128)(2,1)} %constant.24.clone.low_in, ...), custom_call_target="tpu_custom_call" | custom-call | tf_op jit(solution)/shard_map/pallas_call | solution.py:562
  34.9 44.7 %all_to_all.21 = f32[128,48,128]{2,1,0:T(8,128)S(1)} all-to-all(f32[128,48,128]{2,1,0:T(8,128)S(1)} %get-tuple-element.14), channel_id=1, replica_groups=mesh['tx_outer'=2,'tx_inner'=4,'ty'=16] {'ty','tx_outer','tx_inner'}, dimensions={0} | all-to-all | bytes 6291456 | tf_op jit(solution)/shard_map/all_to_all | solution.py:629
  79.6 10.4 %shard_map.206 = f32[6144,128]{1,0:T(8,128)S(1)} custom-call(f32[6144,128]{1,0:T(8,128)S(1)} %bitcast.11, f32[6,2,1024,128]{3,2,1,0:T(8,128)} %tensor_in.1, bf16[4,256,256]{2,1,0:T(8,128)(2,1)} %constant.26.clone.high_in, bf16[4,256,256]{2,1,0:T(8,128)(2,1)} %constant.27.clone.low_in, bf16[4,128,512]{2,1,0:T(8,128)(2,1)} %constant.28.clone.back_high_in, ...), custom_call_target="tpu_custom_call" | custom-call | tf_op jit(solution)/shard_map/pallas_call | solution.py:562
  90.0 45.3 %all_to_all.22.data = f32[128,48,128]{2,1,0:T(8,128)S(1)} all-to-all(f32[128,48,128]{2,1,0:T(8,128)S(1)} %bitcast.12), channel_id=1, replica_groups=mesh['tx_outer'=2,'tx_inner'=4,'ty'=16] {'ty','tx_outer','tx_inner'}, dimensions={0} | all-to-all | bytes 6291456 | tf_op jit(solution)/shard_map/all_to_all | solution.py:646
  135.4 3.2 %shard_map.207 = f32[8,128,128]{2,1,0:T(8,128)S(1)} custom-call(f32[128,48,128]{2,1,0:T(8,128)S(1)} %all_to_all.22.data, f32[8,32,128]{2,1,0:T(8,128)S(1)} %get-tuple-element.15.kept, bf16[1024,256]{1,0:T(8,128)(2,1)} %constant.30.clone.high_in, bf16[1024,256]{1,0:T(8,128)(2,1)} %constant.31.clone.low_in, f32[8,512]{1,0:T(8,128)} %constant.25.clone.turn_in, ...), custom_call_target="tpu_custom_call" | custom-call | tf_op jit(solution)/shard_map/pallas_call | solution.py:562
  138.6 14.7 %all_to_all.23.block = f32[8,128,128]{2,1,0:T(8,128)S(1)} all-to-all(f32[8,128,128]{2,1,0:T(8,128)S(1)} %shard_map.207), channel_id=1, replica_groups=mesh['tx_outer'=2,'tx_inner'=4,'ty'=16] {'tx_outer','tx_inner'}, dimensions={0} | all-to-all | bytes 1048576 | tf_op jit(solution)/shard_map/all_to_all | solution.py:655
  153.3 1.3 shard_map.208
  (1 shorter events, 0.0 us)
Async XLA Ops:
  1.8 1.7 %collective-permute-start.1 = (f32[4,8,128]{2,1,0:T(8,128)S(1)}, f32[4,8,128]{2,1,0:T(8,128)S(1)}, u32[]{:S(2)}, u32[]{:S(2)}) collective-permute-start(f32[4,8,128]{2,1,0:T(8,128)S(1)} %get-tuple-element.18), channel_id=1, source_target_pairs={{0,15},{1,0},{2,1},{3,2},{4,3},{5,4},{6,5},{7,6},{8,7},{9,8},{10,9... | collective-permute-start | bytes 49160 | tf_op jit(solution)/shard_map/ppermute | solution.py:601
  2.1 3.2 %collective-permute-start = (f32[4,8,128]{2,1,0:T(8,128)S(1)}, f32[4,8,128]{2,1,0:T(8,128)S(1)}, u32[]{:S(2)}, u32[]{:S(2)}) collective-permute-start(f32[4,8,128]{2,1,0:T(8,128)S(1)} %get-tuple-element.19), channel_id=1, source_target_pairs={{0,1},{1,2},{2,3},{3,4},{4,5},{5,6},{6,7},{7,8},{8,9},{9,10},{10,1... | collective-permute-start | bytes 49160 | tf_op jit(solution)/shard_map/ppermute | solution.py:601

commit v7 on v6

--- a/solution.py
+++ b/solution.py
@@ -20,8 +20,10 @@
 TABLE_SPAN = 1.6
 RADIX = 4
 REACH = SWEEPS
-OUTER, INNER = 2, 4
-TX = ("tx_outer", "tx_inner")
+PARTS = {"x_hi": 2, "z": 4, "x_lo": 2, "y": 4, "core": 2}
+TX, TY = ("x_hi", "z"), ("x_lo", "y", "core")
+OUTWARD = ("x_lo", "y", "core", "x_hi", "z")
+INWARD = ("y", "z", "x_lo", "x_hi", "core")
 PAIRS = ((0, 3, 4), (3, 1, 5), (4, 5, 2))
 VMEM = pl.BlockSpec(memory_space=pltpu.VMEM)
 ANY = pl.BlockSpec(memory_space=pl.ANY)
@@ -39,6 +41,22 @@
 def waves(products, length):
     angles = 2.0 * math.pi / length * (products % length)
     return (np.cos(angles), np.sin(angles))
+
+
+def ranks(order, axes):
+    sizes = [PARTS[axis] for axis in axes]
+    place = dict(zip(axes, np.indices(sizes).reshape(len(axes), -1), strict=True))
+    rank = np.zeros(math.prod(sizes), np.int64)
+    for axis in order:
+        rank = rank * PARTS[axis] + place[axis]
+    return [int(r) for r in rank]
+
+
+def index_of(axes):
+    at = 0
+    for axis in axes:
+        at = at * PARTS[axis] + lax.axis_index(axis)
+    return at
 
 
 def split(values):
@@ -70,16 +88,16 @@
 def across_tables(points, groups, blocks, strips):
     length = 2 * points
     span = length // RADIX
-    part, block, group = np.indices((2, blocks, groups)).reshape(3, -1)
+    group, block = np.indices((groups, blocks)).reshape(2, -1)
     v = np.arange(span)
-    forward = np.zeros((RADIX, 2 * span, part.size))
-    for b in range(RADIX):
-        y = strips * (groups * block + group) + b
-        cosine, sine = waves(v[:, None] * y[None, :], length)
-        zero = part[None, :] == 0
-        forward[b, :span] = np.where(zero, cosine, sine)
-        forward[b, span:] = np.where(zero, -sine, cosine)
-    return forward[:, :span], forward.transpose(0, 2, 1)[:, : part.size // 2]
+    tables = []
+    for order in (OUTWARD, INWARD):
+        y = np.zeros(groups * blocks, np.int64)
+        y[ranks(order, TX + TY)] = strips * (groups * block + group)
+        tables.append([waves(v[:, None] * (y + b)[None, :], length) for b in range(RADIX)])
+    forward = np.stack([np.concatenate([c, s], 1) for c, s in tables[0]])
+    back = np.stack([np.concatenate([c.T, -s.T], 1) for c, s in tables[1]])
+    return forward, back
 
 
 def fetch(pairs, sems):
@@ -97,11 +115,6 @@
     for grain in range(values.shape[0]):
         total = total + jnp.where(which == grain, values[grain], 0.0)
     return total
-
-
-def rank(t):
-    outer, inner = divmod(t, INNER)
-    return inner * OUTER + outer
 
 
 def edges_kernel(heat_in, kind_in, moment_in, heat, kind, moment, rows, sems):
@@ -134,12 +147,12 @@
                 pair = (heat[at, :], kind[at, :].astype(F32))
             for which, value in enumerate(pair):
                 at = (which * tall + i) * layers
-                out[rank(group), at : at + layers, :] = value
+                out[ranks(TX[::-1], TX)[group], at : at + layers, :] = value
         for comp in range(3):
             for strip in range(strips):
                 at = pl.ds(comp * layers * count + group * strips + strip, layers, stride=count)
                 to = (2 * tall + comp * strips + strip) * layers
-                out[rank(group), to : to + layers, :] = moment[at, :]
+                out[ranks(TX[::-1], TX)[group], to : to + layers, :] = moment[at, :]
 
 
 def heat_rows(block, nodes, factor, threshold, spot_row, spot_col, total_rows):
@@ -148,18 +161,19 @@
     total_cols = groups * width
     strips = (lines // layers - 4 * REACH) // 5
     tall = strips + 2 * REACH
-    place = lax.axis_index("ty") * groups + lax.axis_index(TX[0]) * INNER + lax.axis_index(TX[1])
+    place = index_of(TY) * groups + index_of(TX)
     row_base = place * strips - REACH
     shape = (layers, total_cols)
     column = lax.broadcasted_iota(jnp.int32, shape, 1)
     depth = lax.broadcasted_iota(jnp.int32, shape, 0)
     spacing = TABLE_SPAN / (nodes.shape[0] - 1)
     slopes = [(nodes[j + 1] - nodes[j]) * (1.0 / spacing) for j in range(nodes.shape[0] - 1)]
+    bases = [nodes[j] - slope * (TABLE_LOW + j * spacing) for j, slope in enumerate(slopes)]
 
     def whole(index):
         at = index * layers
         return jnp.concatenate(
-            [block[rank(t), at : at + layers, :] for t in range(groups)], 1
+            [block[t, at : at + layers, :] for t in ranks(TX[::-1], TX)], 1
         )
 
     def chosen(which, values):
@@ -169,11 +183,14 @@
         return total
 
     def conductivity(theta, gain):
-        absolute = theta + AMBIENT_HEAT
-        total = jnp.zeros_like(theta) + nodes[0]
-        for j, slope in enumerate(slopes):
-            total = total + slope * jnp.clip(absolute - (TABLE_LOW + j * spacing), 0.0, spacing)
-        return gain * total
+        absolute = jnp.clip(theta + AMBIENT_HEAT, TABLE_LOW, TABLE_LOW + TABLE_SPAN)
+        base = jnp.full_like(theta, bases[0])
+        slope = jnp.full_like(theta, slopes[0])
+        for j in range(1, len(slopes)):
+            beyond = absolute >= TABLE_LOW + j * spacing
+            base = jnp.where(beyond, bases[j], base)
+            slope = jnp.where(beyond, slopes[j], slope)
+        return gain * (base + slope * absolute)
 
     inside = {}
     thetas = {}
@@ -331,6 +348,8 @@
         parts.append((real, imag))
     slabs = span // width
     wide = slabs * width
+    blocks = RADIX * slabs
+    go = ranks(OUTWARD, TX + TY)
     high_half = lax.broadcasted_iota(jnp.int32, (2 * strips, wide), 0) >= strips
     for u, spectra in enumerate(turns(parts, -1)):
         for comp in range(3):
@@ -350,7 +369,7 @@
                 for part in range(2):
                     at = (comp * 2 + part) * 2 * strips
                     for slab in range(slabs):
-                        out[(u * slabs + slab) * groups + t, at : at + 2 * strips, :] = value[part][
+                        out[go[t * blocks + u * slabs + slab], at : at + 2 * strips, :] = value[part][
                             :, slab * width : (slab + 1) * width
                         ]
 
@@ -462,6 +481,8 @@
     lines = 3 * layers * strips
     span = high.shape[0] // 2
     slabs = span // width
+    blocks = RADIX * slabs
+    back = ranks(INWARD, TX + TY)
     pieces = []
     high_half = lax.broadcasted_iota(jnp.int32, (2 * strips, slabs * width), 0) >= strips
     for u in range(RADIX):
@@ -475,7 +496,7 @@
                     both.append(
                         jnp.concatenate(
                             [
-                                data[(u * slabs + slab) * groups + t, at : at + 2 * strips, :]
+                                data[back[t * blocks + u * slabs + slab], at : at + 2 * strips, :]
                                 for slab in range(slabs)
                             ],
                             1,
@@ -598,7 +619,7 @@
     )(far(heat), far(kind), far(moment))
 
     def moved(value, step):
-        return lax.ppermute(value, "ty", [(i, (i + step) % ty) for i in range(ty)])
+        return lax.ppermute(value, TY, [(i, (i + step) % ty) for i in range(ty)])
 
     above = moved(rows[1], 1)
     below = moved(rows[0], -1)
@@ -626,7 +647,7 @@
         [pltpu.VMEM((tx, lines, width), F32)],
         copies=9,
     )
-    data = lax.all_to_all(spectra, ("ty", *TX), split_axis=0, concat_axis=0, tiled=True)
+    data = lax.all_to_all(spectra, OUTWARD, split_axis=0, concat_axis=0, tiled=True)
     columns = members * comps * width
     field = with_tables(
         spectrum_kernel,
@@ -643,7 +664,7 @@
         megabytes=44,
     )
     field = field.reshape(senders, message, width)
-    data = lax.all_to_all(field, ("ty", *TX), split_axis=0, concat_axis=0, tiled=True)
+    data = lax.all_to_all(field, INWARD, split_axis=0, concat_axis=0, tiled=True)
     scale = -1.0 / (2 * layers * 2 * points_y * 2 * points_x)
     block = with_tables(
         functools.partial(cells_kernel, scale=scale),
@@ -666,18 +687,18 @@
 
 def solution(mesh):
     tx, ty = mesh.shape["tx"], mesh.shape["ty"]
-    parts = jax.sharding.Mesh(mesh.devices.reshape(OUTER, tx // OUTER, ty), (*TX, "ty"))
+    parts = jax.sharding.Mesh(mesh.devices.reshape(*PARTS.values()), tuple(PARTS))
     in_specs = (
-        P(None, "ty", TX),
-        P(None, "ty", TX),
-        P(None, None, "ty", TX),
-        P(None, TX, None, "ty"),
+        P(None, TY, TX),
+        P(None, TY, TX),
+        P(None, None, TY, TX),
+        P(None, TX, None, TY),
         P(),
         P(),
         P(),
         P(),
         P(),
     )
-    out_specs = (P(None, "ty", TX), P(None, None, "ty", TX))
+    out_specs = (P(None, TY, TX), P(None, None, TY, TX))
     body = functools.partial(local, tx, ty)
     return jax.shard_map(body, mesh=parts, in_specs=in_specs, out_specs=out_specs, check_vma=False)

time: 157 us -> 156 us (level)
  no operation moved by 1% of the time
where the time goes in v7:
time: 156 us; the launch traced here: 154 us
  blocking collectives  129 us (83%)
  Pallas kernels  20.9 us (13%)
  waiting for transfers between devices  2.84 us (2%)
    all_to_all x1, blocking collectives, local(): lax.all_to_all(field, INWARD, split_axis=0, concat_axis=0, tiled=True)  46 us
    all_to_all x1, blocking collectives, local(): lax.all_to_all(spectra, OUTWARD, split_axis=0, concat_axis=0, tiled=True)  44.7 us
    all_to_all x1, blocking collectives, local(): lax.all_to_all(block, TX[::-1], split_axis=0, concat_axis=0, tiled=True)  24.3 us
    pallas_call x3, Pallas kernels, with_tables(): call(kernel, out_shape, [VMEM] * len(operands) + [ANY] * (len(tables) + l...  18.1 us
    all_to_all x1, blocking collectives, local(): block = lax.all_to_all(block, TX, split_axis=0, concat_axis=0, tiled=True)  14 us
  transfers between devices with their start and end apart: 2, of which 2 were waited for; matrix products, arithmetic and copies ran while one was open for 0% of the time, Pallas kernels for 0%

profile of v7, /device:TPU:24, one launch (start us, length us, event | category | flops | bytes accessed | tf_op | source)
XLA Modules:
  0.0 154.0 jit_solution(8060143857838156838)
XLA Ops:
  0.6 1.2 shard_map.203
  1.8 0.3 collective-permute-start.1
  2.1 0.3 collective-permute-start
  2.4 1.1 collective-permute-done.1.below
  3.5 1.7 %collective-permute-done.above = f32[4,8,128]{2,1,0:T(8,128)S(1)} collective-permute-done((f32[4,8,128]{2,1,0:T(8,128)S(1)}, f32[4,8,128]{2,1,0:T(8,128)S(1)}, u32[]{:S(2)}, u32[]{:S(2)}) %collective-permute-start) | collective-permute-done | bytes 16416 | tf_op jit(solution)/shard_map/ppermute | solution.py:622
  5.2 0.4 shard_map.204
  5.6 24.3 %all_to_all.20.block = f32[8,224,128]{2,1,0:T(8,128)S(1)} all-to-all(f32[8,224,128]{2,1,0:T(8,128)S(1)} %shard_map.204), channel_id=1, replica_groups=mesh['x_hi'=2,'z'=4,'x_lo'=2,'y'=4,'core'=2] {'z','x_hi'}, dimensions={0} | all-to-all | bytes 1835008 | tf_op jit(solution)/shard_map/all_to_all | solution.py:630
  30.0 4.4 %shard_map.205 = (f32[128,48,128]{2,1,0:T(8,128)S(1)}, f32[8,32,128]{2,1,0:T(8,128)S(1)}) custom-call(f32[8,224,128]{2,1,0:T(8,128)S(1)} %all_to_all.20.block, bf16[512,512]{1,0:T(8,128)(2,1)} %constant.22.clone.order_in, bf16[256,1024]{1,0:T(8,128)(2,1)} %constant.23.clone.high_in, bf16[256,1024]{1,0:T(8,128)(2,1)} %constant.24.clone.low_in, ...), custom_call_target="tpu_custom_call" | custom-call | tf_op jit(solution)/shard_map/pallas_call | solution.py:583
  34.4 44.7 %all_to_all.21 = f32[128,48,128]{2,1,0:T(8,128)S(1)} all-to-all(f32[128,48,128]{2,1,0:T(8,128)S(1)} %get-tuple-element.14), channel_id=1, replica_groups=mesh['x_hi'=2,'z'=4,'x_lo'=2,'y'=4,'core'=2] {'x_lo','y','core','x_hi','z'}, dimensions={0} | all-to-all | bytes 6291456 | tf_op jit(solution)/shard_map/all_to_all | solution.py:650
  79.0 10.4 %shard_map.206 = f32[6144,128]{1,0:T(8,128)S(1)} custom-call(f32[6144,128]{1,0:T(8,128)S(1)} %bitcast.11, f32[6,2,1024,128]{3,2,1,0:T(8,128)} %tensor_in.1, bf16[4,256,256]{2,1,0:T(8,128)(2,1)} %constant.26.clone.high_in, bf16[4,256,256]{2,1,0:T(8,128)(2,1)} %constant.27.clone.low_in, bf16[4,128,512]{2,1,0:T(8,128)(2,1)} %constant.28.clone.back_high_in, ...), custom_call_target="tpu_custom_call" | custom-call | tf_op jit(solution)/shard_map/pallas_call | solution.py:583
  89.5 46.0 %all_to_all.22.data = f32[128,48,128]{2,1,0:T(8,128)S(1)} all-to-all(f32[128,48,128]{2,1,0:T(8,128)S(1)} %bitcast.12), channel_id=1, replica_groups=mesh['x_hi'=2,'z'=4,'x_lo'=2,'y'=4,'core'=2] {'y','z','x_lo','x_hi','core'}, dimensions={0} | all-to-all | bytes 6291456 | tf_op jit(solution)/shard_map/all_to_all | solution.py:667
  135.5 3.2 %shard_map.207 = f32[8,128,128]{2,1,0:T(8,128)S(1)} custom-call(f32[128,48,128]{2,1,0:T(8,128)S(1)} %all_to_all.22.data, f32[8,32,128]{2,1,0:T(8,128)S(1)} %get-tuple-element.15.kept, bf16[1024,256]{1,0:T(8,128)(2,1)} %constant.30.clone.high_in, bf16[1024,256]{1,0:T(8,128)(2,1)} %constant.31.clone.low_in, f32[8,512]{1,0:T(8,128)} %constant.25.clone.turn_in, ...), custom_call_target="tpu_custom_call" | custom-call | tf_op jit(solution)/shard_map/pallas_call | solution.py:583
  138.7 14.0 %all_to_all.23.block = f32[8,128,128]{2,1,0:T(8,128)S(1)} all-to-all(f32[8,128,128]{2,1,0:T(8,128)S(1)} %shard_map.207), channel_id=1, replica_groups=mesh['x_hi'=2,'z'=4,'x_lo'=2,'y'=4,'core'=2] {'x_hi','z'}, dimensions={0} | all-to-all | bytes 1048576 | tf_op jit(solution)/shard_map/all_to_all | solution.py:676
  152.7 1.3 shard_map.208
  (1 shorter events, 0.0 us)
Async XLA Ops:
  1.8 1.7 %collective-permute-start.1 = (f32[4,8,128]{2,1,0:T(8,128)S(1)}, f32[4,8,128]{2,1,0:T(8,128)S(1)}, u32[]{:S(2)}, u32[]{:S(2)}) collective-permute-start(f32[4,8,128]{2,1,0:T(8,128)S(1)} %get-tuple-element.18), channel_id=1, source_target_pairs={{0,15},{1,0},{2,1},{3,2},{4,3},{5,4},{6,5},{7,6},{8,7},{9,8},{10,9... | collective-permute-start | bytes 49160 | tf_op jit(solution)/shard_map/ppermute | solution.py:622
  2.1 3.2 %collective-permute-start = (f32[4,8,128]{2,1,0:T(8,128)S(1)}, f32[4,8,128]{2,1,0:T(8,128)S(1)}, u32[]{:S(2)}, u32[]{:S(2)}) collective-permute-start(f32[4,8,128]{2,1,0:T(8,128)S(1)} %get-tuple-element.19), channel_id=1, source_target_pairs={{0,1},{1,2},{2,3},{3,4},{4,5},{5,6},{6,7},{7,8},{8,9},{9,10},{10,1... | collective-permute-start | bytes 49160 | tf_op jit(solution)/shard_map/ppermute | solution.py:622

commit v8 on v7

--- a/solution.py
+++ b/solution.py
@@ -177,9 +177,9 @@
         )
 
     def chosen(which, values):
-        total = jnp.zeros(which.shape, F32)
-        for grain in range(values.shape[0]):
-            total = total + jnp.where(which == float(grain), values[grain], 0.0)
+        total = jnp.full(which.shape, values[0], F32)
+        for grain in range(1, values.shape[0]):
+            total = jnp.where(which == float(grain), values[grain], total)
         return total
 
     def conductivity(theta, gain):
@@ -200,7 +200,6 @@
         inside[i] = jnp.where((y >= 0) & (y < total_rows), 1.0, 0.0)
         thetas[i] = (whole(i) - AMBIENT_HEAT) * inside[i]
         gains[i] = chosen(whole(tall + i), factor) * inside[i]
-    not_top = depth > 0
     not_bottom = depth < layers - 1
     for sweep in range(SWEEPS):
         shifted = column - spot_col[sweep] + total_cols // 2
@@ -209,16 +208,19 @@
         offset = (shifted - total_cols // 2).astype(F32) * (1.0 / (0.5 * width))
         along = jnp.exp(depth.astype(F32) * (-1.0 / LASER_DEPTH)) * jnp.exp(-0.5 * offset * offset)
         k = {i: conductivity(thetas[i], gains[i]) for i in range(sweep, tall - sweep)}
+        between = {
+            i: (k[i] + k[i + 1]) * (thetas[i + 1] - thetas[i]) for i in range(sweep, tall - sweep - 1)
+        }
         fresh = {}
         for i in range(sweep + 1, tall - sweep - 1):
             theta, own = thetas[i], k[i]
-            flux = (own + k[i - 1]) * (thetas[i - 1] - theta)
-            flux = flux + (own + k[i + 1]) * (thetas[i + 1] - theta)
-            for turn in (1, total_cols - 1):
-                flux = flux + (own + pltpu.roll(own, turn, 1)) * (pltpu.roll(theta, turn, 1) - theta)
-            for turn, valid in ((1, not_top), (layers - 1, not_bottom)):
-                part = (own + pltpu.roll(own, turn, 0)) * (pltpu.roll(theta, turn, 0) - theta)
-                flux = flux + jnp.where(valid, part, 0.0)
+            right = (own + pltpu.roll(own, total_cols - 1, 1)) * (
+                pltpu.roll(theta, total_cols - 1, 1) - theta
+            )
+            down = (own + pltpu.roll(own, layers - 1, 0)) * (pltpu.roll(theta, layers - 1, 0) - theta)
+            down = jnp.where(not_bottom, down, 0.0)
+            flux = (between[i] - between[i - 1]) + (right - pltpu.roll(right, 1, 1))
+            flux = flux + (down - pltpu.roll(down, 1, 0))
             across = (row_base + i - spot_row[sweep]).astype(F32) * (1.0 / 32.0)
             across = jnp.exp(jnp.full((layers, width), -0.5, F32) * (across * across))
             source = along * jnp.concatenate([across] * groups, 1)

time: 156 us -> 156 us (level)
  no operation moved by 1% of the time
where the time goes in v8:
time: 156 us; the launch traced here: 154 us
  blocking collectives  129 us (83%)
  Pallas kernels  20.7 us (13%)
  waiting for transfers between devices  2.84 us (2%)
    all_to_all x1, blocking collectives, local(): lax.all_to_all(field, INWARD, split_axis=0, concat_axis=0, tiled=True)  46.1 us
    all_to_all x1, blocking collectives, local(): lax.all_to_all(spectra, OUTWARD, split_axis=0, concat_axis=0, tiled=True)  44.7 us
    all_to_all x1, blocking collectives, local(): lax.all_to_all(block, TX[::-1], split_axis=0, concat_axis=0, tiled=True)  24.3 us
    pallas_call x3, Pallas kernels, with_tables(): call(kernel, out_shape, [VMEM] * len(operands) + [ANY] * (len(tables) + l...  17.9 us
    all_to_all x1, blocking collectives, local(): block = lax.all_to_all(block, TX, split_axis=0, concat_axis=0, tiled=True)  14 us
  transfers between devices with their start and end apart: 2, of which 2 were waited for; matrix products, arithmetic and copies ran while one was open for 0% of the time, Pallas kernels for 0%

profile of v8, /device:TPU:24, one launch (start us, length us, event | category | flops | bytes accessed | tf_op | source)
XLA Modules:
  0.0 153.8 jit_solution(7954006932806593780)
XLA Ops:
  0.6 1.2 shard_map.203
  1.8 0.3 collective-permute-start.1
  2.1 0.3 collective-permute-start
  2.4 1.1 collective-permute-done.1.below
  3.5 1.7 %collective-permute-done.above = f32[4,8,128]{2,1,0:T(8,128)S(1)} collective-permute-done((f32[4,8,128]{2,1,0:T(8,128)S(1)}, f32[4,8,128]{2,1,0:T(8,128)S(1)}, u32[]{:S(2)}, u32[]{:S(2)}) %collective-permute-start) | collective-permute-done | bytes 16416 | tf_op jit(solution)/shard_map/ppermute | solution.py:624
  5.2 0.4 shard_map.204
  5.6 24.3 %all_to_all.20.block = f32[8,224,128]{2,1,0:T(8,128)S(1)} all-to-all(f32[8,224,128]{2,1,0:T(8,128)S(1)} %shard_map.204), channel_id=1, replica_groups=mesh['x_hi'=2,'z'=4,'x_lo'=2,'y'=4,'core'=2] {'z','x_hi'}, dimensions={0} | all-to-all | bytes 1835008 | tf_op jit(solution)/shard_map/all_to_all | solution.py:632
  30.0 4.2 %shard_map.205 = (f32[128,48,128]{2,1,0:T(8,128)S(1)}, f32[8,32,128]{2,1,0:T(8,128)S(1)}) custom-call(f32[8,224,128]{2,1,0:T(8,128)S(1)} %all_to_all.20.block, bf16[512,512]{1,0:T(8,128)(2,1)} %constant.22.clone.order_in, bf16[256,1024]{1,0:T(8,128)(2,1)} %constant.23.clone.high_in, bf16[256,1024]{1,0:T(8,128)(2,1)} %constant.24.clone.low_in, ...), custom_call_target="tpu_custom_call" | custom-call | tf_op jit(solution)/shard_map/pallas_call | solution.py:585
  34.2 44.7 %all_to_all.21 = f32[128,48,128]{2,1,0:T(8,128)S(1)} all-to-all(f32[128,48,128]{2,1,0:T(8,128)S(1)} %get-tuple-element.14), channel_id=1, replica_groups=mesh['x_hi'=2,'z'=4,'x_lo'=2,'y'=4,'core'=2] {'x_lo','y','core','x_hi','z'}, dimensions={0} | all-to-all | bytes 6291456 | tf_op jit(solution)/shard_map/all_to_all | solution.py:652
  78.9 10.4 %shard_map.206 = f32[6144,128]{1,0:T(8,128)S(1)} custom-call(f32[6144,128]{1,0:T(8,128)S(1)} %bitcast.11, f32[6,2,1024,128]{3,2,1,0:T(8,128)} %tensor_in.1, bf16[4,256,256]{2,1,0:T(8,128)(2,1)} %constant.26.clone.high_in, bf16[4,256,256]{2,1,0:T(8,128)(2,1)} %constant.27.clone.low_in, bf16[4,128,512]{2,1,0:T(8,128)(2,1)} %constant.28.clone.back_high_in, ...), custom_call_target="tpu_custom_call" | custom-call | tf_op jit(solution)/shard_map/pallas_call | solution.py:585
  89.3 46.1 %all_to_all.22.data = f32[128,48,128]{2,1,0:T(8,128)S(1)} all-to-all(f32[128,48,128]{2,1,0:T(8,128)S(1)} %bitcast.12), channel_id=1, replica_groups=mesh['x_hi'=2,'z'=4,'x_lo'=2,'y'=4,'core'=2] {'y','z','x_lo','x_hi','core'}, dimensions={0} | all-to-all | bytes 6291456 | tf_op jit(solution)/shard_map/all_to_all | solution.py:669
  135.4 3.2 %shard_map.207 = f32[8,128,128]{2,1,0:T(8,128)S(1)} custom-call(f32[128,48,128]{2,1,0:T(8,128)S(1)} %all_to_all.22.data, f32[8,32,128]{2,1,0:T(8,128)S(1)} %get-tuple-element.15.kept, bf16[1024,256]{1,0:T(8,128)(2,1)} %constant.30.clone.high_in, bf16[1024,256]{1,0:T(8,128)(2,1)} %constant.31.clone.low_in, f32[8,512]{1,0:T(8,128)} %constant.25.clone.turn_in, ...), custom_call_target="tpu_custom_call" | custom-call | tf_op jit(solution)/shard_map/pallas_call | solution.py:585
  138.6 14.0 %all_to_all.23.block = f32[8,128,128]{2,1,0:T(8,128)S(1)} all-to-all(f32[8,128,128]{2,1,0:T(8,128)S(1)} %shard_map.207), channel_id=1, replica_groups=mesh['x_hi'=2,'z'=4,'x_lo'=2,'y'=4,'core'=2] {'x_hi','z'}, dimensions={0} | all-to-all | bytes 1048576 | tf_op jit(solution)/shard_map/all_to_all | solution.py:678
  152.6 1.3 shard_map.208
  (1 shorter events, 0.0 us)
Async XLA Ops:
  1.8 1.7 %collective-permute-start.1 = (f32[4,8,128]{2,1,0:T(8,128)S(1)}, f32[4,8,128]{2,1,0:T(8,128)S(1)}, u32[]{:S(2)}, u32[]{:S(2)}) collective-permute-start(f32[4,8,128]{2,1,0:T(8,128)S(1)} %get-tuple-element.18), channel_id=1, source_target_pairs={{0,15},{1,0},{2,1},{3,2},{4,3},{5,4},{6,5},{7,6},{8,7},{9,8},{10,9... | collective-permute-start | bytes 49160 | tf_op jit(solution)/shard_map/ppermute | solution.py:624
  2.1 3.2 %collective-permute-start = (f32[4,8,128]{2,1,0:T(8,128)S(1)}, f32[4,8,128]{2,1,0:T(8,128)S(1)}, u32[]{:S(2)}, u32[]{:S(2)}) collective-permute-start(f32[4,8,128]{2,1,0:T(8,128)S(1)} %get-tuple-element.19), channel_id=1, source_target_pairs={{0,1},{1,2},{2,3},{3,4},{4,5},{5,6},{6,7},{7,8},{8,9},{9,10},{10,1... | collective-permute-start | bytes 49160 | tf_op jit(solution)/shard_map/ppermute | solution.py:624
